TPU v7x, 32 devices: a whole 2x2x4 slice. The times are simulated.
32 devices in a mesh: dp: 4 (over x, core), row: 4 (over z), col: 2 (over y).
Axes of the slice: x: 2, y: 2, z: 4, core: 2. Of those that a mesh axis runs over, the one named last changes fastest.
Arguments:
- tokens: float32 [6304, 1024], P('dp', ('row', 'col')), may hold values from -6 to 6
- cotangent: float32 [6304, 1024], P('dp', ('row', 'col')), may hold values from -6 to 6
- w_qkv: bfloat16 [1024, 3, 16, 64], P('row', None, 'col', 'dp'), may hold values from -0.4375 to 0.4375
- b_qkv: bfloat16 [2, 16, 64], P(None, 'col', 'dp'), may hold values from -3 to 3
- w_out: bfloat16 [16, 64, 1024], P('col', 'dp', 'row'), may hold values from -1 to 1
- w_up: bfloat16 [1024, 64, 64], P('row', 'col', 'dp'), may hold values from -0.34375 to 0.34375
- b_up: bfloat16 [64, 64], P('col', 'dp'), may hold values from -3 to 3
- w_down: bfloat16 [64, 64, 1024], P('col', 'dp', 'row'), may hold values from -0.09375 to 0.09375
- vectors: bfloat16 [6, 16, 64], P(None, ('row', 'col'), 'dp'), may hold values from -1.2 to 1.4, as said below
- state_qkv: float32 [2, 1024, 3, 16, 64], P(None, 'row', None, 'col', 'dp'), may hold values from -4.5 to 4.5, as said below
- state_qkv_bias: float32 [2, 2, 16, 64], P(None, None, 'col', 'dp'), may hold values from -4.5 to 4.5, as said below
- state_out: float32 [2, 16, 64, 1024], P(None, 'col', 'dp', 'row'), may hold values from -14.5 to 14.5, as said below
- state_up: float32 [2, 1024, 64, 64], P(None, 'row', 'col', 'dp'), may hold values from -3.9 to 3.9, as said below
- state_up_bias: float32 [2, 64, 64], P(None, 'col', 'dp'), may hold values from -3.9 to 3.9, as said below
- state_down: float32 [2, 64, 64, 1024], P(None, 'col', 'dp', 'row'), may hold values from -7.4 to 7.4, as said below
- state_vectors: float32 [2, 6, 16, 64], P(None, None, ('row', 'col'), 'dp'), may hold values from -14.5 to 14.5, as said below
Outputs:
- layer_out: float32 [6304, 1024], P('dp', ('row', 'col'))
- grad_tokens: float32 [6304, 1024], P('dp', ('row', 'col'))
- grad_w_qkv: float32 [1024, 3, 16, 64], P('row', None, 'col', 'dp')
- grad_b_qkv: float32 [2, 16, 64], P(None, 'col', 'dp')
- grad_w_out: float32 [16, 64, 1024], P('col', 'dp', 'row')
- grad_w_up: float32 [1024, 64, 64], P('row', 'col', 'dp')
- grad_b_up: float32 [64, 64], P('col', 'dp')
- grad_w_down: float32 [64, 64, 1024], P('col', 'dp', 'row')
- grad_vectors: float32 [6, 16, 64], P(None, ('row', 'col'), 'dp')
- change_w_qkv: float32 [1024, 3, 16, 64], P('row', None, 'col', 'dp')
- change_b_qkv: float32 [2, 16, 64], P(None, 'col', 'dp')
- change_w_out: float32 [16, 64, 1024], P('col', 'dp', 'row')
- change_w_up: float32 [1024, 64, 64], P('row', 'col', 'dp')
- change_b_up: float32 [64, 64], P('col', 'dp')
- change_w_down: float32 [64, 64, 1024], P('col', 'dp', 'row')
- change_vectors: float32 [6, 16, 64], P(None, ('row', 'col'), 'dp')
- new_state_qkv: float32 [2, 1024, 3, 16, 64], P(None, 'row', None, 'col', 'dp')
- new_state_qkv_bias: float32 [2, 2, 16, 64], P(None, None, 'col', 'dp')
- new_state_out: float32 [2, 16, 64, 1024], P(None, 'col', 'dp', 'row')
- new_state_up: float32 [2, 1024, 64, 64], P(None, 'row', 'col', 'dp')
- new_state_up_bias: float32 [2, 64, 64], P(None, 'col', 'dp')
- new_state_down: float32 [2, 64, 64, 1024], P(None, 'col', 'dp', 'row')
- new_state_vectors: float32 [2, 6, 16, 64], P(None, None, ('row', 'col'), 'dp')
Inputs may be any that keep to these rules, and one draw needn't show every extreme that they name: `vectors`: rows 0 and 3 are gains between 0.6 and 1.4. `state_qkv`: slice 0 is the first moment; slice 1, the second moment, is positive. `state_qkv_bias`: slice 0 is the first moment; slice 1, the second moment, is positive. `state_out`: slice 0 is the first moment; slice 1, the second moment, is positive. `state_up`: slice 0 is the first moment; slice 1, the second moment, is positive. `state_up_bias`: slice 0 is the first moment; slice 1, the second moment, is positive. `state_down`: slice 0 is the first moment; slice 1, the second moment, is positive. `state_vectors`: slice 0 is the first moment; slice 1, the second moment, is positive.
All inputs are finite; a program needn't handle non-finite values.
Results may differ from a plain program's by a relative error of at most 0.023.
Values may be sent and summed in bfloat16 or wider, within the bound.
No kernel may reach another device: no remote copies, remote signals or barrier semaphores. Data moves between devices by JAX's collectives and lax.ppermute only.
A program may use at most 128 MiB of HBM per device.

v0:
```python
import functools
import math

import jax
import jax.numpy as jnp
from jax import lax
from jax.experimental import pallas as pl
from jax.experimental.pallas import tpu as pltpu
from jax.sharding import PartitionSpec as P

HD = 64
SEQ = 197
PAD = 208
STEP = 10

norm_eps = 1e-06
beta_first = 0.9
beta_second = 0.999
learn_rate = 0.01
weight_decay = 0.05
adam_eps = 1e-08
grad_gain = 32.0

LOW = jnp.bfloat16
WIDE = jnp.float32


def swap(values, name, bit):
    count = lax.axis_size(name)
    return lax.ppermute(values, name, [(i, i ^ bit) for i in range(count)])


def bits_of(name):
    bits, bit = [], 1
    while bit < lax.axis_size(name):
        bits.append(bit)
        bit *= 2
    return bits


def after(value, *others):
    return lax.optimization_barrier((value, *others))[0]


def planes(values):
    blocks = {0: values}
    for bit in reversed(bits_of("dp")[:-1]):
        for place in list(blocks):
            blocks[place ^ bit] = swap(blocks[place], "dp", bit)
    return [blocks[d] for d in range(len(blocks))]


def across(values):
    return swap(values, "dp", lax.axis_size("dp") // 2)


def add_low(left, right):
    return (left.astype(WIDE) + right.astype(WIDE)).astype(left.dtype)


def join(held, name, bit):
    return {d: add_low(held[d], swap(held[d ^ bit], name, bit)) for d in held if not d & bit}


def scatter(blocks, name):
    held = dict(enumerate(blocks))
    for bit in bits_of(name):
        held = join(held, name, bit)
    return held[0]


def xor_order(values, axis, name):
    mine = lax.axis_index(name)
    shape = values.shape
    for bit in bits_of(name):
        split = values.reshape(shape[:axis] + (shape[axis] // (2 * bit), 2, bit) + shape[axis + 1 :])
        flipped = jnp.flip(split, axis + 1)
        values = jnp.where((mine & bit) > 0, flipped, split).reshape(shape)
    return values


def adam_step(weight_old, gradient, first_old, second_old, decay_on):
    first_moment = beta_first * first_old + (1.0 - beta_first) * gradient
    second_moment = beta_second * second_old + (1.0 - beta_second) * gradient * gradient
    first_hat = first_moment / (1.0 - beta_first**STEP)
    second_hat = second_moment / (1.0 - beta_second**STEP)
    change = -learn_rate * (first_hat / (jnp.sqrt(second_hat) + adam_eps) + decay_on * weight_old)
    return change, first_moment, second_moment


def adam_kernel(spec, first, *refs):
    count, sizes, grad_scale = spec
    pieces, refs = refs[:count], refs[count:]
    weights, states, outs = refs[: len(sizes)], refs[len(sizes) : 2 * len(sizes)], refs[2 * len(sizes) :]
    at = 0
    for i, size in enumerate(sizes):
        lines = slice(at, at + size)
        at += size
        total = first[lines].astype(WIDE)
        for piece in pieces:
            total = total + piece[lines].astype(WIDE)
        gradient = total * grad_scale
        change, low_moment, high_moment = adam_step(
            weights[i][...].astype(WIDE), gradient, states[i][0], states[i][1], weight_decay
        )
        outs[3 * i][...] = gradient
        outs[3 * i + 1][...] = change
        outs[3 * i + 2][0] = low_moment
        outs[3 * i + 2][1] = high_moment


def collect_kernel(spec, pos, ones, *refs):
    rows, heads, chunk, parts, width, images = spec
    twos, dys, packs, refs = refs[:images], refs[images : 2 * images], refs[2 * images : 3 * images], refs[3 * images :]
    units, out, = refs[:-1], refs[-1]
    low_col, me, row = pos[0] == 0, pos[1], pos[2]
    out[...] = jnp.zeros_like(out)
    add = lambda items: functools.reduce(lambda a, b: a + b, items)
    two = add([t[0:3, :] for t in twos])
    lines = [ones[0:1, :], ones[1:2, :], two[0:1], two[1:2], two[2:3], add([d[...] for d in dys])]
    pack = add([p[...] for p in packs])
    span = heads * HD
    half = width // 2
    unit_total = add([u[...] for u in units])
    each = unit_total.shape[2] // parts
    def put(d, line, pieces):
        value = jnp.concatenate(pieces, axis=1)
        short = out.shape[2] - value.shape[1]
        if short:
            value = jnp.concatenate([value, jnp.zeros((1, short), WIDE)], axis=1)
        out[pl.ds(d, 1), pl.ds(line, 1), :] = value[None]

    for owner in range(parts):
        d = me ^ owner
        spots = [part * span + h * HD + owner * chunk for part in (0, 2) for h in range(heads)]
        put(d, 0, [pack[:, at : at + chunk] for at in spots])
        put(d, 1, [unit_total[u][:, owner * each : (owner + 1) * each] for u in range(unit_total.shape[0])])
        for k in range(rows):
            pieces = []
            for v in range(6):
                for j in range(2):
                    at = k * width + j * HD + owner * chunk
                    near, far = lines[v][:, at : at + chunk], lines[v][:, at + half : at + half + chunk]
                    pieces.append(jnp.where(low_col, near, far))
            put(d, 4 + (row ^ k), pieces)


def small_adam_kernel(spec, pos, tiny, *refs):
    heads, groups, chunk, grad_scale = spec
    row = pos[2]
    weights, states, grads, changes, fresh = (refs[3 * i : 3 * i + 3] for i in range(5))
    for part in range(2):
        for h in range(heads):
            at = (part * heads + h) * chunk
            grads[0][part, h : h + 1, :] = tiny[0:1, at : at + chunk] * grad_scale
    side = lax.broadcasted_iota(jnp.int32, (groups, chunk), 0)
    table = jnp.zeros((groups, chunk), WIDE)
    for g in range(groups):
        table = jnp.where(side == g, tiny[1:2, g * chunk : (g + 1) * chunk], table)
    grads[1][...] = table.T * grad_scale
    mine = tiny[pl.ds(4 + row, 1), :] * grad_scale
    for v in range(6):
        for j in range(2):
            at = (v * 2 + j) * chunk
            grads[2][v, j : j + 1, :] = mine[:, at : at + chunk]
    for i in range(3):
        change, low_moment, high_moment = adam_step(weights[i][...].astype(WIDE), grads[i][...], states[i][0], states[i][1], 0.0)
        changes[i][...] = change
        fresh[i][0] = low_moment
        fresh[i][1] = high_moment


def dot_nt(left, right):
    return lax.dot_general(left, right, (((1,), (1,)), ((), ())), preferred_element_type=WIDE)


def dot_nn(left, right):
    return lax.dot_general(left, right, (((1,), (0,)), ((), ())), preferred_element_type=WIDE)


def dot_tn(left, right):
    return lax.dot_general(left, right, (((0,), (0,)), ((), ())), preferred_element_type=WIDE)


def moments_of(stream):
    center = jnp.mean(stream, axis=-1, keepdims=True)
    offset = stream - center
    inv_std = lax.rsqrt(jnp.mean(offset * offset, axis=-1, keepdims=True) + norm_eps)
    return offset * inv_std, inv_std


def norm_backward(grad_norm, scaled, inv_std, gain):
    weighted = grad_norm * gain
    return inv_std * (
        weighted
        - jnp.mean(weighted, axis=-1, keepdims=True)
        - scaled * jnp.mean(weighted * scaled, axis=-1, keepdims=True)
    )


def lay_strips(low_col, near, far, rows):
    pieces = []
    for k in range(rows):
        mine, other = near(k), far(k)
        pieces.append(jnp.where(low_col, mine, other))
        pieces.append(jnp.where(low_col, other, mine))
    return jnp.concatenate(pieces, axis=1)


def soft(scores):
    lane = lax.broadcasted_iota(jnp.int32, scores.shape, 1)
    scores = jnp.where(lane < SEQ, scores * (1.0 / math.sqrt(HD)), -1e30)
    raised = jnp.exp(scores - jnp.max(scores, axis=-1, keepdims=True))
    return raised * (1.0 / jnp.sum(raised, axis=-1, keepdims=True))


class Source:
    def __init__(self, refs, count):
        self.refs, self.count = refs, count

    def block(self, k, first, size):
        at = first + (self.count if k == 2 else 0)
        return self.refs[(k + 1) // 2][at : at + size, :]


def lay_heads(target, sources, me, groups, rows):
    own = HD // len(sources)
    for k in range(rows):
        for d, source in enumerate(sources):
            place = me ^ d if len(sources) > 1 else 0
            for g in range(groups):
                at = g * HD + place * own
                if len(sources) > 1:
                    at = pl.multiple_of(at, own)
                target[k, pl.ds(at, own), :] = source.block(k, g * own, own)


def first_kernel(spec, pos, near, far, *refs):
    n, rows, heads, width = spec
    count = 4 * heads * HD // n
    sources = [Source([refs[d], refs[n + d], refs[2 * n + d]], count) for d in range(n)]
    vec_o, x_o, normed_o, packed_o, att_o, part_o, qkv_s = refs[3 * n :]
    low_col, me = pos[0] == 0, pos[1]
    small = refs[2 * n][count:, :].astype(WIDE)
    for d in range(1, n):
        small = small + refs[2 * n + d][count:, :].astype(WIDE)
    each = small.shape[0] // rows
    vec = jnp.concatenate([small[k * each : k * each + 6] for k in range(rows)], axis=1)
    vec_o[0:6, :] = vec
    lay_heads(qkv_s, sources, me, 4 * heads, rows)
    stream = lay_strips(low_col, lambda k: near[k, 0], lambda k: far[k, 0], rows)
    x_o[...] = stream
    scaled, _ = moments_of(stream.astype(WIDE))
    normed = (scaled * vec[0:1] + vec[1:2]).astype(LOW)
    normed_o[...] = normed
    span = heads * HD
    lines = span // width
    for part in range(3):
        total = dot_nt(normed[:, :width], qkv_s[0, part * span : (part + 1) * span, :])
        for k in range(1, rows):
            total = total + dot_nt(normed[:, k * width : (k + 1) * width], qkv_s[k, part * span : (part + 1) * span, :])
        if part != 1:
            line = 6 + (lines if part == 2 else 0)
            total = total + jnp.concatenate([small[line + i : line + i + 1] for i in range(lines)], axis=1)
        packed_o[:, part * span : (part + 1) * span] = total.astype(LOW)
    two = 2 * HD
    lane = lax.broadcasted_iota(jnp.int32, (1, two), 1)
    for pair in range(heads // 2):
        at = pair * two
        queries = packed_o[:, at : at + two]
        key_rows = packed_o[:, span + at : span + at + two]
        values = packed_o[:, 2 * span + at : 2 * span + at + two]
        halves = []
        for side in range(2):
            mask = (lane < HD) if side == 0 else (lane >= HD)
            probs = soft(dot_nt(jnp.where(mask, queries, jnp.zeros_like(queries)), key_rows))
            halves.append(dot_nn(probs.astype(LOW), values))
        att_o[:, at : at + two] = jnp.where(lane < HD, halves[0], halves[1]).astype(LOW)
    for k in range(rows):
        part_o[:, k * width : (k + 1) * width] = dot_nn(att_o[...], qkv_s[k, 3 * span :, :]).astype(LOW)


def row_blocks(ref, row, parts, rows):
    return [jnp.concatenate([ref[d, row ^ k] for d in range(parts)], axis=0) for k in range(rows)]


def feed_kernel(spec, pos, vec, small, x, part, came, near, far, up, down, *refs):
    parts, rows, width = spec
    mid, normed, dy, dy_sum_o, units_o, hid_o, unit_sum_o, top_o, far_o, back_o, mixed_s, back_s = refs
    low_col, row = pos[0] == 0, pos[2]
    step = pl.program_id(0)

    @pl.when(step == 0)
    def _():
        dy[...] = lay_strips(low_col, lambda k: near[k, 0], lambda k: far[k, 0], rows)
        dy_sum_o[...] = jnp.sum(dy[...].astype(WIDE), axis=0, keepdims=True)
        middle = x[...].astype(WIDE) + (part[...].astype(WIDE) + came[...].astype(WIDE) + vec[2:3, :])
        mid[...] = middle
        scaled, _ = moments_of(middle)
        normed[...] = (scaled * vec[3:4, :] + vec[4:5, :]).astype(LOW)
        mixed_s[...] = jnp.zeros_like(mixed_s)
        back_s[...] = jnp.zeros_like(back_s)

    up_rows, down_rows = row_blocks(up, row, parts, rows), row_blocks(down, row, parts, rows)
    hidden = dot_nt(normed[:, :width], up_rows[0])
    for k in range(1, rows):
        hidden = hidden + dot_nt(normed[:, k * width : (k + 1) * width], up_rows[k])
    active, slope = gelu_both(hidden + small[0])
    active = active.astype(LOW)
    units_o[0] = active
    grad = dot_nt(dy[:, :width], down_rows[0])
    for k in range(1, rows):
        grad = grad + dot_nt(dy[:, k * width : (k + 1) * width], down_rows[k])
    grad = (grad * slope).astype(LOW)
    hid_o[0] = grad
    unit_sum_o[0] = jnp.sum(grad.astype(WIDE), axis=0, keepdims=True)
    for k in range(rows):
        at = slice(k * width, (k + 1) * width)
        mixed_s[:, at] += dot_nn(active, down_rows[k])
        back_s[:, at] += dot_nn(grad, up_rows[k])

    @pl.when(step == pl.num_programs(0) - 1)
    def _():
        back_o[...] = back_s[...].astype(LOW)
        half = width // 2
        for k in range(rows):
            left, right = slice(k * width, k * width + half), slice(k * width + half, (k + 1) * width)
            base = mid[...] + vec[5:6, :]
            top_l, top_r = mixed_s[:, left] + base[:, left], mixed_s[:, right] + base[:, right]
            top_o[k] = jnp.where(low_col, top_l, top_r)
            far_o[k] = jnp.where(low_col, mixed_s[:, right], mixed_s[:, left]).astype(LOW)


def feed_grad_kernel(spec, pos, *refs):
    parts, rows, width = spec
    hids, units, normeds, dys, out = refs[0:2], refs[2:4], refs[4:6], refs[6:8], refs[8]
    row = pos[2]

    def write(left, right):
        total = dot_tn(left[0][0], right[0][...]) + dot_tn(left[1][0], right[1][...])
        block = total.shape[0] // parts
        for d in range(parts):
            for k in range(rows):
                out[d, row ^ k] = total[d * block : (d + 1) * block, k * width : (k + 1) * width].astype(LOW)

    half = pl.num_programs(0) // 2

    @pl.when(pl.program_id(0) < half)
    def _():
        write(hids, normeds)

    @pl.when(pl.program_id(0) >= half)
    def _():
        write(units, dys)


def second_kernel(spec, pos, vec, mid, back, came, dy, packed, *refs):
    n, rows, heads, width = spec
    count = 4 * heads * HD // n
    sources = [Source([refs[d], refs[n + d], refs[2 * n + d]], count) for d in range(n)]
    dmid_o, dz_o, dpacked_o, back_o, sums_o, psum_o, qkv_s, datt_s = refs[3 * n :]
    me = pos[1]
    lay_heads(qkv_s, sources, me, 4 * heads, rows)
    span = heads * HD
    grad_norm = back[...].astype(WIDE) + came[...].astype(WIDE)
    scaled, inv_std = moments_of(mid[...])
    dmid = dy[...].astype(WIDE) + norm_backward(grad_norm, scaled, inv_std, vec[3:4, :])
    dmid_o[...] = dmid
    dz = dmid.astype(LOW)
    dz_o[...] = dz
    sums_o[0:1, :] = jnp.sum(dz.astype(WIDE), axis=0, keepdims=True)
    sums_o[1:2, :] = jnp.sum(grad_norm * scaled, axis=0, keepdims=True)
    sums_o[2:3, :] = jnp.sum(grad_norm, axis=0, keepdims=True)
    total = dot_nt(dz[:, :width], qkv_s[0, 3 * span :, :])
    for k in range(1, rows):
        total = total + dot_nt(dz[:, k * width : (k + 1) * width], qkv_s[k, 3 * span :, :])
    datt_s[...] = total.astype(LOW)
    two = 2 * HD
    scale = 1.0 / math.sqrt(HD)
    lane = lax.broadcasted_iota(jnp.int32, (1, two), 1)
    for pair in range(heads // 2):
        at = pair * two
        queries = packed[:, at : at + two]
        key_rows = packed[:, span + at : span + at + two]
        values = packed[:, 2 * span + at : 2 * span + at + two]
        grads = datt_s[:, at : at + two]
        dqs, dks, dvs = [], [], []
        for side in range(2):
            mask = (lane < HD) if side == 0 else (lane >= HD)
            probs = soft(dot_nt(jnp.where(mask, queries, jnp.zeros_like(queries)), key_rows))
            dprobs = dot_nt(jnp.where(mask, grads, jnp.zeros_like(grads)), values)
            dscores = probs * (dprobs - jnp.sum(dprobs * probs, axis=-1, keepdims=True))
            dscores = dscores.astype(LOW)
            dqs.append(dot_nn(dscores, key_rows))
            dks.append(dot_tn(dscores, queries))
            dvs.append(dot_tn(probs.astype(LOW), grads))
        first = lane < HD
        dpacked_o[:, at : at + two] = (jnp.where(first, dqs[0], dqs[1]) * scale).astype(LOW)
        dpacked_o[:, span + at : span + at + two] = (jnp.where(first, dks[0], dks[1]) * scale).astype(LOW)
        dpacked_o[:, 2 * span + at : 2 * span + at + two] = jnp.where(first, dvs[0], dvs[1]).astype(LOW)
    psum_o[...] = jnp.sum(dpacked_o[...].astype(WIDE), axis=0, keepdims=True)
    for k in range(rows):
        back_o[:, k * width : (k + 1) * width] = dot_nn(dpacked_o[...], qkv_s[k, : 3 * span, :]).astype(LOW)


def attn_grad_kernel(spec, pos, *refs):
    n, rows, heads, width = spec
    dpacked, normed, att, dz = refs[0:2], refs[2:4], refs[4:6], refs[6:8]
    outs, total_s = refs[8 : 8 + n], refs[8 + n]
    me = pos[1]
    span = heads * HD
    own = HD // n
    for part in range(4):
        if part < 3:
            at = slice(part * span, (part + 1) * span)
            total = dot_tn(dpacked[0][:, at], normed[0][...]) + dot_tn(dpacked[1][:, at], normed[1][...])
        else:
            total = dot_tn(att[0][...], dz[0][...]) + dot_tn(att[1][...], dz[1][...])
        total_s[...] = total.astype(LOW)
        for d in range(n):
            place = me ^ d if n > 1 else 0
            for g in range(heads):
                line = g * HD + place * own
                if n > 1:
                    line = pl.multiple_of(line, own)
                value = total_s[pl.ds(line, own), :]
                to = (part * heads + g) * own
                for k in range(rows):
                    outs[d][k, to : to + own, :] = value[:, k * width : (k + 1) * width]


def gelu_both(values):
    tail = 0.5 * (1.0 + lax.erf(values * (1.0 / math.sqrt(2.0))))
    bell = jnp.exp(values * values * -0.5) * (1.0 / math.sqrt(2.0 * math.pi))
    return values * tail, tail + values * bell


def last_kernel(spec, pos, vec, *refs):
    rows, width, images = spec
    x, back, came, dmid = (refs[i * images : (i + 1) * images] for i in range(4))
    out_o, sums_o = refs[4 * images :]
    low_col = pos[0] == 0
    half = width // 2
    for i in range(images):
        scaled, inv_std = moments_of(x[i][...].astype(WIDE))
        grad_norm = back[i][...].astype(WIDE) + came[i][...].astype(WIDE)
        value = dmid[i][...] + norm_backward(grad_norm, scaled, inv_std, vec[0:1, :])
        gain_sum = jnp.sum(grad_norm * scaled, axis=0, keepdims=True)
        shift_sum = jnp.sum(grad_norm, axis=0, keepdims=True)
        if i == 0:
            sums_o[0:1, :] = gain_sum
            sums_o[1:2, :] = shift_sum
        else:
            sums_o[0:1, :] += gain_sum
            sums_o[1:2, :] += shift_sum
        for k in range(rows):
            left, right = value[:, k * width : k * width + half], value[:, k * width + half : (k + 1) * width]
            out_o[k, i] = jnp.where(low_col, left, right).astype(LOW)


ROOM = 56 * 1024 * 1024


def whole(array):
    zeros = (0,) * len(array.shape)
    return pl.BlockSpec(tuple(array.shape), lambda *_: zeros)


def run_kernel(body, args, outs, scratch=(), grid=None, in_specs=None, out_specs=None):
    if in_specs is None:
        in_specs = [pl.BlockSpec(memory_space=pltpu.SMEM)] + [whole(a) for a in args[1:]]
    if out_specs is None:
        out_specs = [whole(o) for o in outs]
    return pl.pallas_call(
        body,
        grid=grid or (1,),
        in_specs=in_specs,
        out_specs=out_specs,
        out_shape=outs,
        scratch_shapes=list(scratch),
        compiler_params=pltpu.CompilerParams(vmem_limit_bytes=ROOM),
        cost_estimate=pl.CostEstimate(flops=1024, bytes_accessed=1024, transcendentals=0),
    )(*args)


def shaped(shape, kind):
    return jax.ShapeDtypeStruct(shape, kind)


def on_device(
    tokens, cotangent, w_qkv, b_qkv, w_out, w_up, b_up, w_down, vectors,
    state_qkv, state_qkv_bias, state_out, state_up, state_up_bias, state_down, state_vectors,
):
    parts, rows = lax.axis_size("dp"), lax.axis_size("row")
    col, row_index, me = lax.axis_index("col"), lax.axis_index("row"), lax.axis_index("dp")
    low_col = col == 0
    width = w_qkv.shape[0]
    heads, chunk = w_qkv.shape[2], w_qkv.shape[3]
    groups = w_up.shape[1]
    strip = tokens.shape[1]
    images = tokens.shape[0] // (SEQ * rows)
    model = rows * width
    span = heads * HD
    pos = jnp.stack([col, me, row_index]).astype(jnp.int32)

    qkv_own = w_qkv.transpose(1, 2, 3, 0).reshape(-1, width)
    out_own = w_out.reshape(-1, width)
    up_own = w_up.transpose(1, 2, 0).reshape(-1, width)
    down_own = w_down.reshape(-1, width)
    qkv_count, unit_count = qkv_own.shape[0], up_own.shape[0]
    head_own = jnp.concatenate([qkv_own, out_own])
    head_count = head_own.shape[0]

    at_me = (jnp.arange(parts) == me)[:, None]
    vec_own = jnp.where(at_me, vectors[:, :, None, :], 0).reshape(6, -1)
    vec_far = swap(vec_own, "col", 1)
    vec_pair = jnp.stack([jnp.where(low_col, vec_own, vec_far), jnp.where(low_col, vec_far, vec_own)])
    bias_own = jnp.where(at_me, b_qkv[:, :, None, :], 0).reshape(-1, width)
    unit_own = jnp.where(at_me, b_up.reshape(1, -1), 0).reshape(-1, width)
    small_count = 6 + bias_own.shape[0] + unit_own.shape[0]
    small_each = small_count + -small_count % 16

    def to_send(stream, extra):
        blocks = stream.astype(LOW).reshape(rows, images, SEQ, strip)
        blocks = jnp.pad(blocks, ((0, 0), (0, 0), (0, PAD - SEQ), (0, 0)))
        if extra is not None:
            extra = jnp.pad(extra, ((0, 0), (0, 2), (0, 0)))
            blocks = jnp.concatenate([blocks, jnp.broadcast_to(extra, (rows, *extra.shape))], axis=2)
        return [lax.dynamic_index_in_dim(blocks, row_index ^ k, 0, False) for k in range(rows)]

    def send_images(blocks):
        return [blocks[0]] + [swap(block, "row", k) for k, block in enumerate(blocks) if k]

    def near_two(values):
        return [swap(values, "row", 1), swap(values, "row", 2)]

    token = [pos]

    def fence(*values):
        token[0], *values = lax.optimization_barrier((token[0], *values))
        return values

    assert rows == 4 and images == 2 and lax.axis_size("col") == 2
    feed_all = lax.all_gather(jnp.concatenate([up_own, down_own]), ("dp", "row"), axis=0).reshape(parts, rows, -1, width)
    head_two = near_two(head_own)
    head_x = across(head_own)
    head_plane = planes(head_own)
    token_blocks, dy_blocks = to_send(tokens, vec_pair), to_send(cotangent, None)
    small_same = jnp.pad(jnp.concatenate([bias_own, unit_own]), ((6, small_each - small_count), (0, 0)))
    head_two, head_x, head_plane, token_blocks = fence(head_two, head_x, head_plane, token_blocks)

    head_three = swap(head_two[1], "row", 1)
    came = send_images(token_blocks)
    head_pair = jnp.concatenate(head_two)
    head_pair_x = across(head_pair)
    head_three, came, head_pair_x, head_pair, head_x = fence(head_three, came, head_pair_x, head_pair, head_x)

    small_rows = jnp.stack([jnp.concatenate([b[0, PAD : PAD + 6], b[1, PAD : PAD + 6]], axis=1) for b in came])
    small_rows = jnp.pad(small_rows, ((0, 0), (0, small_each - 6), (0, 0))) + small_same
    head_third = jnp.concatenate([head_three, small_rows.reshape(-1, width)])
    near = jnp.stack([block[:, :PAD] for block in came])
    far = swap(near, "col", 1)
    head_third_x = across(head_third)
    head_own_planes = [*head_plane, *planes(head_x)]
    head_pair_planes = [*planes(head_pair), *planes(head_pair_x)]
    head_third_x, head_third, head_own_planes, head_pair_planes, far, near, dy_blocks = fence(
        head_third_x, head_third, head_own_planes, head_pair_planes, far, near, dy_blocks
    )

    head_third_planes = [*planes(head_third), *planes(head_third_x)]

    split = chunk % 16 == 0
    n = parts if split else 1
    head_weights = [*head_own_planes, *head_pair_planes, *head_third_planes]
    if not split:
        def merge(blocks, lead):
            both = xor_order(jnp.stack(blocks), 0, "dp").reshape(parts, lead, blocks[0].shape[0] // lead, width)
            return both.transpose(1, 0, 2, 3).reshape(-1, width)

        def merge_some(blocks, count, lead, number):
            return [merge([b[k * count : (k + 1) * count] for b in blocks], lead) for k in range(number)]

        small_sum = sum(b[head_count:].astype(WIDE) for b in head_third_planes).astype(LOW)
        head_weights = [
            merge(head_own_planes, 4 * heads),
            jnp.concatenate(merge_some(head_pair_planes, head_count, 4 * heads, 2)),
            jnp.concatenate([*merge_some(head_third_planes, head_count, 4 * heads, 1), small_sum]),
        ]
    head_small = [b[head_count * parts // n :] for b in head_weights[2 * n :]]
    scalars = pl.BlockSpec(memory_space=pltpu.SMEM)
    head_specs = [pl.BlockSpec((head_count * parts // n, width), lambda *_: (0, 0))] * n + [whole(w) for w in head_weights[n:]]
    full, low_full = shaped((PAD, model), WIDE), shaped((PAD, model), LOW)

    def forward_one(i):
        strips = pl.BlockSpec((rows, 1, PAD, strip), lambda *_: (0, i, 0, 0))
        outs = [
            shaped((8, model), WIDE),
            low_full,
            low_full,
            shaped((PAD, 3 * span), LOW),
            shaped((PAD, span), LOW),
            low_full,
        ]
        return run_kernel(
            functools.partial(first_kernel, (n, rows, heads, width)),
            (token[0], near, far, *head_weights),
            outs,
            scratch=[pltpu.VMEM((rows, 4 * span, width), LOW)],
            in_specs=[scalars, strips, strips, *head_specs],
        )

    done = [forward_one(0)]
    done, dy_blocks = fence(done, dy_blocks)

    came_one = [swap(done[0][5], "col", 1)]
    dy_came = send_images(dy_blocks)
    done.append(forward_one(1))
    vec = done[0][0]
    unit_rows = sum(b[6 + bias_own.shape[0] :][: unit_own.shape[0]].astype(WIDE) for b in head_small)
    steps = 4
    block = unit_count // steps
    unit_rows = unit_rows.reshape(parts, steps, block).transpose(1, 0, 2).reshape(steps, 1, parts * block)
    done, came_one, dy_came, unit_rows = fence(done, came_one, dy_came, unit_rows)

    came_one = [*came_one, swap(done[1][5], "col", 1)]
    near_dy = jnp.stack(dy_came)
    far_dy = swap(near_dy, "col", 1)
    far_dy, near_dy, came_one = fence(far_dy, near_dy, came_one)

    unit_spec = pl.BlockSpec((1, PAD, parts * block), lambda u: (u, 0, 0))
    unit_sum_spec = pl.BlockSpec((1, 1, parts * block), lambda u: (u, 0, 0))
    unit_shape = (steps, PAD, parts * block)

    def feed_one(i):
        strips = pl.BlockSpec((rows, 1, PAD, strip), lambda *_: (0, i, 0, 0))
        outs = [
            full,
            low_full,
            low_full,
            shaped((1, model), WIDE),
            shaped(unit_shape, LOW),
            shaped(unit_shape, LOW),
            shaped((steps, 1, parts * block), WIDE),
            shaped((rows, PAD, strip), WIDE),
            shaped((rows, PAD, strip), LOW),
            low_full,
        ]
        out_specs = [whole(o) for o in outs]
        out_specs[4], out_specs[5], out_specs[6] = unit_spec, unit_spec, unit_sum_spec
        acts = (done[i][1], done[i][5], came_one[i])
        return run_kernel(
            functools.partial(feed_kernel, (parts, rows, width)),
            (token[0], vec, unit_rows, *acts, near_dy, far_dy, feed_all, feed_all),
            outs,
            scratch=[pltpu.VMEM((PAD, model), WIDE), pltpu.VMEM((PAD, model), WIDE)],
            grid=(steps,),
            in_specs=[
                scalars, whole(vec), unit_sum_spec, *[whole(a) for a in acts], strips, strips,
                pl.BlockSpec((parts, rows, block, width), lambda u: (0, 0, u, 0)),
                pl.BlockSpec((parts, rows, block, width), lambda u: (0, 0, u + steps, 0)),
            ],
            out_specs=out_specs,
        )

    fed = [feed_one(0)]
    fed, came_one = fence(fed, came_one)
    came_two = [swap(fed[0][9], "col", 1)]
    fed.append(feed_one(1))
    fed, came_two = fence(fed, came_two)

    came_two = [*came_two, swap(fed[1][9], "col", 1)]
    early = pl.BlockSpec((1, PAD, parts * block), lambda u: (jnp.minimum(u, steps - 1), 0, 0))
    late = pl.BlockSpec((1, PAD, parts * block), lambda u: (jnp.maximum(u - steps, 0), 0, 0))
    feed_grad = run_kernel(
        functools.partial(feed_grad_kernel, (parts, rows, width)),
        (token[0], *[f[5] for f in fed], *[f[4] for f in fed], *[f[1] for f in fed], *[f[2] for f in fed]),
        [shaped((parts, rows, 2 * unit_count, width), LOW)],
        grid=(2 * steps,),
        in_specs=[scalars, early, early, late, late, *[whole(low_full)] * 4],
        out_specs=[pl.BlockSpec((parts, rows, block, width), lambda u: (0, 0, u, 0))],
    )[0]
    feed_grad, came_two, fed = fence(feed_grad, came_two, fed)
    feed_total = lax.psum_scatter(feed_grad.reshape(-1, width), ("dp", "row"), scatter_dimension=0, tiled=True)

    def fold(blocks):
        held = dict(enumerate(blocks))
        for bit in bits_of("dp")[:-1]:
            held = join(held, "dp", bit)
        return held[0]

    def ordered(blocks, lead):
        if n == parts:
            return blocks
        both = blocks[0].reshape(rows, lead, parts, -1, width).transpose(2, 0, 1, 3, 4)
        both = xor_order(both.reshape(parts, rows, -1, width), 0, "dp")
        return [both[d] for d in range(parts)]

    half_rows = rows // 2

    def sum_high(near_sum, came_part):
        return [add_low(near_sum[half_rows + k], came_part[k]) for k in range(half_rows)]

    def sum_low(near_sum, came_part):
        return [add_low(near_sum[k], came_part[k]) for k in range(half_rows)]

    def from_images(strips):
        came = [strips[0]] + [swap(strips[k], "row", k) for k in range(1, rows)]
        stacked = xor_order(jnp.stack(came)[:, :, :SEQ], 0, "row")
        return stacked.reshape(-1, strip).astype(WIDE)

    def backward_one(i):
        outs = [full, low_full, shaped((PAD, 3 * span), LOW), low_full, shaped((8, model), WIDE), shaped((1, 3 * span), WIDE)]
        acts = (vec, fed[i][0], fed[i][9], came_two[i], fed[i][2], done[i][3])
        return run_kernel(
            functools.partial(second_kernel, (n, rows, heads, width)),
            (token[0], *acts, *head_weights),
            outs,
            scratch=[pltpu.VMEM((rows, 4 * span, width), LOW), pltpu.VMEM((PAD, span), LOW)],
            in_specs=[scalars, *[whole(a) for a in acts], *head_specs],
        )

    top_far = swap(jnp.stack([f[8] for f in fed]), "col", 1)
    returned = [backward_one(0)]
    returned, top_far = fence(returned, top_far)

    came_three = [swap(returned[0][3], "col", 1)]
    top = jnp.stack([f[7] + t.astype(WIDE) for f, t in zip(fed, top_far)], axis=1).astype(LOW)
    result = from_images(top)
    returned.append(backward_one(1))
    returned, came_three, result = fence(returned, came_three, result)

    came_three = [*came_three, swap(returned[1][3], "col", 1)]
    attn_grad = run_kernel(
        functools.partial(attn_grad_kernel, (n, rows, heads, width)),
        (
            token[0], *[r[2] for r in returned], *[d[2] for d in done], *[d[4] for d in done], *[r[1] for r in returned],
        ),
        [shaped((rows, head_count * parts // n, width), LOW) for _ in range(n)],
        scratch=[pltpu.VMEM((span, model), LOW)],
    )
    attn_grad, came_three = fence(attn_grad, came_three)

    attn_blocks = ordered(attn_grad, 4 * heads)
    attn_far, attn_near = fold(attn_blocks[parts // 2 :]), fold(attn_blocks[: parts // 2])
    grad_strips, sums_one = run_kernel(
        functools.partial(last_kernel, (rows, width, images)),
        (
            token[0], vec, *[d[1] for d in done], *[r[3] for r in returned], *came_three, *[r[0] for r in returned],
        ),
        [shaped((rows, images, PAD, strip), LOW), shaped((8, model), WIDE)],
    )
    attn_far, attn_near, grad_strips, sums_one = fence(attn_far, attn_near, grad_strips, sums_one)

    grad_scale = grad_gain / math.sqrt(tokens.shape[0] * parts)

    lanes = max(unit_count, 2 * heads * chunk, 12 * chunk)
    tiny = run_kernel(
        functools.partial(collect_kernel, (rows, heads, chunk, parts, width, images)),
        (
            token[0], sums_one, *[r[4] for r in returned],
            *[f[3] for f in fed], *[r[5] for r in returned], *[f[6] for f in fed],
        ),
        [shaped((parts, 8, lanes), WIDE)],
    )[0]
    attn_high = across(attn_far[half_rows:])
    tiny = functools.reduce(lambda a, b: a + b, [tiny[0]] + [swap(tiny[d], "dp", d) for d in range(1, parts)])
    def adam(reduced, owns, states, ranges):
        first, pieces = reduced
        outs = []
        for size, _ in ranges:
            outs += [shaped((size, width), WIDE), shaped((size, width), WIDE), shaped((2, size, width), WIDE)]
        args = (first, *pieces, *owns, *states)
        return run_kernel(
            functools.partial(adam_kernel, (len(pieces), [r[0] for r in ranges], grad_scale)),
            args,
            outs,
            in_specs=[whole(a) for a in args],
        )

    state_rows = lambda a, order: a.transpose(order).reshape(2, -1, width)
    out_count = out_own.shape[0]
    attn_high, attn_far, attn_near, grad_strips, tiny = fence(attn_high, attn_far, attn_near, grad_strips, tiny)

    attn_low = across(attn_far[:half_rows])
    attn_two, attn_three = sum_high(attn_near, attn_high)
    attn_three = swap(attn_three, "row", 1)
    grad_tokens = from_images(grad_strips)
    attn_low, attn_two, attn_three, attn_near, grad_tokens, tiny = fence(
        attn_low, attn_two, attn_three, attn_near, grad_tokens, tiny
    )

    attn_zero, attn_one = sum_low(attn_near, attn_low)
    attn_one = swap(attn_one, "row", 1)
    attn_two = swap(add_low(attn_two, attn_three), "row", 2)
    tiny = (tiny + swap(tiny, "row", 1)) + (swap(tiny, "row", 2) + swap(tiny, "row", 3))
    attn_zero, attn_one, attn_two, tiny = fence(attn_zero, attn_one, attn_two, tiny)
    feed_done = adam(
        (feed_total, []),
        [up_own, down_own],
        [state_rows(state_up, (0, 2, 3, 1)), state_rows(state_down, (0, 1, 2, 3))],
        [(unit_count, 0), (unit_count, 0)],
    )

    flat_up = lambda a: jnp.swapaxes(a, -1, -2)
    small_args = (b_qkv, flat_up(b_up), vectors, state_qkv_bias, flat_up(state_up_bias), state_vectors)
    small_kinds = (b_qkv.shape, flat_up(b_up).shape, vectors.shape)
    small_done = run_kernel(
        functools.partial(small_adam_kernel, (heads, groups, chunk, grad_scale)),
        (token[0], tiny, *small_args),
        [shaped(k, WIDE) for k in (*small_kinds, *small_kinds)] + [shaped((2, *k), WIDE) for k in small_kinds],
    )

    attn_done = adam(
        (attn_zero, [attn_one, attn_two]),
        [qkv_own, out_own],
        [state_rows(state_qkv, (0, 2, 3, 4, 1)), state_rows(state_out, (0, 1, 2, 3))],
        [(qkv_count, 0), (out_count, 0)],
    )

    def shape_all(which):
        lead = (2,) if which == 2 else ()
        more = (0,) if which == 2 else ()
        move = lambda order: (*more, *[o + len(lead) for o in order])
        return (
            attn_done[which].reshape(*lead, 3, heads, chunk, width).transpose(move((3, 0, 1, 2))),
            small_done[3 * which],
            attn_done[3 + which].reshape(*lead, *w_out.shape),
            feed_done[which].reshape(*lead, groups, chunk, width).transpose(move((2, 0, 1))),
            flat_up(small_done[3 * which + 1]),
            feed_done[3 + which].reshape(*lead, *w_down.shape),
            small_done[3 * which + 2],
        )

    return (result, grad_tokens, *shape_all(0), *shape_all(1), *shape_all(2))


def solution(mesh):
    placed = (
        P("dp", ("row", "col")),
        P("dp", ("row", "col")),
        P("row", None, "col", "dp"),
        P(None, "col", "dp"),
        P("col", "dp", "row"),
        P("row", "col", "dp"),
        P("col", "dp"),
        P("col", "dp", "row"),
        P(None, ("row", "col"), "dp"),
        P(None, "row", None, "col", "dp"),
        P(None, None, "col", "dp"),
        P(None, "col", "dp", "row"),
        P(None, "row", "col", "dp"),
        P(None, "col", "dp"),
        P(None, "col", "dp", "row"),
        P(None, None, ("row", "col"), "dp"),
    )
    params = placed[2:9]
    return jax.shard_map(
        on_device,
        mesh=mesh,
        in_specs=placed,
        out_specs=(placed[0], placed[0], *params, *params, *placed[9:]),
        check_vma=False,
    )
```

profile of v0, /device:TPU:0, one launch (start us, length us, event | category | flops | bytes accessed | tf_op | source)
XLA Modules:
  0.0 292.3 jit_solution(11609951812980185465)
XLA Ops:
  7.3 1.9 pad_maximum_fusion
  10.3 3.1 %collective-permute-start = (bf16[512,256]{1,0:T(8,128)(2,1)S(1)}, bf16[512,256]{1,0:T(8,128)(2,1)S(1)}, u32[]{:S(2)}, u32[]{:S(2)}) collective-permute-start(bf16[512,256]{1,0:T(8,128)(2,1)S(1)} %pad_maximum_fusion.11.refs_0_), channel_id=1, source_target_pairs={{0,2},{2,0},{4,6},{6,4},{1,3},{3,1},{5,7},{7,5},{8,10},{10,8},{12,... | collective-permute-start | bytes 786440 | tf_op jit(solution)/shard_map/ppermute | solution.py:30
  13.4 2.6 collective-permute-start.1
  17.7 1.6 collective-permute-start.4
  21.5 4.6 %collective-permute-done = bf16[512,256]{1,0:T(8,128)(2,1)S(1)} collective-permute-done((bf16[512,256]{1,0:T(8,128)(2,1)S(1)}, bf16[512,256]{1,0:T(8,128)(2,1)S(1)}, u32[]{:S(2)}, u32[]{:S(2)}) %collective-permute-start) | collective-permute-done | bytes 262176 | tf_op jit(solution)/shard_map/ppermute | solution.py:30
  26.1 1.9 collective-permute-done.1
  28.1 1.5 collective-permute-start.9
  29.8 5.1 %collective-permute-start.5 = (bf16[512,256]{1,0:T(8,128)(2,1)S(1)}, bf16[512,256]{1,0:T(8,128)(2,1)S(1)}, u32[]{:S(2)}, u32[]{:S(2)}) collective-permute-start(bf16[512,256]{1,0:T(8,128)(2,1)S(1)} %collective-permute-done.1), channel_id=1, source_target_pairs={{0,2},{2,0},{4,6},{6,4},{1,3},{3,1},{5,7},{7,5},{8,10},{10,8},{12,... | collective-permute-start | bytes 786440 | tf_op jit(solution)/shard_map/ppermute | solution.py:30
  35.0 3.3 %collective-permute-start.7 = (bf16[2,216,128]{2,1,0:T(8,128)(2,1)S(1)}, bf16[2,216,128]{2,1,0:T(8,128)(2,1)S(1)}, u32[]{:S(2)}, u32[]{:S(2)}) collective-permute-start(bf16[2,216,128]{2,1,0:T(8,128)(2,1)S(1)} %get-tuple-element.271), channel_id=1, source_target_pairs={{0,4},{2,6},{4,0},{6,2},{1,5},{3,7},{5,1},{7,3},{8,12},{10,14},{12... | collective-permute-start | bytes 331784 | tf_op jit(solution)/shard_map/ppermute | solution.py:30
  39.8 14.7 %collective-permute-done.6 = bf16[2,216,128]{2,1,0:T(8,128)(2,1)S(1)} collective-permute-done((bf16[2,216,128]{2,1,0:T(8,128)(2,1)S(1)}, bf16[2,216,128]{2,1,0:T(8,128)(2,1)S(1)}, u32[]{:S(2)}, u32[]{:S(2)}) %collective-permute-start.6) | collective-permute-done | bytes 110624 | tf_op jit(solution)/shard_map/ppermute | solution.py:30
  54.5 2.6 collective-permute-done.8
  60.2 1.6 collective-permute-start.10
  61.7 1.9 convert_element_type.142
  63.7 1.9 reshape.183
  65.6 1.8 fusion.21
  67.4 10.0 %collective-permute-done.10.refs_10_ = bf16[640,256]{1,0:T(8,128)(2,1)S(1)} collective-permute-done((bf16[640,256]{1,0:T(8,128)(2,1)S(1)}, bf16[640,256]{1,0:T(8,128)(2,1)S(1)}, u32[]{:S(2)}, u32[]{:S(2)}) %collective-permute-start.10) | collective-permute-done | bytes 327712 | tf_op jit(solution)/shard_map/ppermute | solution.py:30
  80.6 6.2 %shard_map.335 = (f32[8,1024]{1,0:T(8,128)}, bf16[208,1024]{1,0:T(8,128)(2,1)}, bf16[208,1024]{1,0:T(8,128)(2,1)}, bf16[208,1536]{1,0:T(8,128)(2,1)}, bf16[208,5...) custom-call(s32[3]{0:T(128)} %pad_add_fusion.pos, bf16[4,2,208,128]{3,2,1,0:T(8,128)(2,1)} %pad_maximum_fusion.1.near, ...), custom_call_target="tpu_custom_call" | custom-call | flops 1024 | bytes 1024 | tf_op jit(solution)/shard_map/pallas_call | solution.py:474
  88.8 2.9 collective-permute-start.20
  92.5 6.3 %shard_map.336 = (f32[8,1024]{1,0:T(8,128)}, bf16[208,1024]{1,0:T(8,128)(2,1)}, bf16[208,1024]{1,0:T(8,128)(2,1)}, bf16[208,1536]{1,0:T(8,128)(2,1)}, bf16[208,5...) custom-call(s32[3]{0:T(128)} %pad_add_fusion.pos, bf16[4,2,208,128]{3,2,1,0:T(8,128)(2,1)} %pad_maximum_fusion.1.near, ...), custom_call_target="tpu_custom_call" | custom-call | flops 1024 | bytes 1024 | tf_op jit(solution)/shard_map/pallas_call | solution.py:474
  99.4 4.0 %collective-permute-done.19 = bf16[2,208,128]{2,1,0:T(8,128)(2,1)S(1)} collective-permute-done((bf16[2,208,128]{2,1,0:T(8,128)(2,1)}, bf16[2,208,128]{2,1,0:T(8,128)(2,1)S(1)}, u32[]{:S(2)}, u32[]{:S(2)}) %collective-permute-start.19) | collective-permute-done | bytes 106528 | tf_op jit(solution)/shard_map/ppermute | solution.py:30
  103.5 2.0 collective-permute-start.21
  105.5 10.7 %collective-permute-done.21.far = bf16[4,2,208,128]{3,2,1,0:T(8,128)(2,1)S(1)} collective-permute-done((bf16[4,2,208,128]{3,2,1,0:T(8,128)(2,1)S(1)}, bf16[4,2,208,128]{3,2,1,0:T(8,128)(2,1)S(1)}, u32[]{:S(2)}, u32[]{:S(2)}) %collective-permute-start.21) | collective-permute-done | bytes 426016 | tf_op jit(solution)/shard_map/ppermute | solution.py:30
  116.3 7.6 %collective-permute-done.22.came = bf16[208,1024]{1,0:T(8,128)(2,1)S(1)} collective-permute-done((bf16[208,1024]{1,0:T(8,128)(2,1)}, bf16[208,1024]{1,0:T(8,128)(2,1)S(1)}, u32[]{:S(2)}, u32[]{:S(2)}) %collective-permute-start.22) | collective-permute-done | bytes 426016 | tf_op jit(solution)/shard_map/ppermute | solution.py:30
  123.9 10.9 %shard_map.337 = (f32[208,1024]{1,0:T(8,128)}, bf16[208,1024]{1,0:T(8,128)(2,1)}, bf16[208,1024]{1,0:T(8,128)(2,1)}, f32[1,1024]{1,0:T(1,128)}, bf16[4,208,512]{...) custom-call(s32[3]{0:T(128)} %pad_add_fusion.pos, ...), custom_call_target="tpu_custom_call" | custom-call | flops 1024 | bytes 1024 | tf_op jit(solution)/shard_map/pallas_call | solution.py:474
  135.1 10.7 %shard_map.338 = (f32[208,1024]{1,0:T(8,128)}, bf16[208,1024]{1,0:T(8,128)(2,1)}, bf16[208,1024]{1,0:T(8,128)(2,1)}, f32[1,1024]{1,0:T(1,128)}, bf16[4,208,512]{...) custom-call(s32[3]{0:T(128)} %pad_add_fusion.pos, ...), custom_call_target="tpu_custom_call" | custom-call | flops 1024 | bytes 1024 | tf_op jit(solution)/shard_map/pallas_call | solution.py:474
  145.8 1.8 collective-permute-start.24
  147.7 11.1 %shard_map.339 = bf16[4,4,1024,256]{3,2,1,0:T(8,128)(2,1)} custom-call(s32[3]{0:T(128)} %pad_add_fusion.pos, bf16[4,208,512]{2,1,0:T(8,128)(2,1)} %get-tuple-element.374.refs_0_, bf16[4,208,512]{2,1,0:T(8,128)(2,1)} %get-tuple-element.375.refs_1_, bf16[4,208,512]{2,1,0:T(8,128)(2,1)} %get-tuple-element.376.refs_2_, ...), custom_call_target="tpu_custom_call" | custom-call | flops 1024 | bytes 1024 | tf_op jit(solution)/shard_map/pallas_call | solution.py:474
  160.4 10.1 %shard_map.340 = (f32[208,1024]{1,0:T(8,128)}, bf16[208,1024]{1,0:T(8,128)(2,1)}, bf16[208,1536]{1,0:T(8,128)(2,1)}, bf16[208,1024]{1,0:T(8,128)(2,1)}, f32[8,1024]{1,0:T(8,128)}, /*index=5*/f32[1,1536]{1,0:T(1,128)}) custom-call(s32[3]{0:T(128)} %pad_add_fusion.pos, f32[8,1024]{1,0:T(8,128)} %get-tuple-element.310.vec, f32[208,1024]{1,0:T(8,128)} %get-tuple-element.396.mid, ...), custom_call_target="tpu_custom_call" | custom-call | flops 1024 | bytes 1024 | tf_op jit(solution)/shard_map/pallas_call | solution.py:474
  171.6 6.1 %collective-permute-start.28 = (bf16[2,208,128]{2,1,0:T(8,128)(2,1)S(1)}, bf16[2,208,128]{2,1,0:T(8,128)(2,1)S(1)}, u32[]{:S(2)}, u32[]{:S(2)}) collective-permute-start(bf16[2,208,128]{2,1,0:T(8,128)(2,1)S(1)} %get-tuple-element.526), channel_id=1, source_target_pairs={{0,4},{2,6},{4,0},{6,2},{1,5},{3,7},{5,1},{7,3},{8,12},{10,14},{12... | collective-permute-start | bytes 319496 | tf_op jit(solution)/shard_map/ppermute | solution.py:30
  179.0 10.8 %shard_map.341 = (f32[208,1024]{1,0:T(8,128)}, bf16[208,1024]{1,0:T(8,128)(2,1)}, bf16[208,1536]{1,0:T(8,128)(2,1)}, bf16[208,1024]{1,0:T(8,128)(2,1)}, f32[8,1024]{1,0:T(8,128)}, /*index=5*/f32[1,1536]{1,0:T(1,128)}) custom-call(s32[3]{0:T(128)} %pad_add_fusion.pos, f32[8,1024]{1,0:T(8,128)} %get-tuple-element.310.vec, f32[208,1024]{1,0:T(8,128)} %get-tuple-element.416.mid, ...), custom_call_target="tpu_custom_call" | custom-call | flops 1024 | bytes 1024 | tf_op jit(solution)/shard_map/pallas_call | solution.py:474
  191.7 7.1 %shard_map.342 = (bf16[4,512,256]{2,1,0:T(8,128)(2,1)}, bf16[4,512,256]{2,1,0:T(8,128)(2,1)}, bf16[4,512,256]{2,1,0:T(8,128)(2,1)}, bf16[4,512,256]{2,1,0:T(8,128)(2,1)}) custom-call(s32[3]{0:T(128)} %pad_add_fusion.pos, bf16[208,1536]{1,0:T(8,128)(2,1)} %get-tuple-element.432.refs_0_, bf16[208,1536]{1,0:T(8,128)(2,1)} %get-tuple-element.433.refs_1_, ...), custom_call_target="tpu_custom_call" | custom-call | flops 1024 | bytes 1024 | tf_op jit(solution)/shard_map/pallas_call | solution.py:474
  199.9 4.4 %shard_map.343 = (bf16[4,2,208,128]{3,2,1,0:T(8,128)(2,1)}, f32[8,1024]{1,0:T(8,128)}) custom-call(s32[3]{0:T(128)} %pad_add_fusion.pos, f32[8,1024]{1,0:T(8,128)} %get-tuple-element.310.vec, bf16[208,1024]{1,0:T(8,128)(2,1)} %get-tuple-element.334.x.refs_0_, bf16[208,1024]{1,0:T(8,128)(2,1)} %get-tuple-element.361.x.refs_1_, ...), custom_call_target="tpu_custom_call" | custom-call | flops 1024 | bytes 1024 | tf_op jit(solution)/shard_map/pallas_call | solution.py:474
  205.8 1.5 collective-permute-start.33
  207.4 1.9 shard_map.344
  211.9 7.2 %collective-permute-done.36 = f32[8,512]{1,0:T(8,128)S(1)} collective-permute-done((f32[8,512]{1,0:T(8,128)S(1)}, f32[8,512]{1,0:T(8,128)S(1)}, u32[]{:S(2)}, u32[]{:S(2)}) %collective-permute-start.36) | collective-permute-done | bytes 16416 | tf_op jit(solution)/shard_map/ppermute | solution.py:30
  221.8 1.6 collective-permute-start.37
  224.4 2.2 collective-permute-start.40
  228.8 3.6 %collective-permute-done.41 = bf16[2,208,128]{2,1,0:T(8,128)(2,1)S(1)} collective-permute-done((bf16[2,208,128]{2,1,0:T(8,128)(2,1)S(1)}, bf16[2,208,128]{2,1,0:T(8,128)(2,1)S(1)}, u32[]{:S(2)}, u32[]{:S(2)}) %collective-permute-start.41) | collective-permute-done | bytes 106528 | tf_op jit(solution)/shard_map/ppermute | solution.py:30
  232.5 5.9 %collective-permute-done.40 = bf16[2,208,128]{2,1,0:T(8,128)(2,1)S(1)} collective-permute-done((bf16[2,208,128]{2,1,0:T(8,128)(2,1)S(1)}, bf16[2,208,128]{2,1,0:T(8,128)(2,1)S(1)}, u32[]{:S(2)}, u32[]{:S(2)}) %collective-permute-start.40) | collective-permute-done | bytes 106528 | tf_op jit(solution)/shard_map/ppermute | solution.py:30
  239.5 1.9 collective-permute-done.38
  241.4 4.8 %collective-permute-done.37 = bf16[2,512,256]{2,1,0:T(8,128)(2,1)S(1)} collective-permute-done((bf16[2,512,256]{2,1,0:T(8,128)(2,1)}, bf16[2,512,256]{2,1,0:T(8,128)(2,1)S(1)}, u32[]{:S(2)}, u32[]{:S(2)}) %collective-permute-start.37) | collective-permute-done | bytes 524320 | tf_op jit(solution)/shard_map/ppermute | solution.py:30
  247.0 3.2 %collective-permute-start.43 = (bf16[512,256]{1,0:T(8,128)(2,1)S(1)}, bf16[512,256]{1,0:T(8,128)(2,1)S(1)}, u32[]{:S(2)}, u32[]{:S(2)}) collective-permute-start(bf16[512,256]{1,0:T(8,128)(2,1)S(1)} %add_convert_fusion.2), channel_id=1, source_target_pairs={{0,4},{2,6},{4,0},{6,2},{1,5},{3,7},{5,1},{7,3},{8,12},{10,14},{12... | collective-permute-start | bytes 786440 | tf_op jit(solution)/shard_map/ppermute | solution.py:30
  250.3 2.5 collective-permute-start.46
  253.7 14.0 %collective-permute-done.45 = f32[8,512]{1,0:T(8,128)S(1)} collective-permute-done((f32[8,512]{1,0:T(8,128)S(1)}, f32[8,512]{1,0:T(8,128)S(1)}, u32[]{:S(2)}, u32[]{:S(2)}) %collective-permute-start.45) | collective-permute-done | bytes 16416 | tf_op jit(solution)/shard_map/ppermute | solution.py:30
  269.1 3.2 %shard_map.345 = (f32[384,256]{1,0:T(8,128)}, f32[384,256]{1,0:T(8,128)}, f32[2,384,256]{2,1,0:T(8,128)}, f32[128,256]{1,0:T(8,128)}, f32[128,256]{1,0:T(8,128)}, /*index=5*/f32[2,128,256]{2,1,0:T(8,128)}) custom-call(bf16[512,256]{1,0:T(8,128)(2,1)} %get-tuple-element.484.first, bf16[512,256]{1,0:T(8,128)(2,1)} %copy-done.29, bf16[512,256]{1,0:T(8,128)(2,1)} %copy-done.30, ...), custom_call_target="tpu_custom_call" | custom-call | flops 1024 | bytes 1024 | tf_op jit(solution)/shard_map/pallas_call | solution.py:474
  272.3 3.7 %shard_map.346 = (f32[2,8,16]{2,1,0:T(8,128)}, f32[16,32]{1,0:T(8,128)}, f32[6,2,16]{2,1,0:T(2,128)}, f32[2,8,16]{2,1,0:T(8,128)}, f32[16,32]{1,0:T(8,128)}, /*i...) custom-call(s32[3]{0:T(128)} %pad_add_fusion.pos, ...), custom_call_target="tpu_custom_call" | custom-call | flops 1024 | bytes 1024 | tf_op jit(solution)/shard_map/pallas_call | solution.py:474
  276.0 5.1 %reduce-scatter.2.cloned.1.call-done.first = bf16[1024,256]{1,0:T(8,128)(2,1)} async-done(((bf16[16384,256]{1,0:T(8,128)(2,1)}), bf16[1024,256]{1,0:T(8,128)(2,1)}) %reduce-scatter.2.cloned.1.call-update) | async-done | bytes 524304 | tf_op jit(solution)/shard_map/reduce_scatter | solution.py:683
  281.2 4.3 %shard_map.347 = (f32[512,256]{1,0:T(8,128)}, f32[512,256]{1,0:T(8,128)}, f32[2,512,256]{2,1,0:T(8,128)}, f32[512,256]{1,0:T(8,128)}, f32[512,256]{1,0:T(8,128)}, /*index=5*/f32[2,512,256]{2,1,0:T(8,128)}) custom-call(bf16[1024,256]{1,0:T(8,128)(2,1)} %reduce-scatter.2.cloned.1.call-done.first, bf16[512,256]{1,0:T(8,128)(2,1)} %bitcast.185, ...), custom_call_target="tpu_custom_call" | custom-call | flops 1024 | bytes 1024 | tf_op jit(solution)/shard_map/pallas_call | solution.py:474
  (205 shorter events, 38.2 us)
Async XLA Ops:
  7.2 116.7 %all-gather.3.cloned.1.call-start = ((), (), s32[]{:S(2)}) async-start(), calls=%async_computation.2 | async-start | bytes 8912896 | tf_op jit(solution)/shard_map/all_gather | solution.py:544
  9.2 272.0 %reduce-scatter.2.cloned.1.call-start = ((), (), s32[]{:S(2)}) async-start(), calls=%async_computation.1 | async-start | bytes 8912896 | tf_op jit(solution)/shard_map/reduce_scatter | solution.py:683
  10.3 15.8 %collective-permute-start = (bf16[512,256]{1,0:T(8,128)(2,1)S(1)}, bf16[512,256]{1,0:T(8,128)(2,1)S(1)}, u32[]{:S(2)}, u32[]{:S(2)}) collective-permute-start(bf16[512,256]{1,0:T(8,128)(2,1)S(1)} %pad_maximum_fusion.11.refs_0_), channel_id=1, source_target_pairs={{0,2},{2,0},{4,6},{6,4},{1,3},{3,1},{5,7},{7,5},{8,10},{10,8},{12,... | collective-permute-start | bytes 786440 | tf_op jit(solution)/shard_map/ppermute | solution.py:30
  13.4 14.7 %collective-permute-start.1 = (bf16[512,256]{1,0:T(8,128)(2,1)S(1)}, bf16[512,256]{1,0:T(8,128)(2,1)S(1)}, u32[]{:S(2)}, u32[]{:S(2)}) collective-permute-start(bf16[512,256]{1,0:T(8,128)(2,1)S(1)} %pad_maximum_fusion.11.refs_0_), channel_id=1, source_target_pairs={{0,4},{2,6},{4,0},{6,2},{1,5},{3,7},{5,1},{7,3},{8,12},{10,14},{12... | collective-permute-start | bytes 786440 | tf_op jit(solution)/shard_map/ppermute | solution.py:30
  15.9 12.1 %collective-permute-start.2 = (bf16[512,256]{1,0:T(8,128)(2,1)S(1)}, bf16[512,256]{1,0:T(8,128)(2,1)S(1)}, u32[]{:S(2)}, u32[]{:S(2)}) collective-permute-start(bf16[512,256]{1,0:T(8,128)(2,1)S(1)} %pad_maximum_fusion.11.refs_0_), channel_id=1, source_target_pairs={{0,16},{8,24},{16,0},{24,8},{1,17},{9,25},{17,1},{25,9},{2,18},{10... | collective-permute-start | bytes 786440 | tf_op jit(solution)/shard_map/ppermute | solution.py:30
  17.4 10.6 %collective-permute-start.3 = (bf16[512,256]{1,0:T(8,128)(2,1)S(1)}, bf16[512,256]{1,0:T(8,128)(2,1)S(1)}, u32[]{:S(2)}, u32[]{:S(2)}) collective-permute-start(bf16[512,256]{1,0:T(8,128)(2,1)S(1)} %pad_maximum_fusion.11.refs_0_), channel_id=1, source_target_pairs={{0,8},{8,0},{16,24},{24,16},{1,9},{9,1},{17,25},{25,17},{2,10},{10... | collective-permute-start | bytes 786440 | tf_op jit(solution)/shard_map/ppermute | solution.py:30
  17.7 3.6 %collective-permute-start.4 = (bf16[6,128]{1,0:T(8,128)(2,1)S(1)}, bf16[6,128]{1,0:T(8,128)(2,1)S(1)}, u32[]{:S(2)}, u32[]{:S(2)}) collective-permute-start(bf16[6,128]{1,0:T(8,128)(2,1)S(1)} %broadcast_select_fusion.2), channel_id=1, source_target_pairs={{0,1},{1,0},{2,3},{3,2},{4,5},{5,4},{6,7},{7,6},{8,9},{9,8},{10,11... | collective-permute-start | bytes 4616 | tf_op jit(solution)/shard_map/ppermute | solution.py:30
  28.1 29.0 %collective-permute-start.9 = (bf16[1024,256]{1,0:T(8,128)(2,1)S(1)}, bf16[1024,256]{1,0:T(8,128)(2,1)S(1)}, u32[]{:S(2)}, u32[]{:S(2)}) collective-permute-start(bf16[1024,256]{1,0:T(8,128)(2,1)S(1)} %constant_dynamic-update-slice_fusion.refs_4_), channel_id=1, source_target_pairs={{0,16},{8,24},{16,0},{24,8},{1,17},{9,25},{17,1},{25,9},{2,18},{10... | collective-permute-start | bytes 1572872 | tf_op jit(solution)/shard_map/ppermute | solution.py:30
  29.8 27.3 %collective-permute-start.5 = (bf16[512,256]{1,0:T(8,128)(2,1)S(1)}, bf16[512,256]{1,0:T(8,128)(2,1)S(1)}, u32[]{:S(2)}, u32[]{:S(2)}) collective-permute-start(bf16[512,256]{1,0:T(8,128)(2,1)S(1)} %collective-permute-done.1), channel_id=1, source_target_pairs={{0,2},{2,0},{4,6},{6,4},{1,3},{3,1},{5,7},{7,5},{8,10},{10,8},{12,... | collective-permute-start | bytes 786440 | tf_op jit(solution)/shard_map/ppermute | solution.py:30
  35.0 19.5 %collective-permute-start.6 = (bf16[2,216,128]{2,1,0:T(8,128)(2,1)S(1)}, bf16[2,216,128]{2,1,0:T(8,128)(2,1)S(1)}, u32[]{:S(2)}, u32[]{:S(2)}) collective-permute-start(bf16[2,216,128]{2,1,0:T(8,128)(2,1)S(1)} %get-tuple-element.270), channel_id=1, source_target_pairs={{0,2},{2,0},{4,6},{6,4},{1,3},{3,1},{5,7},{7,5},{8,10},{10,8},{12,... | collective-permute-start | bytes 331784 | tf_op jit(solution)/shard_map/ppermute | solution.py:30
  35.0 19.5 %collective-permute-start.7 = (bf16[2,216,128]{2,1,0:T(8,128)(2,1)S(1)}, bf16[2,216,128]{2,1,0:T(8,128)(2,1)S(1)}, u32[]{:S(2)}, u32[]{:S(2)}) collective-permute-start(bf16[2,216,128]{2,1,0:T(8,128)(2,1)S(1)} %get-tuple-element.271), channel_id=1, source_target_pairs={{0,4},{2,6},{4,0},{6,2},{1,5},{3,7},{5,1},{7,3},{8,12},{10,14},{12... | collective-permute-start | bytes 331784 | tf_op jit(solution)/shard_map/ppermute | solution.py:30
  38.4 18.7 %collective-permute-start.8 = (bf16[2,216,128]{2,1,0:T(8,128)(2,1)S(1)}, bf16[2,216,128]{2,1,0:T(8,128)(2,1)S(1)}, u32[]{:S(2)}, u32[]{:S(2)}) collective-permute-start(bf16[2,216,128]{2,1,0:T(8,128)(2,1)S(1)} %get-tuple-element.272), channel_id=1, source_target_pairs={{0,6},{2,4},{4,2},{6,0},{1,7},{3,5},{5,3},{7,1},{8,14},{10,12},{12... | collective-permute-start | bytes 331784 | tf_op jit(solution)/shard_map/ppermute | solution.py:30
  57.1 20.3 %collective-permute-start.12 = (bf16[1024,256]{1,0:T(8,128)(2,1)S(1)}, bf16[1024,256]{1,0:T(8,128)(2,1)S(1)}, u32[]{:S(2)}, u32[]{:S(2)}) collective-permute-start(bf16[1024,256]{1,0:T(8,128)(2,1)S(1)} %constant_dynamic-update-slice_fusion.refs_4_), channel_id=1, source_target_pairs={{0,8},{8,0},{16,24},{24,16},{1,9},{9,1},{17,25},{25,17},{2,10},{10... | collective-permute-start | bytes 1572872 | tf_op jit(solution)/shard_map/ppermute | solution.py:30
  57.2 20.2 %collective-permute-start.13 = (bf16[1024,256]{1,0:T(8,128)(2,1)S(1)}, bf16[1024,256]{1,0:T(8,128)(2,1)S(1)}, u32[]{:S(2)}, u32[]{:S(2)}) collective-permute-start(bf16[1024,256]{1,0:T(8,128)(2,1)S(1)} %collective-permute-done.9.refs_6_), channel_id=1, source_target_pairs={{0,8},{8,0},{16,24},{24,16},{1,9},{9,1},{17,25},{25,17},{2,10},{10... | collective-permute-start | bytes 1572872 | tf_op jit(solution)/shard_map/ppermute | solution.py:30
  58.5 18.9 %collective-permute-start.14 = (bf16[4,2,208,128]{3,2,1,0:T(8,128)(2,1)}, bf16[4,2,208,128]{3,2,1,0:T(8,128)(2,1)}, u32[]{:S(2)}, u32[]{:S(2)}) collective-permute-start(bf16[4,2,208,128]{3,2,1,0:T(8,128)(2,1)} %pad_maximum_fusion.1.near), channel_id=1, source_target_pairs={{0,1},{1,0},{2,3},{3,2},{4,5},{5,4},{6,7},{7,6},{8,9},{9,8},{10,11... | collective-permute-start | bytes 1277960 | tf_op jit(solution)/shard_map/ppermute | solution.py:30
  60.2 17.2 %collective-permute-start.10 = (bf16[640,256]{1,0:T(8,128)(2,1)S(1)}, bf16[640,256]{1,0:T(8,128)(2,1)S(1)}, u32[]{:S(2)}, u32[]{:S(2)}) collective-permute-start(bf16[640,256]{1,0:T(8,128)(2,1)S(1)} %pad_maximum_fusion.10.refs_8_), channel_id=1, source_target_pairs={{0,16},{8,24},{16,0},{24,8},{1,17},{9,25},{17,1},{25,9},{2,18},{10... | collective-permute-start | bytes 983048 | tf_op jit(solution)/shard_map/ppermute | solution.py:30
  61.7 5.6 %collective-permute-start.11 = (bf16[512,256]{1,0:T(8,128)(2,1)S(1)}, bf16[512,256]{1,0:T(8,128)(2,1)S(1)}, u32[]{:S(2)}, u32[]{:S(2)}) collective-permute-start(bf16[512,256]{1,0:T(8,128)(2,1)S(1)} %collective-permute-done.2.refs_2_), channel_id=1, source_target_pairs={{0,8},{8,0},{16,24},{24,16},{1,9},{9,1},{17,25},{25,17},{2,10},{10... | collective-permute-start | bytes 786440 | tf_op jit(solution)/shard_map/ppermute | solution.py:30
  77.5 2.1 collective-permute-start.16
  86.8 16.5 %collective-permute-start.17 = (bf16[208,1024]{1,0:T(8,128)(2,1)}, bf16[208,1024]{1,0:T(8,128)(2,1)S(1)}, u32[]{:S(2)}, u32[]{:S(2)}) collective-permute-start(bf16[208,1024]{1,0:T(8,128)(2,1)} %get-tuple-element.335.part), channel_id=1, source_target_pairs={{0,1},{1,0},{2,3},{3,2},{4,5},{5,4},{6,7},{7,6},{8,9},{9,8},{10,11... | collective-permute-start | bytes 1277960 | tf_op jit(solution)/shard_map/ppermute | solution.py:30
  87.3 12.1 %collective-permute-start.18 = (bf16[2,208,128]{2,1,0:T(8,128)(2,1)}, bf16[2,208,128]{2,1,0:T(8,128)(2,1)S(1)}, u32[]{:S(2)}, u32[]{:S(2)}) collective-permute-start(bf16[2,208,128]{2,1,0:T(8,128)(2,1)} %get-tuple-element.322), channel_id=1, source_target_pairs={{0,2},{2,0},{4,6},{6,4},{1,3},{3,1},{5,7},{7,5},{8,10},{10,8},{12,... | collective-permute-start | bytes 319496 | tf_op jit(solution)/shard_map/ppermute | solution.py:30
  87.3 16.1 %collective-permute-start.19 = (bf16[2,208,128]{2,1,0:T(8,128)(2,1)}, bf16[2,208,128]{2,1,0:T(8,128)(2,1)S(1)}, u32[]{:S(2)}, u32[]{:S(2)}) collective-permute-start(bf16[2,208,128]{2,1,0:T(8,128)(2,1)} %get-tuple-element.323), channel_id=1, source_target_pairs={{0,4},{2,6},{4,0},{6,2},{1,5},{3,7},{5,1},{7,3},{8,12},{10,14},{12... | collective-permute-start | bytes 319496 | tf_op jit(solution)/shard_map/ppermute | solution.py:30
  88.8 14.6 %collective-permute-start.20 = (bf16[2,208,128]{2,1,0:T(8,128)(2,1)}, bf16[2,208,128]{2,1,0:T(8,128)(2,1)S(1)}, u32[]{:S(2)}, u32[]{:S(2)}) collective-permute-start(bf16[2,208,128]{2,1,0:T(8,128)(2,1)} %get-tuple-element.324), channel_id=1, source_target_pairs={{0,6},{2,4},{4,2},{6,0},{1,7},{3,5},{5,3},{7,1},{8,14},{10,12},{12... | collective-permute-start | bytes 319496 | tf_op jit(solution)/shard_map/ppermute | solution.py:30
  103.5 12.8 %collective-permute-start.21 = (bf16[4,2,208,128]{3,2,1,0:T(8,128)(2,1)S(1)}, bf16[4,2,208,128]{3,2,1,0:T(8,128)(2,1)S(1)}, u32[]{:S(2)}, u32[]{:S(2)}) collective-permute-start(bf16[4,2,208,128]{3,2,1,0:T(8,128)(2,1)S(1)} %pad_maximum_fusion.2.near), channel_id=1, source_target_pairs={{0,1},{1,0},{2,3},{3,2},{4,5},{5,4},{6,7},{7,6},{8,9},{9,8},{10,11... | collective-permute-start | bytes 1277960 | tf_op jit(solution)/shard_map/ppermute | solution.py:30
  105.5 18.4 %collective-permute-start.22 = (bf16[208,1024]{1,0:T(8,128)(2,1)}, bf16[208,1024]{1,0:T(8,128)(2,1)S(1)}, u32[]{:S(2)}, u32[]{:S(2)}) collective-permute-start(bf16[208,1024]{1,0:T(8,128)(2,1)} %get-tuple-element.331.part), channel_id=1, source_target_pairs={{0,1},{1,0},{2,3},{3,2},{4,5},{5,4},{6,7},{7,6},{8,9},{9,8},{10,11... | collective-permute-start | bytes 1277960 | tf_op jit(solution)/shard_map/ppermute | solution.py:30
  134.8 11.0 %collective-permute-start.23 = (bf16[208,1024]{1,0:T(8,128)(2,1)}, bf16[208,1024]{1,0:T(8,128)(2,1)S(1)}, u32[]{:S(2)}, u32[]{:S(2)}) collective-permute-start(bf16[208,1024]{1,0:T(8,128)(2,1)} %get-tuple-element.397.back), channel_id=1, source_target_pairs={{0,1},{1,0},{2,3},{3,2},{4,5},{5,4},{6,7},{7,6},{8,9},{9,8},{10,11... | collective-permute-start | bytes 1277960 | tf_op jit(solution)/shard_map/ppermute | solution.py:30
  145.8 12.9 %collective-permute-start.24 = (bf16[208,1024]{1,0:T(8,128)(2,1)}, bf16[208,1024]{1,0:T(8,128)(2,1)S(1)}, u32[]{:S(2)}, u32[]{:S(2)}) collective-permute-start(bf16[208,1024]{1,0:T(8,128)(2,1)} %get-tuple-element.417.back), channel_id=1, source_target_pairs={{0,1},{1,0},{2,3},{3,2},{4,5},{5,4},{6,7},{7,6},{8,9},{9,8},{10,11... | collective-permute-start | bytes 1277960 | tf_op jit(solution)/shard_map/ppermute | solution.py:30
  160.0 10.4 %collective-permute-start.25 = (bf16[2,4,208,128]{3,2,1,0:T(8,128)(2,1)S(1)}, bf16[2,4,208,128]{3,2,1,0:T(8,128)(2,1)S(1)}, u32[]{:S(2)}, u32[]{:S(2)}) collective-permute-start(bf16[2,4,208,128]{3,2,1,0:T(8,128)(2,1)S(1)} %pad_maximum_fusion.3), channel_id=1, source_target_pairs={{0,1},{1,0},{2,3},{3,2},{4,5},{5,4},{6,7},{7,6},{8,9},{9,8},{10,11... | collective-permute-start | bytes 1277960 | tf_op jit(solution)/shard_map/ppermute | solution.py:30
  170.6 19.1 %collective-permute-start.29 = (bf16[2,208,128]{2,1,0:T(8,128)(2,1)S(1)}, bf16[2,208,128]{2,1,0:T(8,128)(2,1)S(1)}, u32[]{:S(2)}, u32[]{:S(2)}) collective-permute-start(bf16[2,208,128]{2,1,0:T(8,128)(2,1)S(1)} %get-tuple-element.525), channel_id=1, source_target_pairs={{0,6},{2,4},{4,2},{6,0},{1,7},{3,5},{5,3},{7,1},{8,14},{10,12},{12... | collective-permute-start | bytes 319496 | tf_op jit(solution)/shard_map/ppermute | solution.py:30
  171.6 18.1 %collective-permute-start.28 = (bf16[2,208,128]{2,1,0:T(8,128)(2,1)S(1)}, bf16[2,208,128]{2,1,0:T(8,128)(2,1)S(1)}, u32[]{:S(2)}, u32[]{:S(2)}) collective-permute-start(bf16[2,208,128]{2,1,0:T(8,128)(2,1)S(1)} %get-tuple-element.526), channel_id=1, source_target_pairs={{0,4},{2,6},{4,0},{6,2},{1,5},{3,7},{5,1},{7,3},{8,12},{10,14},{12... | collective-permute-start | bytes 319496 | tf_op jit(solution)/shard_map/ppermute | solution.py:30
  177.7 12.1 %collective-permute-start.27 = (bf16[2,208,128]{2,1,0:T(8,128)(2,1)S(1)}, bf16[2,208,128]{2,1,0:T(8,128)(2,1)S(1)}, u32[]{:S(2)}, u32[]{:S(2)}) collective-permute-start(bf16[2,208,128]{2,1,0:T(8,128)(2,1)S(1)} %get-tuple-element.524), channel_id=1, source_target_pairs={{0,2},{2,0},{4,6},{6,4},{1,3},{3,1},{5,7},{7,5},{8,10},{10,8},{12,... | collective-permute-start | bytes 319496 | tf_op jit(solution)/shard_map/ppermute | solution.py:30
  177.7 13.2 %collective-permute-start.26 = (bf16[208,1024]{1,0:T(8,128)(2,1)S(1)}, bf16[208,1024]{1,0:T(8,128)(2,1)S(1)}, u32[]{:S(2)}, u32[]{:S(2)}) collective-permute-start(bf16[208,1024]{1,0:T(8,128)(2,1)S(1)} %copy-done.19), channel_id=1, source_target_pairs={{0,1},{1,0},{2,3},{3,2},{4,5},{5,4},{6,7},{7,6},{8,9},{9,8},{10,11... | collective-permute-start | bytes 1277960 | tf_op jit(solution)/shard_map/ppermute | solution.py:30
  190.9 8.2 %collective-permute-start.30 = (bf16[208,1024]{1,0:T(8,128)(2,1)S(1)}, bf16[208,1024]{1,0:T(8,128)(2,1)S(1)}, u32[]{:S(2)}, u32[]{:S(2)}) collective-permute-start(bf16[208,1024]{1,0:T(8,128)(2,1)S(1)} %copy-done.21), channel_id=1, source_target_pairs={{0,1},{1,0},{2,3},{3,2},{4,5},{5,4},{6,7},{7,6},{8,9},{9,8},{10,11... | collective-permute-start | bytes 1277960 | tf_op jit(solution)/shard_map/ppermute | solution.py:30
  199.1 5.2 %collective-permute-start.31 = (bf16[4,512,256]{2,1,0:T(8,128)(2,1)}, bf16[4,512,256]{2,1,0:T(8,128)(2,1)S(1)}, u32[]{:S(2)}, u32[]{:S(2)}) collective-permute-start(bf16[4,512,256]{2,1,0:T(8,128)(2,1)} %get-tuple-element.448), channel_id=1, source_target_pairs={{0,8},{8,0},{16,24},{24,16},{1,9},{9,1},{17,25},{25,17},{2,10},{10... | collective-permute-start | bytes 3145736 | tf_op jit(solution)/shard_map/ppermute | solution.py:30
  199.1 5.5 %collective-permute-start.32 = (bf16[4,512,256]{2,1,0:T(8,128)(2,1)}, bf16[4,512,256]{2,1,0:T(8,128)(2,1)S(1)}, u32[]{:S(2)}, u32[]{:S(2)}) collective-permute-start(bf16[4,512,256]{2,1,0:T(8,128)(2,1)} %get-tuple-element.450), channel_id=1, source_target_pairs={{0,8},{8,0},{16,24},{24,16},{1,9},{9,1},{17,25},{25,17},{2,10},{10... | collective-permute-start | bytes 3145736 | tf_op jit(solution)/shard_map/ppermute | solution.py:30
  205.8 15.2 %collective-permute-start.33 = (bf16[2,512,256]{2,1,0:T(8,128)(2,1)S(1)}, bf16[2,512,256]{2,1,0:T(8,128)(2,1)S(1)}, u32[]{:S(2)}, u32[]{:S(2)}) collective-permute-start(bf16[2,512,256]{2,1,0:T(8,128)(2,1)S(1)} %slice.157), channel_id=1, source_target_pairs={{0,16},{8,24},{16,0},{24,8},{1,17},{9,25},{17,1},{25,9},{2,18},{10... | collective-permute-start | bytes 1572872 | tf_op jit(solution)/shard_map/ppermute | solution.py:30
  210.1 9.1 %collective-permute-start.36 = (f32[8,512]{1,0:T(8,128)S(1)}, f32[8,512]{1,0:T(8,128)S(1)}, u32[]{:S(2)}, u32[]{:S(2)}) collective-permute-start(f32[8,512]{1,0:T(8,128)S(1)} %get-tuple-element.542), channel_id=1, source_target_pairs={{0,24},{8,16},{16,8},{24,0},{1,25},{9,17},{17,9},{25,1},{2,26},{10... | collective-permute-start | bytes 49160 | tf_op jit(solution)/shard_map/ppermute | solution.py:30
  210.1 10.2 %collective-permute-start.35 = (f32[8,512]{1,0:T(8,128)S(1)}, f32[8,512]{1,0:T(8,128)S(1)}, u32[]{:S(2)}, u32[]{:S(2)}) collective-permute-start(f32[8,512]{1,0:T(8,128)S(1)} %get-tuple-element.543), channel_id=1, source_target_pairs={{0,16},{8,24},{16,0},{24,8},{1,17},{9,25},{17,1},{25,9},{2,18},{10... | collective-permute-start | bytes 49160 | tf_op jit(solution)/shard_map/ppermute | solution.py:30
  211.3 8.9 %collective-permute-start.34 = (f32[8,512]{1,0:T(8,128)S(1)}, f32[8,512]{1,0:T(8,128)S(1)}, u32[]{:S(2)}, u32[]{:S(2)}) collective-permute-start(f32[8,512]{1,0:T(8,128)S(1)} %get-tuple-element.541), channel_id=1, source_target_pairs={{0,8},{8,0},{16,24},{24,16},{1,9},{9,1},{17,25},{25,17},{2,10},{10... | collective-permute-start | bytes 49160 | tf_op jit(solution)/shard_map/ppermute | solution.py:30
  221.8 24.3 %collective-permute-start.37 = (bf16[2,512,256]{2,1,0:T(8,128)(2,1)}, bf16[2,512,256]{2,1,0:T(8,128)(2,1)S(1)}, u32[]{:S(2)}, u32[]{:S(2)}) collective-permute-start(bf16[2,512,256]{2,1,0:T(8,128)(2,1)} %slice.162), channel_id=1, source_target_pairs={{0,16},{8,24},{16,0},{24,8},{1,17},{9,25},{17,1},{25,9},{2,18},{10... | collective-permute-start | bytes 1572872 | tf_op jit(solution)/shard_map/ppermute | solution.py:30
  223.4 9.0 %collective-permute-start.41 = (bf16[2,208,128]{2,1,0:T(8,128)(2,1)S(1)}, bf16[2,208,128]{2,1,0:T(8,128)(2,1)S(1)}, u32[]{:S(2)}, u32[]{:S(2)}) collective-permute-start(bf16[2,208,128]{2,1,0:T(8,128)(2,1)S(1)} %get-tuple-element.520), channel_id=1, source_target_pairs={{0,6},{2,4},{4,2},{6,0},{1,7},{3,5},{5,3},{7,1},{8,14},{10,12},{12... | collective-permute-start | bytes 319496 | tf_op jit(solution)/shard_map/ppermute | solution.py:30
  224.4 14.0 %collective-permute-start.40 = (bf16[2,208,128]{2,1,0:T(8,128)(2,1)S(1)}, bf16[2,208,128]{2,1,0:T(8,128)(2,1)S(1)}, u32[]{:S(2)}, u32[]{:S(2)}) collective-permute-start(bf16[2,208,128]{2,1,0:T(8,128)(2,1)S(1)} %get-tuple-element.521), channel_id=1, source_target_pairs={{0,4},{2,6},{4,0},{6,2},{1,5},{3,7},{5,1},{7,3},{8,12},{10,14},{12... | collective-permute-start | bytes 319496 | tf_op jit(solution)/shard_map/ppermute | solution.py:30
  226.6 11.7 %collective-permute-start.39 = (bf16[2,208,128]{2,1,0:T(8,128)(2,1)S(1)}, bf16[2,208,128]{2,1,0:T(8,128)(2,1)S(1)}, u32[]{:S(2)}, u32[]{:S(2)}) collective-permute-start(bf16[2,208,128]{2,1,0:T(8,128)(2,1)S(1)} %get-tuple-element.522), channel_id=1, source_target_pairs={{0,2},{2,0},{4,6},{6,4},{1,3},{3,1},{5,7},{7,5},{8,10},{10,8},{12,... | collective-permute-start | bytes 319496 | tf_op jit(solution)/shard_map/ppermute | solution.py:30
  228.0 13.4 %collective-permute-start.38 = (bf16[512,256]{1,0:T(8,128)(2,1)S(1)}, bf16[512,256]{1,0:T(8,128)(2,1)S(1)}, u32[]{:S(2)}, u32[]{:S(2)}) collective-permute-start(bf16[512,256]{1,0:T(8,128)(2,1)S(1)} %get-tuple-element.513), channel_id=1, source_target_pairs={{0,2},{2,0},{4,6},{6,4},{1,3},{3,1},{5,7},{7,5},{8,10},{10,8},{12,... | collective-permute-start | bytes 786440 | tf_op jit(solution)/shard_map/ppermute | solution.py:30
  247.0 21.3 %collective-permute-start.42 = (bf16[512,256]{1,0:T(8,128)(2,1)S(1)}, bf16[512,256]{1,0:T(8,128)(2,1)S(1)}, u32[]{:S(2)}, u32[]{:S(2)}) collective-permute-start(bf16[512,256]{1,0:T(8,128)(2,1)S(1)} %get-tuple-element.511), channel_id=1, source_target_pairs={{0,2},{2,0},{4,6},{6,4},{1,3},{3,1},{5,7},{7,5},{8,10},{10,8},{12,... | collective-permute-start | bytes 786440 | tf_op jit(solution)/shard_map/ppermute | solution.py:30
  247.0 21.3 %collective-permute-start.43 = (bf16[512,256]{1,0:T(8,128)(2,1)S(1)}, bf16[512,256]{1,0:T(8,128)(2,1)S(1)}, u32[]{:S(2)}, u32[]{:S(2)}) collective-permute-start(bf16[512,256]{1,0:T(8,128)(2,1)S(1)} %add_convert_fusion.2), channel_id=1, source_target_pairs={{0,4},{2,6},{4,0},{6,2},{1,5},{3,7},{5,1},{7,3},{8,12},{10,14},{12... | collective-permute-start | bytes 786440 | tf_op jit(solution)/shard_map/ppermute | solution.py:30
  250.2 17.5 %collective-permute-start.45 = (f32[8,512]{1,0:T(8,128)S(1)}, f32[8,512]{1,0:T(8,128)S(1)}, u32[]{:S(2)}, u32[]{:S(2)}) collective-permute-start(f32[8,512]{1,0:T(8,128)S(1)} %fusion.39), channel_id=1, source_target_pairs={{0,4},{2,6},{4,0},{6,2},{1,5},{3,7},{5,1},{7,3},{8,12},{10,14},{12... | collective-permute-start | bytes 49160 | tf_op jit(solution)/shard_map/ppermute | solution.py:30
  250.3 17.4 %collective-permute-start.46 = (f32[8,512]{1,0:T(8,128)S(1)}, f32[8,512]{1,0:T(8,128)S(1)}, u32[]{:S(2)}, u32[]{:S(2)}) collective-permute-start(f32[8,512]{1,0:T(8,128)S(1)} %fusion.39), channel_id=1, source_target_pairs={{0,6},{2,4},{4,2},{6,0},{1,7},{3,5},{5,3},{7,1},{8,14},{10,12},{12... | collective-permute-start | bytes 49160 | tf_op jit(solution)/shard_map/ppermute | solution.py:30
  252.8 14.9 %collective-permute-start.44 = (f32[8,512]{1,0:T(8,128)S(1)}, f32[8,512]{1,0:T(8,128)S(1)}, u32[]{:S(2)}, u32[]{:S(2)}) collective-permute-start(f32[8,512]{1,0:T(8,128)S(1)} %fusion.39), channel_id=1, source_target_pairs={{0,2},{2,0},{4,6},{6,4},{1,3},{3,1},{5,7},{7,5},{8,10},{10,8},{12,... | collective-permute-start | bytes 49160 | tf_op jit(solution)/shard_map/ppermute | solution.py:30
  (37 other events, 373.9 us)
Sparse Core Ops, SparseCore 0:
  10.8 102.9 all-gather.2
  158.9 122.1 reduce-scatter.1
where the time goes:
time: 293 us; the launch traced here: 292 us
  waiting for transfers between devices  103 us (35%)
  Pallas kernels  90.6 us (31%)
  starting transfers between devices  60.5 us (21%)
  between operations  14.7 us (5%)
  local copies, waits for them, and re-layouts  13 us (4%)
  other arithmetic  10.8 us (4%)
    ppermute x47, waiting for transfers between devices, swap(): return lax.ppermute(values, name, [(i, i ^ bit) for i in range(count)])  97.5 us
    pallas_call x13, Pallas kernels, run_kernel(): pl.pallas_call(body, grid=grid or (1,), in_specs=in_specs, out_specs=out_...  90.6 us
    ppermute x47, starting transfers between devices, swap(): return lax.ppermute(values, name, [(i, i ^ bit) for i in range(count)])  60.4 us
  transfers between devices with their start and end apart: 49, of which 20 were waited for; matrix products, arithmetic and copies ran while one was open for 6% of the time, Pallas kernels for 26%

commit v1 on v0

--- a/solution.py
+++ b/solution.py
@@ -563,8 +563,9 @@
     head_third_x = across(head_third)
     head_own_planes = [*head_plane, *planes(head_x)]
     head_pair_planes = [*planes(head_pair), *planes(head_pair_x)]
-    head_third_x, head_third, head_own_planes, head_pair_planes, far, near, dy_blocks = fence(
-        head_third_x, head_third, head_own_planes, head_pair_planes, far, near, dy_blocks
+    dy_came = send_images(dy_blocks)
+    head_third_x, head_third, head_own_planes, head_pair_planes, far, near, dy_came = fence(
+        head_third_x, head_third, head_own_planes, head_pair_planes, far, near, dy_came
     )
 
     head_third_planes = [*planes(head_third), *planes(head_third_x)]
@@ -609,23 +610,21 @@
             in_specs=[scalars, strips, strips, *head_specs],
         )
 
+    near_dy = jnp.stack(dy_came)
+    far_dy = swap(near_dy, "col", 1)
     done = [forward_one(0)]
-    done, dy_blocks = fence(done, dy_blocks)
+    done, far_dy, near_dy = fence(done, far_dy, near_dy)
 
     came_one = [swap(done[0][5], "col", 1)]
-    dy_came = send_images(dy_blocks)
     done.append(forward_one(1))
     vec = done[0][0]
     unit_rows = sum(b[6 + bias_own.shape[0] :][: unit_own.shape[0]].astype(WIDE) for b in head_small)
     steps = 4
     block = unit_count // steps
     unit_rows = unit_rows.reshape(parts, steps, block).transpose(1, 0, 2).reshape(steps, 1, parts * block)
-    done, came_one, dy_came, unit_rows = fence(done, came_one, dy_came, unit_rows)
+    done, came_one, unit_rows = fence(done, came_one, unit_rows)
 
     came_one = [*came_one, swap(done[1][5], "col", 1)]
-    near_dy = jnp.stack(dy_came)
-    far_dy = swap(near_dy, "col", 1)
-    far_dy, near_dy, came_one = fence(far_dy, near_dy, came_one)
 
     unit_spec = pl.BlockSpec((1, PAD, parts * block), lambda u: (u, 0, 0))
     unit_sum_spec = pl.BlockSpec((1, 1, parts * block), lambda u: (u, 0, 0))
@@ -679,7 +678,7 @@
         in_specs=[scalars, early, early, late, late, *[whole(low_full)] * 4],
         out_specs=[pl.BlockSpec((parts, rows, block, width), lambda u: (0, 0, u, 0))],
     )[0]
-    feed_grad, came_two, fed = fence(feed_grad, came_two, fed)
+    feed_grad, fed = fence(feed_grad, fed)
     feed_total = lax.psum_scatter(feed_grad.reshape(-1, width), ("dp", "row"), scatter_dimension=0, tiled=True)
 
     def fold(blocks):

time: 293 us -> 280 us (0.956)
  waiting for transfers between devices: 103 us -> 86.7 us
  starting transfers between devices: 60.5 us -> 65.4 us
    ppermute x47, waiting for transfers between devices: 97.5 us -> 86.3 us  [swap(): return lax.ppermute(values, name, [(i, i ^ bit) for i in range(count)])]
    ppermute x47, starting transfers between devices: 60.4 us -> 65.3 us  [swap(): return lax.ppermute(values, name, [(i, i ^ bit) for i in range(count)])]
    reduce_scatter x1, waiting for transfers between devices: 5.13 us -> 0.36 us  [on_device(): lax.psum_scatter(feed_grad.reshape(-1, width), ('dp', 'row'), scatter_dim...]
    unnamed x74 -> x82, local copies, waits for them, and re-layouts: 4.29 us -> 7.21 us
  transfers between devices with their start and end apart: 49 -> 49, of which waited for: 20 -> 22; matrix products, arithmetic and copies ran while one was open for 6% -> 5% of each run, Pallas kernels for 26% -> 27%
where the time goes in v1:
time: 280 us; the launch traced here: 279 us
  Pallas kernels  90.1 us (32%)
  waiting for transfers between devices  86.7 us (31%)
  starting transfers between devices  65.4 us (23%)
  between operations  14.8 us (5%)
  local copies, waits for them, and re-layouts  12.3 us (4%)
  other arithmetic  9.88 us (4%)
    pallas_call x13, Pallas kernels, run_kernel(): pl.pallas_call(body, grid=grid or (1,), in_specs=in_specs, out_specs=out_...  90.1 us
    ppermute x47, waiting for transfers between devices, swap(): return lax.ppermute(values, name, [(i, i ^ bit) for i in range(count)])  86.3 us
    ppermute x47, starting transfers between devices, swap(): return lax.ppermute(values, name, [(i, i ^ bit) for i in range(count)])  65.3 us
    unnamed x82, local copies, waits for them, and re-layouts  7.21 us
  transfers between devices with their start and end apart: 49, of which 22 were waited for; matrix products, arithmetic and copies ran while one was open for 5% of the time, Pallas kernels for 27%

profile of v1, /device:TPU:0, one launch (start us, length us, event | category | flops | bytes accessed | tf_op | source)
XLA Modules:
  0.0 279.1 jit_solution(10428551394673729953)
XLA Ops:
  7.3 1.9 pad_maximum_fusion
  10.3 3.1 %collective-permute-start = (bf16[512,256]{1,0:T(8,128)(2,1)S(1)}, bf16[512,256]{1,0:T(8,128)(2,1)}, u32[]{:S(2)}, u32[]{:S(2)}) collective-permute-start(bf16[512,256]{1,0:T(8,128)(2,1)S(1)} %pad_maximum_fusion.11.refs_0_), channel_id=1, source_target_pairs={{0,2},{2,0},{4,6},{6,4},{1,3},{3,1},{5,7},{7,5},{8,10},{10,8},{12,... | collective-permute-start | bytes 786440 | tf_op jit(solution)/shard_map/ppermute | solution.py:30
  13.3 2.6 collective-permute-start.1
  15.9 1.5 collective-permute-start.2
  17.7 1.6 collective-permute-start.4
  22.2 4.0 %collective-permute-done = bf16[512,256]{1,0:T(8,128)(2,1)} collective-permute-done((bf16[512,256]{1,0:T(8,128)(2,1)S(1)}, bf16[512,256]{1,0:T(8,128)(2,1)}, u32[]{:S(2)}, u32[]{:S(2)}) %collective-permute-start) | collective-permute-done | bytes 262176 | tf_op jit(solution)/shard_map/ppermute | solution.py:30
  26.2 1.9 collective-permute-done.1
  29.3 1.5 collective-permute-start.9
  31.2 4.4 %collective-permute-start.5 = (bf16[512,256]{1,0:T(8,128)(2,1)S(1)}, bf16[512,256]{1,0:T(8,128)(2,1)}, u32[]{:S(2)}, u32[]{:S(2)}) collective-permute-start(bf16[512,256]{1,0:T(8,128)(2,1)S(1)} %collective-permute-done.1), channel_id=1, source_target_pairs={{0,2},{2,0},{4,6},{6,4},{1,3},{3,1},{5,7},{7,5},{8,10},{10,8},{12,... | collective-permute-start | bytes 786440 | tf_op jit(solution)/shard_map/ppermute | solution.py:30
  36.1 4.4 %collective-permute-start.7 = (bf16[2,216,128]{2,1,0:T(8,128)(2,1)S(1)}, bf16[2,216,128]{2,1,0:T(8,128)(2,1)S(1)}, u32[]{:S(2)}, u32[]{:S(2)}) collective-permute-start(bf16[2,216,128]{2,1,0:T(8,128)(2,1)S(1)} %copy-done.36), channel_id=1, source_target_pairs={{0,4},{2,6},{4,0},{6,2},{1,5},{3,7},{5,1},{7,3},{8,12},{10,14},{12... | collective-permute-start | bytes 331784 | tf_op jit(solution)/shard_map/ppermute | solution.py:30
  40.5 1.4 collective-permute-start.8
  41.9 12.6 %collective-permute-done.6 = bf16[2,216,128]{2,1,0:T(8,128)(2,1)S(1)} collective-permute-done((bf16[2,216,128]{2,1,0:T(8,128)(2,1)}, bf16[2,216,128]{2,1,0:T(8,128)(2,1)S(1)}, u32[]{:S(2)}, u32[]{:S(2)}) %collective-permute-start.6) | collective-permute-done | bytes 110624 | tf_op jit(solution)/shard_map/ppermute | solution.py:30
  54.5 4.4 %collective-permute-start.16 = (bf16[2,208,128]{2,1,0:T(8,128)(2,1)S(1)}, bf16[2,208,128]{2,1,0:T(8,128)(2,1)S(1)}, u32[]{:S(2)}, u32[]{:S(2)}) collective-permute-start(bf16[2,208,128]{2,1,0:T(8,128)(2,1)S(1)} %get-tuple-element.505), channel_id=1, source_target_pairs={{0,4},{2,6},{4,0},{6,2},{1,5},{3,7},{5,1},{7,3},{8,12},{10,14},{12... | collective-permute-start | bytes 319496 | tf_op jit(solution)/shard_map/ppermute | solution.py:30
  60.5 1.3 collective-permute-start.14
  62.8 7.4 %collective-permute-done.16 = bf16[2,208,128]{2,1,0:T(8,128)(2,1)S(1)} collective-permute-done((bf16[2,208,128]{2,1,0:T(8,128)(2,1)S(1)}, bf16[2,208,128]{2,1,0:T(8,128)(2,1)S(1)}, u32[]{:S(2)}, u32[]{:S(2)}) %collective-permute-start.16) | collective-permute-done | bytes 106528 | tf_op jit(solution)/shard_map/ppermute | solution.py:30
  70.1 1.9 collective-permute-start.10
  72.0 1.5 collective-permute-done.11.refs_3_
  73.5 11.2 %collective-permute-done.10.refs_10_ = bf16[640,256]{1,0:T(8,128)(2,1)S(1)} collective-permute-done((bf16[640,256]{1,0:T(8,128)(2,1)S(1)}, bf16[640,256]{1,0:T(8,128)(2,1)S(1)}, u32[]{:S(2)}, u32[]{:S(2)}) %collective-permute-start.10) | collective-permute-done | bytes 327712 | tf_op jit(solution)/shard_map/ppermute | solution.py:30
  84.9 2.4 collective-permute-start.20
  90.4 6.5 %shard_map.335 = (f32[8,1024]{1,0:T(8,128)}, bf16[208,1024]{1,0:T(8,128)(2,1)}, bf16[208,1024]{1,0:T(8,128)(2,1)}, bf16[208,1536]{1,0:T(8,128)(2,1)}, bf16[208,5...) custom-call(s32[3]{0:T(128)} %pad_add_fusion.pos, bf16[4,2,208,128]{3,2,1,0:T(8,128)(2,1)} %copy-done.12, ...), custom_call_target="tpu_custom_call" | custom-call | flops 1024 | bytes 1024 | tf_op jit(solution)/shard_map/pallas_call | solution.py:474
  99.1 6.4 %shard_map.336 = (f32[8,1024]{1,0:T(8,128)}, bf16[208,1024]{1,0:T(8,128)(2,1)}, bf16[208,1024]{1,0:T(8,128)(2,1)}, bf16[208,1536]{1,0:T(8,128)(2,1)}, bf16[208,5...) custom-call(s32[3]{0:T(128)} %pad_add_fusion.pos, bf16[4,2,208,128]{3,2,1,0:T(8,128)(2,1)} %copy-done.12, ...), custom_call_target="tpu_custom_call" | custom-call | flops 1024 | bytes 1024 | tf_op jit(solution)/shard_map/pallas_call | solution.py:474
  105.4 4.1 %collective-permute-done.21.came = bf16[208,1024]{1,0:T(8,128)(2,1)S(1)} collective-permute-done((bf16[208,1024]{1,0:T(8,128)(2,1)}, bf16[208,1024]{1,0:T(8,128)(2,1)S(1)}, u32[]{:S(2)}, u32[]{:S(2)}) %collective-permute-start.21) | collective-permute-done | bytes 426016 | tf_op jit(solution)/shard_map/ppermute | solution.py:30
  110.3 10.8 %shard_map.337 = (f32[208,1024]{1,0:T(8,128)}, bf16[208,1024]{1,0:T(8,128)(2,1)}, bf16[208,1024]{1,0:T(8,128)(2,1)}, f32[1,1024]{1,0:T(1,128)}, bf16[4,208,512]{...) custom-call(s32[3]{0:T(128)} %pad_add_fusion.pos, ...), custom_call_target="tpu_custom_call" | custom-call | flops 1024 | bytes 1024 | tf_op jit(solution)/shard_map/pallas_call | solution.py:474
  121.2 1.3 collective-permute-start.23
  122.5 10.7 %shard_map.338 = (f32[208,1024]{1,0:T(8,128)}, bf16[208,1024]{1,0:T(8,128)(2,1)}, bf16[208,1024]{1,0:T(8,128)(2,1)}, f32[1,1024]{1,0:T(1,128)}, bf16[4,208,512]{...) custom-call(s32[3]{0:T(128)} %pad_add_fusion.pos, ...), custom_call_target="tpu_custom_call" | custom-call | flops 1024 | bytes 1024 | tf_op jit(solution)/shard_map/pallas_call | solution.py:474
  133.2 11.2 %shard_map.339 = bf16[4,4,1024,256]{3,2,1,0:T(8,128)(2,1)} custom-call(s32[3]{0:T(128)} %pad_add_fusion.pos, bf16[4,208,512]{2,1,0:T(8,128)(2,1)} %get-tuple-element.350.refs_0_, bf16[4,208,512]{2,1,0:T(8,128)(2,1)} %get-tuple-element.351.refs_1_, bf16[4,208,512]{2,1,0:T(8,128)(2,1)} %get-tuple-element.352.refs_2_, ...), custom_call_target="tpu_custom_call" | custom-call | flops 1024 | bytes 1024 | tf_op jit(solution)/shard_map/pallas_call | solution.py:474
  146.4 1.3 collective-permute-start.25
  147.6 10.1 %shard_map.340 = (f32[208,1024]{1,0:T(8,128)}, bf16[208,1024]{1,0:T(8,128)(2,1)}, bf16[208,1536]{1,0:T(8,128)(2,1)}, bf16[208,1024]{1,0:T(8,128)(2,1)}, f32[8,1024]{1,0:T(8,128)}, /*index=5*/f32[1,1536]{1,0:T(1,128)}) custom-call(s32[3]{0:T(128)} %pad_add_fusion.pos, f32[8,1024]{1,0:T(8,128)} %get-tuple-element.297.vec, f32[208,1024]{1,0:T(8,128)} %get-tuple-element.371.mid, ...), custom_call_target="tpu_custom_call" | custom-call | flops 1024 | bytes 1024 | tf_op jit(solution)/shard_map/pallas_call | solution.py:474
  158.5 4.2 %collective-permute-start.29 = (bf16[2,208,128]{2,1,0:T(8,128)(2,1)S(1)}, bf16[2,208,128]{2,1,0:T(8,128)(2,1)S(1)}, u32[]{:S(2)}, u32[]{:S(2)}) collective-permute-start(bf16[2,208,128]{2,1,0:T(8,128)(2,1)S(1)} %get-tuple-element.499), channel_id=1, source_target_pairs={{0,6},{2,4},{4,2},{6,0},{1,7},{3,5},{5,3},{7,1},{8,14},{10,12},{12... | collective-permute-start | bytes 319496 | tf_op jit(solution)/shard_map/ppermute | solution.py:30
  164.1 2.9 %collective-permute-done.25.came = bf16[208,1024]{1,0:T(8,128)(2,1)S(1)} collective-permute-done((bf16[208,1024]{1,0:T(8,128)(2,1)S(1)}, bf16[208,1024]{1,0:T(8,128)(2,1)S(1)}, u32[]{:S(2)}, u32[]{:S(2)}) %collective-permute-start.25) | collective-permute-done | bytes 426016 | tf_op jit(solution)/shard_map/ppermute | solution.py:30
  167.8 10.2 %shard_map.341 = (f32[208,1024]{1,0:T(8,128)}, bf16[208,1024]{1,0:T(8,128)(2,1)}, bf16[208,1536]{1,0:T(8,128)(2,1)}, bf16[208,1024]{1,0:T(8,128)(2,1)}, f32[8,1024]{1,0:T(8,128)}, /*index=5*/f32[1,1536]{1,0:T(1,128)}) custom-call(s32[3]{0:T(128)} %pad_add_fusion.pos, f32[8,1024]{1,0:T(8,128)} %get-tuple-element.297.vec, f32[208,1024]{1,0:T(8,128)} %get-tuple-element.391.mid, ...), custom_call_target="tpu_custom_call" | custom-call | flops 1024 | bytes 1024 | tf_op jit(solution)/shard_map/pallas_call | solution.py:474
  179.2 1.2 collective-permute-start.30
  180.4 6.6 %shard_map.342 = (bf16[4,512,256]{2,1,0:T(8,128)(2,1)}, bf16[4,512,256]{2,1,0:T(8,128)(2,1)}, bf16[4,512,256]{2,1,0:T(8,128)(2,1)}, bf16[4,512,256]{2,1,0:T(8,128)(2,1)}) custom-call(s32[3]{0:T(128)} %pad_add_fusion.pos, bf16[208,1536]{1,0:T(8,128)(2,1)} %get-tuple-element.406.refs_0_, bf16[208,1536]{1,0:T(8,128)(2,1)} %get-tuple-element.407.refs_1_, ...), custom_call_target="tpu_custom_call" | custom-call | flops 1024 | bytes 1024 | tf_op jit(solution)/shard_map/pallas_call | solution.py:474
  188.1 4.4 %shard_map.343 = (bf16[4,2,208,128]{3,2,1,0:T(8,128)(2,1)}, f32[8,1024]{1,0:T(8,128)}) custom-call(s32[3]{0:T(128)} %pad_add_fusion.pos, f32[8,1024]{1,0:T(8,128)} %get-tuple-element.297.vec, bf16[208,1024]{1,0:T(8,128)(2,1)} %get-tuple-element.310.x.refs_0_, bf16[208,1024]{1,0:T(8,128)(2,1)} %get-tuple-element.337.x.refs_1_, ...), custom_call_target="tpu_custom_call" | custom-call | flops 1024 | bytes 1024 | tf_op jit(solution)/shard_map/pallas_call | solution.py:474
  195.1 1.9 shard_map.344
  199.7 7.3 %collective-permute-done.36 = f32[8,512]{1,0:T(8,128)S(1)} collective-permute-done((f32[8,512]{1,0:T(8,128)S(1)}, f32[8,512]{1,0:T(8,128)S(1)}, u32[]{:S(2)}, u32[]{:S(2)}) %collective-permute-start.36) | collective-permute-done | bytes 16416 | tf_op jit(solution)/shard_map/ppermute | solution.py:30
  207.0 1.5 collective-permute-done.35
  210.4 10.1 %collective-permute-start.41 = (bf16[2,208,128]{2,1,0:T(8,128)(2,1)S(1)}, bf16[2,208,128]{2,1,0:T(8,128)(2,1)S(1)}, u32[]{:S(2)}, u32[]{:S(2)}) collective-permute-start(bf16[2,208,128]{2,1,0:T(8,128)(2,1)S(1)} %get-tuple-element.494), channel_id=1, source_target_pairs={{0,6},{2,4},{4,2},{6,0},{1,7},{3,5},{5,3},{7,1},{8,14},{10,12},{12... | collective-permute-start | bytes 319496 | tf_op jit(solution)/shard_map/ppermute | solution.py:30
  222.0 1.4 collective-permute-start.38
  224.3 3.4 %collective-permute-done.40 = bf16[2,208,128]{2,1,0:T(8,128)(2,1)S(1)} collective-permute-done((bf16[2,208,128]{2,1,0:T(8,128)(2,1)S(1)}, bf16[2,208,128]{2,1,0:T(8,128)(2,1)S(1)}, u32[]{:S(2)}, u32[]{:S(2)}) %collective-permute-start.40) | collective-permute-done | bytes 106528 | tf_op jit(solution)/shard_map/ppermute | solution.py:30
  229.9 3.6 %collective-permute-done.38 = bf16[512,256]{1,0:T(8,128)(2,1)S(1)} collective-permute-done((bf16[512,256]{1,0:T(8,128)(2,1)}, bf16[512,256]{1,0:T(8,128)(2,1)S(1)}, u32[]{:S(2)}, u32[]{:S(2)}) %collective-permute-start.38) | collective-permute-done | bytes 262176 | tf_op jit(solution)/shard_map/ppermute | solution.py:30
  234.3 1.5 collective-permute-start.42
  235.9 1.6 collective-permute-start.43
  237.5 1.4 collective-permute-start.45
  241.0 18.3 %collective-permute-done.45 = f32[8,512]{1,0:T(8,128)S(1)} collective-permute-done((f32[8,512]{1,0:T(8,128)S(1)}, f32[8,512]{1,0:T(8,128)S(1)}, u32[]{:S(2)}, u32[]{:S(2)}) %collective-permute-start.45) | collective-permute-done | bytes 16416 | tf_op jit(solution)/shard_map/ppermute | solution.py:30
  260.6 3.3 %shard_map.345 = (f32[384,256]{1,0:T(8,128)}, f32[384,256]{1,0:T(8,128)}, f32[2,384,256]{2,1,0:T(8,128)}, f32[128,256]{1,0:T(8,128)}, f32[128,256]{1,0:T(8,128)}, /*index=5*/f32[2,128,256]{2,1,0:T(8,128)}) custom-call(bf16[512,256]{1,0:T(8,128)(2,1)} %get-tuple-element.458.first, bf16[512,256]{1,0:T(8,128)(2,1)} %copy-done.32, bf16[512,256]{1,0:T(8,128)(2,1)} %copy-done.33, ...), custom_call_target="tpu_custom_call" | custom-call | flops 1024 | bytes 1024 | tf_op jit(solution)/shard_map/pallas_call | solution.py:474
  263.9 3.7 %shard_map.346 = (f32[2,8,16]{2,1,0:T(8,128)}, f32[16,32]{1,0:T(8,128)}, f32[6,2,16]{2,1,0:T(2,128)}, f32[2,8,16]{2,1,0:T(8,128)}, f32[16,32]{1,0:T(8,128)}, /*i...) custom-call(s32[3]{0:T(128)} %pad_add_fusion.pos, ...), custom_call_target="tpu_custom_call" | custom-call | flops 1024 | bytes 1024 | tf_op jit(solution)/shard_map/pallas_call | solution.py:474
  268.0 4.3 %shard_map.347 = (f32[512,256]{1,0:T(8,128)}, f32[512,256]{1,0:T(8,128)}, f32[2,512,256]{2,1,0:T(8,128)}, f32[512,256]{1,0:T(8,128)}, f32[512,256]{1,0:T(8,128)}, /*index=5*/f32[2,512,256]{2,1,0:T(8,128)}) custom-call(bf16[1024,256]{1,0:T(8,128)(2,1)} %reduce-scatter.2.cloned.1.call-done.first, bf16[512,256]{1,0:T(8,128)(2,1)} %bitcast.185, ...), custom_call_target="tpu_custom_call" | custom-call | flops 1024 | bytes 1024 | tf_op jit(solution)/shard_map/pallas_call | solution.py:474
  (213 shorter events, 38.3 us)
Async XLA Ops:
  7.2 102.6 %all-gather.3.cloned.1.call-start = ((), (), s32[]{:S(2)}) async-start(), calls=%async_computation.2 | async-start | bytes 8912896 | tf_op jit(solution)/shard_map/all_gather | solution.py:544
  9.2 258.8 %reduce-scatter.2.cloned.1.call-start = ((), (), s32[]{:S(2)}) async-start(), calls=%async_computation.1 | async-start | bytes 8912896 | tf_op jit(solution)/shard_map/reduce_scatter | solution.py:682
  10.3 15.9 %collective-permute-start = (bf16[512,256]{1,0:T(8,128)(2,1)S(1)}, bf16[512,256]{1,0:T(8,128)(2,1)}, u32[]{:S(2)}, u32[]{:S(2)}) collective-permute-start(bf16[512,256]{1,0:T(8,128)(2,1)S(1)} %pad_maximum_fusion.11.refs_0_), channel_id=1, source_target_pairs={{0,2},{2,0},{4,6},{6,4},{1,3},{3,1},{5,7},{7,5},{8,10},{10,8},{12,... | collective-permute-start | bytes 786440 | tf_op jit(solution)/shard_map/ppermute | solution.py:30
  13.3 14.7 %collective-permute-start.1 = (bf16[512,256]{1,0:T(8,128)(2,1)S(1)}, bf16[512,256]{1,0:T(8,128)(2,1)S(1)}, u32[]{:S(2)}, u32[]{:S(2)}) collective-permute-start(bf16[512,256]{1,0:T(8,128)(2,1)S(1)} %pad_maximum_fusion.11.refs_0_), channel_id=1, source_target_pairs={{0,4},{2,6},{4,0},{6,2},{1,5},{3,7},{5,1},{7,3},{8,12},{10,14},{12... | collective-permute-start | bytes 786440 | tf_op jit(solution)/shard_map/ppermute | solution.py:30
  15.9 12.1 %collective-permute-start.2 = (bf16[512,256]{1,0:T(8,128)(2,1)S(1)}, bf16[512,256]{1,0:T(8,128)(2,1)S(1)}, u32[]{:S(2)}, u32[]{:S(2)}) collective-permute-start(bf16[512,256]{1,0:T(8,128)(2,1)S(1)} %pad_maximum_fusion.11.refs_0_), channel_id=1, source_target_pairs={{0,16},{8,24},{16,0},{24,8},{1,17},{9,25},{17,1},{25,9},{2,18},{10... | collective-permute-start | bytes 786440 | tf_op jit(solution)/shard_map/ppermute | solution.py:30
  17.4 10.6 %collective-permute-start.3 = (bf16[512,256]{1,0:T(8,128)(2,1)S(1)}, bf16[512,256]{1,0:T(8,128)(2,1)S(1)}, u32[]{:S(2)}, u32[]{:S(2)}) collective-permute-start(bf16[512,256]{1,0:T(8,128)(2,1)S(1)} %pad_maximum_fusion.11.refs_0_), channel_id=1, source_target_pairs={{0,8},{8,0},{16,24},{24,16},{1,9},{9,1},{17,25},{25,17},{2,10},{10... | collective-permute-start | bytes 786440 | tf_op jit(solution)/shard_map/ppermute | solution.py:30
  17.7 3.6 %collective-permute-start.4 = (bf16[6,128]{1,0:T(8,128)(2,1)S(1)}, bf16[6,128]{1,0:T(8,128)(2,1)S(1)}, u32[]{:S(2)}, u32[]{:S(2)}) collective-permute-start(bf16[6,128]{1,0:T(8,128)(2,1)S(1)} %broadcast_select_fusion.2), channel_id=1, source_target_pairs={{0,1},{1,0},{2,3},{3,2},{4,5},{5,4},{6,7},{7,6},{8,9},{9,8},{10,11... | collective-permute-start | bytes 4616 | tf_op jit(solution)/shard_map/ppermute | solution.py:30
  29.3 29.7 %collective-permute-start.9 = (bf16[1024,256]{1,0:T(8,128)(2,1)S(1)}, bf16[1024,256]{1,0:T(8,128)(2,1)S(1)}, u32[]{:S(2)}, u32[]{:S(2)}) collective-permute-start(bf16[1024,256]{1,0:T(8,128)(2,1)S(1)} %constant_dynamic-update-slice_fusion.refs_4_), channel_id=1, source_target_pairs={{0,16},{8,24},{16,0},{24,8},{1,17},{9,25},{17,1},{25,9},{2,18},{10... | collective-permute-start | bytes 1572872 | tf_op jit(solution)/shard_map/ppermute | solution.py:30
  31.2 27.7 %collective-permute-start.5 = (bf16[512,256]{1,0:T(8,128)(2,1)S(1)}, bf16[512,256]{1,0:T(8,128)(2,1)}, u32[]{:S(2)}, u32[]{:S(2)}) collective-permute-start(bf16[512,256]{1,0:T(8,128)(2,1)S(1)} %collective-permute-done.1), channel_id=1, source_target_pairs={{0,2},{2,0},{4,6},{6,4},{1,3},{3,1},{5,7},{7,5},{8,10},{10,8},{12,... | collective-permute-start | bytes 786440 | tf_op jit(solution)/shard_map/ppermute | solution.py:30
  36.1 18.5 %collective-permute-start.6 = (bf16[2,216,128]{2,1,0:T(8,128)(2,1)}, bf16[2,216,128]{2,1,0:T(8,128)(2,1)S(1)}, u32[]{:S(2)}, u32[]{:S(2)}) collective-permute-start(bf16[2,216,128]{2,1,0:T(8,128)(2,1)} %get-tuple-element.257), channel_id=1, source_target_pairs={{0,2},{2,0},{4,6},{6,4},{1,3},{3,1},{5,7},{7,5},{8,10},{10,8},{12,... | collective-permute-start | bytes 331784 | tf_op jit(solution)/shard_map/ppermute | solution.py:30
  36.1 18.4 %collective-permute-start.7 = (bf16[2,216,128]{2,1,0:T(8,128)(2,1)S(1)}, bf16[2,216,128]{2,1,0:T(8,128)(2,1)S(1)}, u32[]{:S(2)}, u32[]{:S(2)}) collective-permute-start(bf16[2,216,128]{2,1,0:T(8,128)(2,1)S(1)} %copy-done.36), channel_id=1, source_target_pairs={{0,4},{2,6},{4,0},{6,2},{1,5},{3,7},{5,1},{7,3},{8,12},{10,14},{12... | collective-permute-start | bytes 331784 | tf_op jit(solution)/shard_map/ppermute | solution.py:30
  40.5 18.4 %collective-permute-start.8 = (bf16[2,216,128]{2,1,0:T(8,128)(2,1)S(1)}, bf16[2,216,128]{2,1,0:T(8,128)(2,1)S(1)}, u32[]{:S(2)}, u32[]{:S(2)}) collective-permute-start(bf16[2,216,128]{2,1,0:T(8,128)(2,1)S(1)} %get-tuple-element.259), channel_id=1, source_target_pairs={{0,6},{2,4},{4,2},{6,0},{1,7},{3,5},{5,3},{7,1},{8,14},{10,12},{12... | collective-permute-start | bytes 331784 | tf_op jit(solution)/shard_map/ppermute | solution.py:30
  54.5 5.9 %collective-permute-start.15 = (bf16[2,208,128]{2,1,0:T(8,128)(2,1)S(1)}, bf16[2,208,128]{2,1,0:T(8,128)(2,1)S(1)}, u32[]{:S(2)}, u32[]{:S(2)}) collective-permute-start(bf16[2,208,128]{2,1,0:T(8,128)(2,1)S(1)} %get-tuple-element.504), channel_id=1, source_target_pairs={{0,2},{2,0},{4,6},{6,4},{1,3},{3,1},{5,7},{7,5},{8,10},{10,8},{12,... | collective-permute-start | bytes 319496 | tf_op jit(solution)/shard_map/ppermute | solution.py:30
  54.5 15.6 %collective-permute-start.16 = (bf16[2,208,128]{2,1,0:T(8,128)(2,1)S(1)}, bf16[2,208,128]{2,1,0:T(8,128)(2,1)S(1)}, u32[]{:S(2)}, u32[]{:S(2)}) collective-permute-start(bf16[2,208,128]{2,1,0:T(8,128)(2,1)S(1)} %get-tuple-element.505), channel_id=1, source_target_pairs={{0,4},{2,6},{4,0},{6,2},{1,5},{3,7},{5,1},{7,3},{8,12},{10,14},{12... | collective-permute-start | bytes 319496 | tf_op jit(solution)/shard_map/ppermute | solution.py:30
  58.9 13.1 %collective-permute-start.17 = (bf16[2,208,128]{2,1,0:T(8,128)(2,1)S(1)}, bf16[2,208,128]{2,1,0:T(8,128)(2,1)S(1)}, u32[]{:S(2)}, u32[]{:S(2)}) collective-permute-start(bf16[2,208,128]{2,1,0:T(8,128)(2,1)S(1)} %get-tuple-element.503), channel_id=1, source_target_pairs={{0,6},{2,4},{4,2},{6,0},{1,7},{3,5},{5,3},{7,1},{8,14},{10,12},{12... | collective-permute-start | bytes 319496 | tf_op jit(solution)/shard_map/ppermute | solution.py:30
  58.9 25.8 %collective-permute-start.12 = (bf16[1024,256]{1,0:T(8,128)(2,1)S(1)}, bf16[1024,256]{1,0:T(8,128)(2,1)S(1)}, u32[]{:S(2)}, u32[]{:S(2)}) collective-permute-start(bf16[1024,256]{1,0:T(8,128)(2,1)S(1)} %constant_dynamic-update-slice_fusion.refs_4_), channel_id=1, source_target_pairs={{0,8},{8,0},{16,24},{24,16},{1,9},{9,1},{17,25},{25,17},{2,10},{10... | collective-permute-start | bytes 1572872 | tf_op jit(solution)/shard_map/ppermute | solution.py:30
  59.0 25.8 %collective-permute-start.13 = (bf16[1024,256]{1,0:T(8,128)(2,1)S(1)}, bf16[1024,256]{1,0:T(8,128)(2,1)S(1)}, u32[]{:S(2)}, u32[]{:S(2)}) collective-permute-start(bf16[1024,256]{1,0:T(8,128)(2,1)S(1)} %collective-permute-done.9.refs_6_), channel_id=1, source_target_pairs={{0,8},{8,0},{16,24},{24,16},{1,9},{9,1},{17,25},{25,17},{2,10},{10... | collective-permute-start | bytes 1572872 | tf_op jit(solution)/shard_map/ppermute | solution.py:30
  60.5 24.3 %collective-permute-start.14 = (bf16[4,2,208,128]{3,2,1,0:T(8,128)(2,1)S(1)}, bf16[4,2,208,128]{3,2,1,0:T(8,128)(2,1)S(1)}, u32[]{:S(2)}, u32[]{:S(2)}) collective-permute-start(bf16[4,2,208,128]{3,2,1,0:T(8,128)(2,1)S(1)} %pad_maximum_fusion.1.near), channel_id=1, source_target_pairs={{0,1},{1,0},{2,3},{3,2},{4,5},{5,4},{6,7},{7,6},{8,9},{9,8},{10,11... | collective-permute-start | bytes 1277960 | tf_op jit(solution)/shard_map/ppermute | solution.py:30
  70.1 14.6 %collective-permute-start.10 = (bf16[640,256]{1,0:T(8,128)(2,1)S(1)}, bf16[640,256]{1,0:T(8,128)(2,1)S(1)}, u32[]{:S(2)}, u32[]{:S(2)}) collective-permute-start(bf16[640,256]{1,0:T(8,128)(2,1)S(1)} %pad_maximum_fusion.10.refs_8_), channel_id=1, source_target_pairs={{0,16},{8,24},{16,0},{24,8},{1,17},{9,25},{17,1},{25,9},{2,18},{10... | collective-permute-start | bytes 983048 | tf_op jit(solution)/shard_map/ppermute | solution.py:30
  84.9 12.0 %collective-permute-start.20 = (bf16[4,2,208,128]{3,2,1,0:T(8,128)(2,1)S(1)}, bf16[4,2,208,128]{3,2,1,0:T(8,128)(2,1)S(1)}, u32[]{:S(2)}, u32[]{:S(2)}) collective-permute-start(bf16[4,2,208,128]{3,2,1,0:T(8,128)(2,1)S(1)} %pad_maximum_fusion.2.near), channel_id=1, source_target_pairs={{0,1},{1,0},{2,3},{3,2},{4,5},{5,4},{6,7},{7,6},{8,9},{9,8},{10,11... | collective-permute-start | bytes 1277960 | tf_op jit(solution)/shard_map/ppermute | solution.py:30
  87.3 1.6 collective-permute-start.18
  87.3 2.1 collective-permute-start.19
  97.6 11.9 %collective-permute-start.21 = (bf16[208,1024]{1,0:T(8,128)(2,1)}, bf16[208,1024]{1,0:T(8,128)(2,1)S(1)}, u32[]{:S(2)}, u32[]{:S(2)}) collective-permute-start(bf16[208,1024]{1,0:T(8,128)(2,1)} %get-tuple-element.311.part), channel_id=1, source_target_pairs={{0,1},{1,0},{2,3},{3,2},{4,5},{5,4},{6,7},{7,6},{8,9},{9,8},{10,11... | collective-permute-start | bytes 1277960 | tf_op jit(solution)/shard_map/ppermute | solution.py:30
  109.6 11.6 %collective-permute-start.22 = (bf16[208,1024]{1,0:T(8,128)(2,1)}, bf16[208,1024]{1,0:T(8,128)(2,1)S(1)}, u32[]{:S(2)}, u32[]{:S(2)}) collective-permute-start(bf16[208,1024]{1,0:T(8,128)(2,1)} %get-tuple-element.325.part), channel_id=1, source_target_pairs={{0,1},{1,0},{2,3},{3,2},{4,5},{5,4},{6,7},{7,6},{8,9},{9,8},{10,11... | collective-permute-start | bytes 1277960 | tf_op jit(solution)/shard_map/ppermute | solution.py:30
  121.2 12.0 %collective-permute-start.23 = (bf16[208,1024]{1,0:T(8,128)(2,1)}, bf16[208,1024]{1,0:T(8,128)(2,1)S(1)}, u32[]{:S(2)}, u32[]{:S(2)}) collective-permute-start(bf16[208,1024]{1,0:T(8,128)(2,1)} %get-tuple-element.372.back), channel_id=1, source_target_pairs={{0,1},{1,0},{2,3},{3,2},{4,5},{5,4},{6,7},{7,6},{8,9},{9,8},{10,11... | collective-permute-start | bytes 1277960 | tf_op jit(solution)/shard_map/ppermute | solution.py:30
  145.5 12.8 %collective-permute-start.24 = (bf16[2,4,208,128]{3,2,1,0:T(8,128)(2,1)S(1)}, bf16[2,4,208,128]{3,2,1,0:T(8,128)(2,1)S(1)}, u32[]{:S(2)}, u32[]{:S(2)}) collective-permute-start(bf16[2,4,208,128]{3,2,1,0:T(8,128)(2,1)S(1)} %pad_maximum_fusion.3), channel_id=1, source_target_pairs={{0,1},{1,0},{2,3},{3,2},{4,5},{5,4},{6,7},{7,6},{8,9},{9,8},{10,11... | collective-permute-start | bytes 1277960 | tf_op jit(solution)/shard_map/ppermute | solution.py:30
  146.4 20.7 %collective-permute-start.25 = (bf16[208,1024]{1,0:T(8,128)(2,1)S(1)}, bf16[208,1024]{1,0:T(8,128)(2,1)S(1)}, u32[]{:S(2)}, u32[]{:S(2)}) collective-permute-start(bf16[208,1024]{1,0:T(8,128)(2,1)S(1)} %copy-done.20), channel_id=1, source_target_pairs={{0,1},{1,0},{2,3},{3,2},{4,5},{5,4},{6,7},{7,6},{8,9},{9,8},{10,11... | collective-permute-start | bytes 1277960 | tf_op jit(solution)/shard_map/ppermute | solution.py:30
  158.5 19.5 %collective-permute-start.29 = (bf16[2,208,128]{2,1,0:T(8,128)(2,1)S(1)}, bf16[2,208,128]{2,1,0:T(8,128)(2,1)S(1)}, u32[]{:S(2)}, u32[]{:S(2)}) collective-permute-start(bf16[2,208,128]{2,1,0:T(8,128)(2,1)S(1)} %get-tuple-element.499), channel_id=1, source_target_pairs={{0,6},{2,4},{4,2},{6,0},{1,7},{3,5},{5,3},{7,1},{8,14},{10,12},{12... | collective-permute-start | bytes 319496 | tf_op jit(solution)/shard_map/ppermute | solution.py:30
  162.7 15.3 %collective-permute-start.28 = (bf16[2,208,128]{2,1,0:T(8,128)(2,1)S(1)}, bf16[2,208,128]{2,1,0:T(8,128)(2,1)S(1)}, u32[]{:S(2)}, u32[]{:S(2)}) collective-permute-start(bf16[2,208,128]{2,1,0:T(8,128)(2,1)S(1)} %get-tuple-element.500), channel_id=1, source_target_pairs={{0,4},{2,6},{4,0},{6,2},{1,5},{3,7},{5,1},{7,3},{8,12},{10,14},{12... | collective-permute-start | bytes 319496 | tf_op jit(solution)/shard_map/ppermute | solution.py:30
  162.7 15.3 %collective-permute-start.27 = (bf16[2,208,128]{2,1,0:T(8,128)(2,1)S(1)}, bf16[2,208,128]{2,1,0:T(8,128)(2,1)S(1)}, u32[]{:S(2)}, u32[]{:S(2)}) collective-permute-start(bf16[2,208,128]{2,1,0:T(8,128)(2,1)S(1)} %get-tuple-element.498), channel_id=1, source_target_pairs={{0,2},{2,0},{4,6},{6,4},{1,3},{3,1},{5,7},{7,5},{8,10},{10,8},{12,... | collective-permute-start | bytes 319496 | tf_op jit(solution)/shard_map/ppermute | solution.py:30
  163.4 15.8 %collective-permute-start.26 = (bf16[208,1024]{1,0:T(8,128)(2,1)S(1)}, bf16[208,1024]{1,0:T(8,128)(2,1)S(1)}, u32[]{:S(2)}, u32[]{:S(2)}) collective-permute-start(bf16[208,1024]{1,0:T(8,128)(2,1)S(1)} %copy-done.23), channel_id=1, source_target_pairs={{0,1},{1,0},{2,3},{3,2},{4,5},{5,4},{6,7},{7,6},{8,9},{9,8},{10,11... | collective-permute-start | bytes 1277960 | tf_op jit(solution)/shard_map/ppermute | solution.py:30
  179.2 8.2 %collective-permute-start.30 = (bf16[208,1024]{1,0:T(8,128)(2,1)S(1)}, bf16[208,1024]{1,0:T(8,128)(2,1)S(1)}, u32[]{:S(2)}, u32[]{:S(2)}) collective-permute-start(bf16[208,1024]{1,0:T(8,128)(2,1)S(1)} %copy-done.25), channel_id=1, source_target_pairs={{0,1},{1,0},{2,3},{3,2},{4,5},{5,4},{6,7},{7,6},{8,9},{9,8},{10,11... | collective-permute-start | bytes 1277960 | tf_op jit(solution)/shard_map/ppermute | solution.py:30
  187.4 5.2 %collective-permute-start.31 = (bf16[4,512,256]{2,1,0:T(8,128)(2,1)}, bf16[4,512,256]{2,1,0:T(8,128)(2,1)S(1)}, u32[]{:S(2)}, u32[]{:S(2)}) collective-permute-start(bf16[4,512,256]{2,1,0:T(8,128)(2,1)} %get-tuple-element.422), channel_id=1, source_target_pairs={{0,8},{8,0},{16,24},{24,16},{1,9},{9,1},{17,25},{25,17},{2,10},{10... | collective-permute-start | bytes 3145736 | tf_op jit(solution)/shard_map/ppermute | solution.py:30
  187.4 5.5 %collective-permute-start.32 = (bf16[4,512,256]{2,1,0:T(8,128)(2,1)}, bf16[4,512,256]{2,1,0:T(8,128)(2,1)S(1)}, u32[]{:S(2)}, u32[]{:S(2)}) collective-permute-start(bf16[4,512,256]{2,1,0:T(8,128)(2,1)} %get-tuple-element.424), channel_id=1, source_target_pairs={{0,8},{8,0},{16,24},{24,16},{1,9},{9,1},{17,25},{25,17},{2,10},{10... | collective-permute-start | bytes 3145736 | tf_op jit(solution)/shard_map/ppermute | solution.py:30
  194.1 15.1 %collective-permute-start.33 = (bf16[2,512,256]{2,1,0:T(8,128)(2,1)S(1)}, bf16[2,512,256]{2,1,0:T(8,128)(2,1)S(1)}, u32[]{:S(2)}, u32[]{:S(2)}) collective-permute-start(bf16[2,512,256]{2,1,0:T(8,128)(2,1)S(1)} %slice.157), channel_id=1, source_target_pairs={{0,16},{8,24},{16,0},{24,8},{1,17},{9,25},{17,1},{25,9},{2,18},{10... | collective-permute-start | bytes 1572872 | tf_op jit(solution)/shard_map/ppermute | solution.py:30
  197.8 9.1 %collective-permute-start.36 = (f32[8,512]{1,0:T(8,128)S(1)}, f32[8,512]{1,0:T(8,128)S(1)}, u32[]{:S(2)}, u32[]{:S(2)}) collective-permute-start(f32[8,512]{1,0:T(8,128)S(1)} %get-tuple-element.516), channel_id=1, source_target_pairs={{0,24},{8,16},{16,8},{24,0},{1,25},{9,17},{17,9},{25,1},{2,26},{10... | collective-permute-start | bytes 49160 | tf_op jit(solution)/shard_map/ppermute | solution.py:30
  198.0 10.5 %collective-permute-start.35 = (f32[8,512]{1,0:T(8,128)S(1)}, f32[8,512]{1,0:T(8,128)S(1)}, u32[]{:S(2)}, u32[]{:S(2)}) collective-permute-start(f32[8,512]{1,0:T(8,128)S(1)} %get-tuple-element.517), channel_id=1, source_target_pairs={{0,16},{8,24},{16,0},{24,8},{1,17},{9,25},{17,1},{25,9},{2,18},{10... | collective-permute-start | bytes 49160 | tf_op jit(solution)/shard_map/ppermute | solution.py:30
  199.0 9.5 %collective-permute-start.34 = (f32[8,512]{1,0:T(8,128)S(1)}, f32[8,512]{1,0:T(8,128)S(1)}, u32[]{:S(2)}, u32[]{:S(2)}) collective-permute-start(f32[8,512]{1,0:T(8,128)S(1)} %get-tuple-element.515), channel_id=1, source_target_pairs={{0,8},{8,0},{16,24},{24,16},{1,9},{9,1},{17,25},{25,17},{2,10},{10... | collective-permute-start | bytes 49160 | tf_op jit(solution)/shard_map/ppermute | solution.py:30
  209.3 24.2 %collective-permute-start.37 = (bf16[2,512,256]{2,1,0:T(8,128)(2,1)S(1)}, bf16[2,512,256]{2,1,0:T(8,128)(2,1)S(1)}, u32[]{:S(2)}, u32[]{:S(2)}) collective-permute-start(bf16[2,512,256]{2,1,0:T(8,128)(2,1)S(1)} %slice.162), channel_id=1, source_target_pairs={{0,16},{8,24},{16,0},{24,8},{1,17},{9,25},{17,1},{25,9},{2,18},{10... | collective-permute-start | bytes 1572872 | tf_op jit(solution)/shard_map/ppermute | solution.py:30
  210.4 13.9 %collective-permute-start.41 = (bf16[2,208,128]{2,1,0:T(8,128)(2,1)S(1)}, bf16[2,208,128]{2,1,0:T(8,128)(2,1)S(1)}, u32[]{:S(2)}, u32[]{:S(2)}) collective-permute-start(bf16[2,208,128]{2,1,0:T(8,128)(2,1)S(1)} %get-tuple-element.494), channel_id=1, source_target_pairs={{0,6},{2,4},{4,2},{6,0},{1,7},{3,5},{5,3},{7,1},{8,14},{10,12},{12... | collective-permute-start | bytes 319496 | tf_op jit(solution)/shard_map/ppermute | solution.py:30
  220.5 7.2 %collective-permute-start.40 = (bf16[2,208,128]{2,1,0:T(8,128)(2,1)S(1)}, bf16[2,208,128]{2,1,0:T(8,128)(2,1)S(1)}, u32[]{:S(2)}, u32[]{:S(2)}) collective-permute-start(bf16[2,208,128]{2,1,0:T(8,128)(2,1)S(1)} %get-tuple-element.495), channel_id=1, source_target_pairs={{0,4},{2,6},{4,0},{6,2},{1,5},{3,7},{5,1},{7,3},{8,12},{10,14},{12... | collective-permute-start | bytes 319496 | tf_op jit(solution)/shard_map/ppermute | solution.py:30
  220.5 8.3 %collective-permute-start.39 = (bf16[2,208,128]{2,1,0:T(8,128)(2,1)S(1)}, bf16[2,208,128]{2,1,0:T(8,128)(2,1)S(1)}, u32[]{:S(2)}, u32[]{:S(2)}) collective-permute-start(bf16[2,208,128]{2,1,0:T(8,128)(2,1)S(1)} %get-tuple-element.496), channel_id=1, source_target_pairs={{0,2},{2,0},{4,6},{6,4},{1,3},{3,1},{5,7},{7,5},{8,10},{10,8},{12,... | collective-permute-start | bytes 319496 | tf_op jit(solution)/shard_map/ppermute | solution.py:30
  222.0 11.5 %collective-permute-start.38 = (bf16[512,256]{1,0:T(8,128)(2,1)}, bf16[512,256]{1,0:T(8,128)(2,1)S(1)}, u32[]{:S(2)}, u32[]{:S(2)}) collective-permute-start(bf16[512,256]{1,0:T(8,128)(2,1)} %get-tuple-element.487), channel_id=1, source_target_pairs={{0,2},{2,0},{4,6},{6,4},{1,3},{3,1},{5,7},{7,5},{8,10},{10,8},{12,... | collective-permute-start | bytes 786440 | tf_op jit(solution)/shard_map/ppermute | solution.py:30
  234.3 25.6 %collective-permute-start.42 = (bf16[512,256]{1,0:T(8,128)(2,1)S(1)}, bf16[512,256]{1,0:T(8,128)(2,1)S(1)}, u32[]{:S(2)}, u32[]{:S(2)}) collective-permute-start(bf16[512,256]{1,0:T(8,128)(2,1)S(1)} %get-tuple-element.485), channel_id=1, source_target_pairs={{0,2},{2,0},{4,6},{6,4},{1,3},{3,1},{5,7},{7,5},{8,10},{10,8},{12,... | collective-permute-start | bytes 786440 | tf_op jit(solution)/shard_map/ppermute | solution.py:30
  235.9 23.9 %collective-permute-start.43 = (bf16[512,256]{1,0:T(8,128)(2,1)S(1)}, bf16[512,256]{1,0:T(8,128)(2,1)S(1)}, u32[]{:S(2)}, u32[]{:S(2)}) collective-permute-start(bf16[512,256]{1,0:T(8,128)(2,1)S(1)} %add_convert_fusion.2), channel_id=1, source_target_pairs={{0,4},{2,6},{4,0},{6,2},{1,5},{3,7},{5,1},{7,3},{8,12},{10,14},{12... | collective-permute-start | bytes 786440 | tf_op jit(solution)/shard_map/ppermute | solution.py:30
  237.5 21.8 %collective-permute-start.45 = (f32[8,512]{1,0:T(8,128)S(1)}, f32[8,512]{1,0:T(8,128)S(1)}, u32[]{:S(2)}, u32[]{:S(2)}) collective-permute-start(f32[8,512]{1,0:T(8,128)S(1)} %fusion.39), channel_id=1, source_target_pairs={{0,4},{2,6},{4,0},{6,2},{1,5},{3,7},{5,1},{7,3},{8,12},{10,14},{12... | collective-permute-start | bytes 49160 | tf_op jit(solution)/shard_map/ppermute | solution.py:30
  238.9 20.3 %collective-permute-start.46 = (f32[8,512]{1,0:T(8,128)S(1)}, f32[8,512]{1,0:T(8,128)S(1)}, u32[]{:S(2)}, u32[]{:S(2)}) collective-permute-start(f32[8,512]{1,0:T(8,128)S(1)} %fusion.39), channel_id=1, source_target_pairs={{0,6},{2,4},{4,2},{6,0},{1,7},{3,5},{5,3},{7,1},{8,14},{10,12},{12... | collective-permute-start | bytes 49160 | tf_op jit(solution)/shard_map/ppermute | solution.py:30
  239.8 19.4 %collective-permute-start.44 = (f32[8,512]{1,0:T(8,128)S(1)}, f32[8,512]{1,0:T(8,128)S(1)}, u32[]{:S(2)}, u32[]{:S(2)}) collective-permute-start(f32[8,512]{1,0:T(8,128)S(1)} %fusion.39), channel_id=1, source_target_pairs={{0,2},{2,0},{4,6},{6,4},{1,3},{3,1},{5,7},{7,5},{8,10},{10,8},{12,... | collective-permute-start | bytes 49160 | tf_op jit(solution)/shard_map/ppermute | solution.py:30
  (41 other events, 427.4 us)
Sparse Core Ops, SparseCore 0:
  10.8 95.6 all-gather.2
  144.6 123.3 reduce-scatter.1

commit v2 on v1

--- a/solution.py
+++ b/solution.py
@@ -332,16 +332,20 @@
 
 
 def feed_grad_kernel(spec, pos, *refs):
-    parts, rows, width = spec
+    parts, rows, width, groups = spec
     hids, units, normeds, dys, out = refs[0:2], refs[2:4], refs[4:6], refs[6:8], refs[8]
     row = pos[2]
 
     def write(left, right):
-        total = dot_tn(left[0][0], right[0][...]) + dot_tn(left[1][0], right[1][...])
-        block = total.shape[0] // parts
-        for d in range(parts):
-            for k in range(rows):
-                out[d, row ^ k] = total[d * block : (d + 1) * block, k * width : (k + 1) * width].astype(LOW)
+        wide = [jnp.concatenate([ref[g] for g in range(groups)], axis=1) for ref in left]
+        total = dot_tn(jnp.concatenate(wide, axis=0), jnp.concatenate([ref[...] for ref in right], axis=0))
+        block = total.shape[0] // (groups * parts)
+        for g in range(groups):
+            for d in range(parts):
+                at = (g * parts + d) * block
+                for k in range(rows):
+                    value = total[at : at + block, k * width : (k + 1) * width]
+                    out[d, row ^ k, g * block : (g + 1) * block, :] = value.astype(LOW)
 
     half = pl.num_programs(0) // 2
 
@@ -541,7 +545,7 @@
         return values
 
     assert rows == 4 and images == 2 and lax.axis_size("col") == 2
-    feed_all = lax.all_gather(jnp.concatenate([up_own, down_own]), ("dp", "row"), axis=0).reshape(parts, rows, -1, width)
+    feed_all = lax.all_gather(jnp.concatenate([after(up_own, head_own), down_own]), ("dp", "row"), axis=0).reshape(parts, rows, -1, width)
     head_two = near_two(head_own)
     head_x = across(head_own)
     head_plane = planes(head_own)
@@ -668,17 +672,18 @@
     fed, came_two = fence(fed, came_two)
 
     came_two = [*came_two, swap(fed[1][9], "col", 1)]
-    early = pl.BlockSpec((1, PAD, parts * block), lambda u: (jnp.minimum(u, steps - 1), 0, 0))
-    late = pl.BlockSpec((1, PAD, parts * block), lambda u: (jnp.maximum(u - steps, 0), 0, 0))
+    turns = steps // 2
+    early = pl.BlockSpec((2, PAD, parts * block), lambda u: (jnp.minimum(u, turns - 1), 0, 0))
+    late = pl.BlockSpec((2, PAD, parts * block), lambda u: (jnp.maximum(u - turns, 0), 0, 0))
     feed_grad = run_kernel(
-        functools.partial(feed_grad_kernel, (parts, rows, width)),
+        functools.partial(feed_grad_kernel, (parts, rows, width, 2)),
         (token[0], *[f[5] for f in fed], *[f[4] for f in fed], *[f[1] for f in fed], *[f[2] for f in fed]),
         [shaped((parts, rows, 2 * unit_count, width), LOW)],
-        grid=(2 * steps,),
+        grid=(2 * turns,),
         in_specs=[scalars, early, early, late, late, *[whole(low_full)] * 4],
-        out_specs=[pl.BlockSpec((parts, rows, block, width), lambda u: (0, 0, u, 0))],
+        out_specs=[pl.BlockSpec((parts, rows, 2 * block, width), lambda u: (0, 0, u, 0))],
     )[0]
-    feed_grad, fed = fence(feed_grad, fed)
+    feed_grad, fed, came_two = fence(feed_grad, fed, came_two)
     feed_total = lax.psum_scatter(feed_grad.reshape(-1, width), ("dp", "row"), scatter_dimension=0, tiled=True)
 
     def fold(blocks):
@@ -784,6 +789,7 @@
     attn_two, attn_three = sum_high(attn_near, attn_high)
     attn_three = swap(attn_three, "row", 1)
     grad_tokens = from_images(grad_strips)
+    tiny = (tiny + swap(tiny, "row", 1)) + (swap(tiny, "row", 2) + swap(tiny, "row", 3))
     attn_low, attn_two, attn_three, attn_near, grad_tokens, tiny = fence(
         attn_low, attn_two, attn_three, attn_near, grad_tokens, tiny
     )
@@ -791,8 +797,7 @@
     attn_zero, attn_one = sum_low(attn_near, attn_low)
     attn_one = swap(attn_one, "row", 1)
     attn_two = swap(add_low(attn_two, attn_three), "row", 2)
-    tiny = (tiny + swap(tiny, "row", 1)) + (swap(tiny, "row", 2) + swap(tiny, "row", 3))
-    attn_zero, attn_one, attn_two, tiny = fence(attn_zero, attn_one, attn_two, tiny)
+    attn_zero, attn_one, attn_two = fence(attn_zero, attn_one, attn_two)
     feed_done = adam(
         (feed_total, []),
         [up_own, down_own],

time: 280 us -> 277 us (0.989)
  waiting for transfers between devices: 86.7 us -> 90.3 us
  starting transfers between devices: 65.4 us -> 62.6 us
    reduce_scatter x1, waiting for transfers between devices: 0.36 us -> 5.69 us  [on_device(): lax.psum_scatter(feed_grad.reshape(-1, width), ('dp', 'row'), scatter_dim...]
    unnamed x82 -> x78, local copies, waits for them, and re-layouts: 7.21 us -> 5.04 us
  transfers between devices with their start and end apart: 49 -> 49, of which waited for: 22 -> 20; matrix products, arithmetic and copies ran while one was open for 5% -> 4% of each run, Pallas kernels for 27% -> 31%
where the time goes in v2:
time: 277 us; the launch traced here: 276 us
  waiting for transfers between devices  90.3 us (33%)
  Pallas kernels  89 us (32%)
  starting transfers between devices  62.6 us (23%)
  between operations  14.8 us (5%)
  local copies, waits for them, and re-layouts  10.1 us (4%)
  other arithmetic  8.99 us (3%)
    pallas_call x13, Pallas kernels, run_kernel(): pl.pallas_call(body, grid=grid or (1,), in_specs=in_specs, out_specs=out_...  89 us
    ppermute x47, waiting for transfers between devices, swap(): return lax.ppermute(values, name, [(i, i ^ bit) for i in range(count)])  84.6 us
    ppermute x47, starting transfers between devices, swap(): return lax.ppermute(values, name, [(i, i ^ bit) for i in range(count)])  62.5 us
    reduce_scatter x1, waiting for transfers between devices, on_device(): lax.psum_scatter(feed_grad.reshape(-1, width), ('dp', 'row'), scatter_dim...  5.69 us
  transfers between devices with their start and end apart: 49, of which 20 were waited for; matrix products, arithmetic and copies ran while one was open for 4% of the time, Pallas kernels for 31%

profile of v2, /device:TPU:0, one launch (start us, length us, event | category | flops | bytes accessed | tf_op | source)
XLA Modules:
  0.0 275.8 jit_solution(10436971187257944667)
XLA Ops:
  8.3 2.0 pad_maximum_fusion
  10.3 3.1 %collective-permute-start = (bf16[512,256]{1,0:T(8,128)(2,1)S(1)}, bf16[512,256]{1,0:T(8,128)(2,1)S(1)}, u32[]{:S(2)}, u32[]{:S(2)}) collective-permute-start(bf16[512,256]{1,0:T(8,128)(2,1)S(1)} %pad_maximum_fusion.11.refs_0_), channel_id=1, source_target_pairs={{0,2},{2,0},{4,6},{6,4},{1,3},{3,1},{5,7},{7,5},{8,10},{10,8},{12,... | collective-permute-start | bytes 786440 | tf_op jit(solution)/shard_map/ppermute | solution.py:30
  13.4 2.6 collective-permute-start.1
  16.0 1.5 collective-permute-start.2
  17.8 1.6 collective-permute-start.4
  22.3 3.9 %collective-permute-done = bf16[512,256]{1,0:T(8,128)(2,1)S(1)} collective-permute-done((bf16[512,256]{1,0:T(8,128)(2,1)S(1)}, bf16[512,256]{1,0:T(8,128)(2,1)S(1)}, u32[]{:S(2)}, u32[]{:S(2)}) %collective-permute-start) | collective-permute-done | bytes 262176 | tf_op jit(solution)/shard_map/ppermute | solution.py:30
  26.2 1.9 collective-permute-done.1
  28.2 1.5 collective-permute-start.9
  30.2 4.3 %collective-permute-start.5 = (bf16[512,256]{1,0:T(8,128)(2,1)S(1)}, bf16[512,256]{1,0:T(8,128)(2,1)S(1)}, u32[]{:S(2)}, u32[]{:S(2)}) collective-permute-start(bf16[512,256]{1,0:T(8,128)(2,1)S(1)} %collective-permute-done.1), channel_id=1, source_target_pairs={{0,2},{2,0},{4,6},{6,4},{1,3},{3,1},{5,7},{7,5},{8,10},{10,8},{12,... | collective-permute-start | bytes 786440 | tf_op jit(solution)/shard_map/ppermute | solution.py:30
  35.0 4.0 %collective-permute-start.7 = (bf16[2,216,128]{2,1,0:T(8,128)(2,1)}, bf16[2,216,128]{2,1,0:T(8,128)(2,1)S(1)}, u32[]{:S(2)}, u32[]{:S(2)}) collective-permute-start(bf16[2,216,128]{2,1,0:T(8,128)(2,1)} %get-tuple-element.260), channel_id=1, source_target_pairs={{0,4},{2,6},{4,0},{6,2},{1,5},{3,7},{5,1},{7,3},{8,12},{10,14},{12... | collective-permute-start | bytes 331784 | tf_op jit(solution)/shard_map/ppermute | solution.py:30
  39.0 1.4 collective-permute-start.8
  40.4 14.3 %collective-permute-done.6 = bf16[2,216,128]{2,1,0:T(8,128)(2,1)S(1)} collective-permute-done((bf16[2,216,128]{2,1,0:T(8,128)(2,1)}, bf16[2,216,128]{2,1,0:T(8,128)(2,1)S(1)}, u32[]{:S(2)}, u32[]{:S(2)}) %collective-permute-start.6) | collective-permute-done | bytes 110624 | tf_op jit(solution)/shard_map/ppermute | solution.py:30
  54.7 4.6 %collective-permute-start.16 = (bf16[2,208,128]{2,1,0:T(8,128)(2,1)S(1)}, bf16[2,208,128]{2,1,0:T(8,128)(2,1)S(1)}, u32[]{:S(2)}, u32[]{:S(2)}) collective-permute-start(bf16[2,208,128]{2,1,0:T(8,128)(2,1)S(1)} %get-tuple-element.509), channel_id=1, source_target_pairs={{0,4},{2,6},{4,0},{6,2},{1,5},{3,7},{5,1},{7,3},{8,12},{10,14},{12... | collective-permute-start | bytes 319496 | tf_op jit(solution)/shard_map/ppermute | solution.py:30
  60.6 1.5 collective-permute-start.14
  62.2 7.8 %collective-permute-done.16 = bf16[2,208,128]{2,1,0:T(8,128)(2,1)S(1)} collective-permute-done((bf16[2,208,128]{2,1,0:T(8,128)(2,1)S(1)}, bf16[2,208,128]{2,1,0:T(8,128)(2,1)S(1)}, u32[]{:S(2)}, u32[]{:S(2)}) %collective-permute-start.16) | collective-permute-done | bytes 106528 | tf_op jit(solution)/shard_map/ppermute | solution.py:30
  71.1 1.5 collective-permute-done.11.refs_3_
  72.6 11.9 %collective-permute-done.10.refs_10_ = bf16[640,256]{1,0:T(8,128)(2,1)S(1)} collective-permute-done((bf16[640,256]{1,0:T(8,128)(2,1)S(1)}, bf16[640,256]{1,0:T(8,128)(2,1)S(1)}, u32[]{:S(2)}, u32[]{:S(2)}) %collective-permute-start.10) | collective-permute-done | bytes 327712 | tf_op jit(solution)/shard_map/ppermute | solution.py:30
  84.6 1.3 collective-permute-start.20
  89.0 6.2 %shard_map.335 = (f32[8,1024]{1,0:T(8,128)}, bf16[208,1024]{1,0:T(8,128)(2,1)}, bf16[208,1024]{1,0:T(8,128)(2,1)}, bf16[208,1536]{1,0:T(8,128)(2,1)}, bf16[208,5...) custom-call(s32[3]{0:T(128)} %pad_add_fusion.pos, bf16[4,2,208,128]{3,2,1,0:T(8,128)(2,1)} %copy-done.12, ...), custom_call_target="tpu_custom_call" | custom-call | flops 1024 | bytes 1024 | tf_op jit(solution)/shard_map/pallas_call | solution.py:478
  98.2 6.4 %shard_map.336 = (f32[8,1024]{1,0:T(8,128)}, bf16[208,1024]{1,0:T(8,128)(2,1)}, bf16[208,1024]{1,0:T(8,128)(2,1)}, bf16[208,1536]{1,0:T(8,128)(2,1)}, bf16[208,5...) custom-call(s32[3]{0:T(128)} %pad_add_fusion.pos, bf16[4,2,208,128]{3,2,1,0:T(8,128)(2,1)} %copy-done.12, ...), custom_call_target="tpu_custom_call" | custom-call | flops 1024 | bytes 1024 | tf_op jit(solution)/shard_map/pallas_call | solution.py:478
  104.5 3.5 %collective-permute-done.21.came = bf16[208,1024]{1,0:T(8,128)(2,1)S(1)} collective-permute-done((bf16[208,1024]{1,0:T(8,128)(2,1)}, bf16[208,1024]{1,0:T(8,128)(2,1)S(1)}, u32[]{:S(2)}, u32[]{:S(2)}) %collective-permute-start.21) | collective-permute-done | bytes 426016 | tf_op jit(solution)/shard_map/ppermute | solution.py:30
  108.8 10.8 %shard_map.337 = (f32[208,1024]{1,0:T(8,128)}, bf16[208,1024]{1,0:T(8,128)(2,1)}, bf16[208,1024]{1,0:T(8,128)(2,1)}, f32[1,1024]{1,0:T(1,128)}, bf16[4,208,512]{...) custom-call(s32[3]{0:T(128)} %pad_add_fusion.pos, ...), custom_call_target="tpu_custom_call" | custom-call | flops 1024 | bytes 1024 | tf_op jit(solution)/shard_map/pallas_call | solution.py:478
  119.7 1.3 collective-permute-start.23
  121.0 10.7 %shard_map.338 = (f32[208,1024]{1,0:T(8,128)}, bf16[208,1024]{1,0:T(8,128)(2,1)}, bf16[208,1024]{1,0:T(8,128)(2,1)}, f32[1,1024]{1,0:T(1,128)}, bf16[4,208,512]{...) custom-call(s32[3]{0:T(128)} %pad_add_fusion.pos, ...), custom_call_target="tpu_custom_call" | custom-call | flops 1024 | bytes 1024 | tf_op jit(solution)/shard_map/pallas_call | solution.py:478
  132.6 9.2 %shard_map.339 = bf16[4,4,1024,256]{3,2,1,0:T(8,128)(2,1)} custom-call(s32[3]{0:T(128)} %pad_add_fusion.pos, bf16[4,208,512]{2,1,0:T(8,128)(2,1)} %get-tuple-element.353.refs_0_, bf16[4,208,512]{2,1,0:T(8,128)(2,1)} %get-tuple-element.354.refs_1_, bf16[4,208,512]{2,1,0:T(8,128)(2,1)} %get-tuple-element.355.refs_2_, ...), custom_call_target="tpu_custom_call" | custom-call | flops 1024 | bytes 1024 | tf_op jit(solution)/shard_map/pallas_call | solution.py:478
  144.9 10.1 %shard_map.340 = (f32[208,1024]{1,0:T(8,128)}, bf16[208,1024]{1,0:T(8,128)(2,1)}, bf16[208,1536]{1,0:T(8,128)(2,1)}, bf16[208,1024]{1,0:T(8,128)(2,1)}, f32[8,1024]{1,0:T(8,128)}, /*index=5*/f32[1,1536]{1,0:T(1,128)}) custom-call(s32[3]{0:T(128)} %pad_add_fusion.pos, f32[8,1024]{1,0:T(8,128)} %get-tuple-element.299.vec, f32[208,1024]{1,0:T(8,128)} %get-tuple-element.375.mid, ...), custom_call_target="tpu_custom_call" | custom-call | flops 1024 | bytes 1024 | tf_op jit(solution)/shard_map/pallas_call | solution.py:478
  155.2 5.8 %collective-permute-start.29 = (bf16[2,208,128]{2,1,0:T(8,128)(2,1)S(1)}, bf16[2,208,128]{2,1,0:T(8,128)(2,1)S(1)}, u32[]{:S(2)}, u32[]{:S(2)}) collective-permute-start(bf16[2,208,128]{2,1,0:T(8,128)(2,1)S(1)} %get-tuple-element.503), channel_id=1, source_target_pairs={{0,6},{2,4},{4,2},{6,0},{1,7},{3,5},{5,3},{7,1},{8,14},{10,12},{12... | collective-permute-start | bytes 319496 | tf_op jit(solution)/shard_map/ppermute | solution.py:30
  162.6 10.8 %shard_map.341 = (f32[208,1024]{1,0:T(8,128)}, bf16[208,1024]{1,0:T(8,128)(2,1)}, bf16[208,1536]{1,0:T(8,128)(2,1)}, bf16[208,1024]{1,0:T(8,128)(2,1)}, f32[8,1024]{1,0:T(8,128)}, /*index=5*/f32[1,1536]{1,0:T(1,128)}) custom-call(s32[3]{0:T(128)} %pad_add_fusion.pos, f32[8,1024]{1,0:T(8,128)} %get-tuple-element.299.vec, f32[208,1024]{1,0:T(8,128)} %get-tuple-element.395.mid, ...), custom_call_target="tpu_custom_call" | custom-call | flops 1024 | bytes 1024 | tf_op jit(solution)/shard_map/pallas_call | solution.py:478
  175.7 7.1 %shard_map.342 = (bf16[4,512,256]{2,1,0:T(8,128)(2,1)}, bf16[4,512,256]{2,1,0:T(8,128)(2,1)}, bf16[4,512,256]{2,1,0:T(8,128)(2,1)}, bf16[4,512,256]{2,1,0:T(8,128)(2,1)}) custom-call(s32[3]{0:T(128)} %pad_add_fusion.pos, bf16[208,1536]{1,0:T(8,128)(2,1)} %get-tuple-element.411.refs_0_, bf16[208,1536]{1,0:T(8,128)(2,1)} %get-tuple-element.412.refs_1_, ...), custom_call_target="tpu_custom_call" | custom-call | flops 1024 | bytes 1024 | tf_op jit(solution)/shard_map/pallas_call | solution.py:478
  184.0 4.5 %shard_map.343 = (bf16[4,2,208,128]{3,2,1,0:T(8,128)(2,1)}, f32[8,1024]{1,0:T(8,128)}) custom-call(s32[3]{0:T(128)} %pad_add_fusion.pos, f32[8,1024]{1,0:T(8,128)} %get-tuple-element.299.vec, bf16[208,1024]{1,0:T(8,128)(2,1)} %get-tuple-element.312.x.refs_0_, bf16[208,1024]{1,0:T(8,128)(2,1)} %get-tuple-element.340.x.refs_1_, ...), custom_call_target="tpu_custom_call" | custom-call | flops 1024 | bytes 1024 | tf_op jit(solution)/shard_map/pallas_call | solution.py:478
  190.0 1.6 collective-permute-start.33
  191.6 1.9 shard_map.344
  196.2 7.1 %collective-permute-done.36 = f32[8,512]{1,0:T(8,128)S(1)} collective-permute-done((f32[8,512]{1,0:T(8,128)S(1)}, f32[8,512]{1,0:T(8,128)S(1)}, u32[]{:S(2)}, u32[]{:S(2)}) %collective-permute-start.36) | collective-permute-done | bytes 16416 | tf_op jit(solution)/shard_map/ppermute | solution.py:30
  205.2 2.3 collective-permute-start.43
  207.5 1.5 collective-permute-start.44
  209.3 1.5 collective-permute-start.37
  211.6 1.8 collective-permute-start.38
  213.5 2.4 collective-permute-start.41
  215.9 2.1 collective-permute-start.39
  218.6 6.9 %collective-permute-done.41 = bf16[2,208,128]{2,1,0:T(8,128)(2,1)S(1)} collective-permute-done((bf16[2,208,128]{2,1,0:T(8,128)(2,1)S(1)}, bf16[2,208,128]{2,1,0:T(8,128)(2,1)S(1)}, u32[]{:S(2)}, u32[]{:S(2)}) %collective-permute-start.41) | collective-permute-done | bytes 106528 | tf_op jit(solution)/shard_map/ppermute | solution.py:30
  225.5 1.7 collective-permute-done.39
  228.3 2.8 collective-permute-done.37
  232.0 3.6 %collective-permute-start.46 = (bf16[512,256]{1,0:T(8,128)(2,1)S(1)}, bf16[512,256]{1,0:T(8,128)(2,1)S(1)}, u32[]{:S(2)}, u32[]{:S(2)}) collective-permute-start(bf16[512,256]{1,0:T(8,128)(2,1)S(1)} %add_convert_fusion.2), channel_id=1, source_target_pairs={{0,4},{2,6},{4,0},{6,2},{1,5},{3,7},{5,1},{7,3},{8,12},{10,14},{12... | collective-permute-start | bytes 786440 | tf_op jit(solution)/shard_map/ppermute | solution.py:30
  235.6 15.6 %collective-permute-done.45.refs_0_ = bf16[512,256]{1,0:T(8,128)(2,1)S(1)} collective-permute-done((bf16[512,256]{1,0:T(8,128)(2,1)S(1)}, bf16[512,256]{1,0:T(8,128)(2,1)S(1)}, u32[]{:S(2)}, u32[]{:S(2)}) %collective-permute-start.45) | collective-permute-done | bytes 262176 | tf_op jit(solution)/shard_map/ppermute | solution.py:30
  252.0 3.2 %shard_map.345 = (f32[384,256]{1,0:T(8,128)}, f32[384,256]{1,0:T(8,128)}, f32[2,384,256]{2,1,0:T(8,128)}, f32[128,256]{1,0:T(8,128)}, f32[128,256]{1,0:T(8,128)}, /*index=5*/f32[2,128,256]{2,1,0:T(8,128)}) custom-call(bf16[512,256]{1,0:T(8,128)(2,1)} %get-tuple-element.462.first, bf16[512,256]{1,0:T(8,128)(2,1)} %copy-done.31, bf16[512,256]{1,0:T(8,128)(2,1)} %copy-done.32, ...), custom_call_target="tpu_custom_call" | custom-call | flops 1024 | bytes 1024 | tf_op jit(solution)/shard_map/pallas_call | solution.py:478
  255.3 3.7 %shard_map.346 = (f32[2,8,16]{2,1,0:T(8,128)}, f32[16,32]{1,0:T(8,128)}, f32[6,2,16]{2,1,0:T(2,128)}, f32[2,8,16]{2,1,0:T(8,128)}, f32[16,32]{1,0:T(8,128)}, /*i...) custom-call(s32[3]{0:T(128)} %pad_add_fusion.pos, ...), custom_call_target="tpu_custom_call" | custom-call | flops 1024 | bytes 1024 | tf_op jit(solution)/shard_map/pallas_call | solution.py:478
  259.0 5.7 %reduce-scatter.2.cloned.1.call-done.first = bf16[1024,256]{1,0:T(8,128)(2,1)} async-done(((bf16[16384,256]{1,0:T(8,128)(2,1)}), bf16[1024,256]{1,0:T(8,128)(2,1)}) %reduce-scatter.2.cloned.1.call-update) | async-done | bytes 524304 | tf_op jit(solution)/shard_map/reduce_scatter | solution.py:687
  264.7 4.3 %shard_map.347 = (f32[512,256]{1,0:T(8,128)}, f32[512,256]{1,0:T(8,128)}, f32[2,512,256]{2,1,0:T(8,128)}, f32[512,256]{1,0:T(8,128)}, f32[512,256]{1,0:T(8,128)}, /*index=5*/f32[2,512,256]{2,1,0:T(8,128)}) custom-call(bf16[1024,256]{1,0:T(8,128)(2,1)} %reduce-scatter.2.cloned.1.call-done.first, bf16[512,256]{1,0:T(8,128)(2,1)} %bitcast.185, ...), custom_call_target="tpu_custom_call" | custom-call | flops 1024 | bytes 1024 | tf_op jit(solution)/shard_map/pallas_call | solution.py:478
  (209 shorter events, 34.0 us)
Async XLA Ops:
  7.2 101.6 %all-gather.3.cloned.1.call-start = ((), (), s32[]{:S(2)}) async-start(), calls=%async_computation.2 | async-start | bytes 8912896 | tf_op jit(solution)/shard_map/all_gather | solution.py:548
  10.3 254.4 %reduce-scatter.2.cloned.1.call-start = ((), (), s32[]{:S(2)}) async-start(), calls=%async_computation.1 | async-start | bytes 8912896 | tf_op jit(solution)/shard_map/reduce_scatter | solution.py:687
  10.3 15.8 %collective-permute-start = (bf16[512,256]{1,0:T(8,128)(2,1)S(1)}, bf16[512,256]{1,0:T(8,128)(2,1)S(1)}, u32[]{:S(2)}, u32[]{:S(2)}) collective-permute-start(bf16[512,256]{1,0:T(8,128)(2,1)S(1)} %pad_maximum_fusion.11.refs_0_), channel_id=1, source_target_pairs={{0,2},{2,0},{4,6},{6,4},{1,3},{3,1},{5,7},{7,5},{8,10},{10,8},{12,... | collective-permute-start | bytes 786440 | tf_op jit(solution)/shard_map/ppermute | solution.py:30
  13.4 14.6 %collective-permute-start.1 = (bf16[512,256]{1,0:T(8,128)(2,1)S(1)}, bf16[512,256]{1,0:T(8,128)(2,1)S(1)}, u32[]{:S(2)}, u32[]{:S(2)}) collective-permute-start(bf16[512,256]{1,0:T(8,128)(2,1)S(1)} %pad_maximum_fusion.11.refs_0_), channel_id=1, source_target_pairs={{0,4},{2,6},{4,0},{6,2},{1,5},{3,7},{5,1},{7,3},{8,12},{10,14},{12... | collective-permute-start | bytes 786440 | tf_op jit(solution)/shard_map/ppermute | solution.py:30
  16.0 12.1 %collective-permute-start.2 = (bf16[512,256]{1,0:T(8,128)(2,1)S(1)}, bf16[512,256]{1,0:T(8,128)(2,1)S(1)}, u32[]{:S(2)}, u32[]{:S(2)}) collective-permute-start(bf16[512,256]{1,0:T(8,128)(2,1)S(1)} %pad_maximum_fusion.11.refs_0_), channel_id=1, source_target_pairs={{0,16},{8,24},{16,0},{24,8},{1,17},{9,25},{17,1},{25,9},{2,18},{10... | collective-permute-start | bytes 786440 | tf_op jit(solution)/shard_map/ppermute | solution.py:30
  17.5 10.6 %collective-permute-start.3 = (bf16[512,256]{1,0:T(8,128)(2,1)S(1)}, bf16[512,256]{1,0:T(8,128)(2,1)S(1)}, u32[]{:S(2)}, u32[]{:S(2)}) collective-permute-start(bf16[512,256]{1,0:T(8,128)(2,1)S(1)} %pad_maximum_fusion.11.refs_0_), channel_id=1, source_target_pairs={{0,8},{8,0},{16,24},{24,16},{1,9},{9,1},{17,25},{25,17},{2,10},{10... | collective-permute-start | bytes 786440 | tf_op jit(solution)/shard_map/ppermute | solution.py:30
  17.8 3.7 %collective-permute-start.4 = (bf16[6,128]{1,0:T(8,128)(2,1)S(1)}, bf16[6,128]{1,0:T(8,128)(2,1)S(1)}, u32[]{:S(2)}, u32[]{:S(2)}) collective-permute-start(bf16[6,128]{1,0:T(8,128)(2,1)S(1)} %broadcast_select_fusion.2), channel_id=1, source_target_pairs={{0,1},{1,0},{2,3},{3,2},{4,5},{5,4},{6,7},{7,6},{8,9},{9,8},{10,11... | collective-permute-start | bytes 4616 | tf_op jit(solution)/shard_map/ppermute | solution.py:30
  28.2 31.1 %collective-permute-start.9 = (bf16[1024,256]{1,0:T(8,128)(2,1)S(1)}, bf16[1024,256]{1,0:T(8,128)(2,1)S(1)}, u32[]{:S(2)}, u32[]{:S(2)}) collective-permute-start(bf16[1024,256]{1,0:T(8,128)(2,1)S(1)} %constant_dynamic-update-slice_fusion.refs_4_), channel_id=1, source_target_pairs={{0,16},{8,24},{16,0},{24,8},{1,17},{9,25},{17,1},{25,9},{2,18},{10... | collective-permute-start | bytes 1572872 | tf_op jit(solution)/shard_map/ppermute | solution.py:30
  30.2 29.1 %collective-permute-start.5 = (bf16[512,256]{1,0:T(8,128)(2,1)S(1)}, bf16[512,256]{1,0:T(8,128)(2,1)S(1)}, u32[]{:S(2)}, u32[]{:S(2)}) collective-permute-start(bf16[512,256]{1,0:T(8,128)(2,1)S(1)} %collective-permute-done.1), channel_id=1, source_target_pairs={{0,2},{2,0},{4,6},{6,4},{1,3},{3,1},{5,7},{7,5},{8,10},{10,8},{12,... | collective-permute-start | bytes 786440 | tf_op jit(solution)/shard_map/ppermute | solution.py:30
  34.9 19.7 %collective-permute-start.6 = (bf16[2,216,128]{2,1,0:T(8,128)(2,1)}, bf16[2,216,128]{2,1,0:T(8,128)(2,1)S(1)}, u32[]{:S(2)}, u32[]{:S(2)}) collective-permute-start(bf16[2,216,128]{2,1,0:T(8,128)(2,1)} %get-tuple-element.259), channel_id=1, source_target_pairs={{0,2},{2,0},{4,6},{6,4},{1,3},{3,1},{5,7},{7,5},{8,10},{10,8},{12,... | collective-permute-start | bytes 331784 | tf_op jit(solution)/shard_map/ppermute | solution.py:30
  35.0 19.7 %collective-permute-start.7 = (bf16[2,216,128]{2,1,0:T(8,128)(2,1)}, bf16[2,216,128]{2,1,0:T(8,128)(2,1)S(1)}, u32[]{:S(2)}, u32[]{:S(2)}) collective-permute-start(bf16[2,216,128]{2,1,0:T(8,128)(2,1)} %get-tuple-element.260), channel_id=1, source_target_pairs={{0,4},{2,6},{4,0},{6,2},{1,5},{3,7},{5,1},{7,3},{8,12},{10,14},{12... | collective-permute-start | bytes 331784 | tf_op jit(solution)/shard_map/ppermute | solution.py:30
  39.0 20.3 %collective-permute-start.8 = (bf16[2,216,128]{2,1,0:T(8,128)(2,1)S(1)}, bf16[2,216,128]{2,1,0:T(8,128)(2,1)S(1)}, u32[]{:S(2)}, u32[]{:S(2)}) collective-permute-start(bf16[2,216,128]{2,1,0:T(8,128)(2,1)S(1)} %get-tuple-element.261), channel_id=1, source_target_pairs={{0,6},{2,4},{4,2},{6,0},{1,7},{3,5},{5,3},{7,1},{8,14},{10,12},{12... | collective-permute-start | bytes 331784 | tf_op jit(solution)/shard_map/ppermute | solution.py:30
  54.6 6.0 %collective-permute-start.15 = (bf16[2,208,128]{2,1,0:T(8,128)(2,1)S(1)}, bf16[2,208,128]{2,1,0:T(8,128)(2,1)S(1)}, u32[]{:S(2)}, u32[]{:S(2)}) collective-permute-start(bf16[2,208,128]{2,1,0:T(8,128)(2,1)S(1)} %get-tuple-element.508), channel_id=1, source_target_pairs={{0,2},{2,0},{4,6},{6,4},{1,3},{3,1},{5,7},{7,5},{8,10},{10,8},{12,... | collective-permute-start | bytes 319496 | tf_op jit(solution)/shard_map/ppermute | solution.py:30
  54.7 15.3 %collective-permute-start.16 = (bf16[2,208,128]{2,1,0:T(8,128)(2,1)S(1)}, bf16[2,208,128]{2,1,0:T(8,128)(2,1)S(1)}, u32[]{:S(2)}, u32[]{:S(2)}) collective-permute-start(bf16[2,208,128]{2,1,0:T(8,128)(2,1)S(1)} %get-tuple-element.509), channel_id=1, source_target_pairs={{0,4},{2,6},{4,0},{6,2},{1,5},{3,7},{5,1},{7,3},{8,12},{10,14},{12... | collective-permute-start | bytes 319496 | tf_op jit(solution)/shard_map/ppermute | solution.py:30
  59.3 11.8 %collective-permute-start.17 = (bf16[2,208,128]{2,1,0:T(8,128)(2,1)S(1)}, bf16[2,208,128]{2,1,0:T(8,128)(2,1)S(1)}, u32[]{:S(2)}, u32[]{:S(2)}) collective-permute-start(bf16[2,208,128]{2,1,0:T(8,128)(2,1)S(1)} %get-tuple-element.507), channel_id=1, source_target_pairs={{0,6},{2,4},{4,2},{6,0},{1,7},{3,5},{5,3},{7,1},{8,14},{10,12},{12... | collective-permute-start | bytes 319496 | tf_op jit(solution)/shard_map/ppermute | solution.py:30
  59.3 25.2 %collective-permute-start.12 = (bf16[1024,256]{1,0:T(8,128)(2,1)S(1)}, bf16[1024,256]{1,0:T(8,128)(2,1)S(1)}, u32[]{:S(2)}, u32[]{:S(2)}) collective-permute-start(bf16[1024,256]{1,0:T(8,128)(2,1)S(1)} %constant_dynamic-update-slice_fusion.refs_4_), channel_id=1, source_target_pairs={{0,8},{8,0},{16,24},{24,16},{1,9},{9,1},{17,25},{25,17},{2,10},{10... | collective-permute-start | bytes 1572872 | tf_op jit(solution)/shard_map/ppermute | solution.py:30
  59.4 25.1 %collective-permute-start.13 = (bf16[1024,256]{1,0:T(8,128)(2,1)S(1)}, bf16[1024,256]{1,0:T(8,128)(2,1)S(1)}, u32[]{:S(2)}, u32[]{:S(2)}) collective-permute-start(bf16[1024,256]{1,0:T(8,128)(2,1)S(1)} %collective-permute-done.9.refs_6_), channel_id=1, source_target_pairs={{0,8},{8,0},{16,24},{24,16},{1,9},{9,1},{17,25},{25,17},{2,10},{10... | collective-permute-start | bytes 1572872 | tf_op jit(solution)/shard_map/ppermute | solution.py:30
  60.6 23.9 %collective-permute-start.14 = (bf16[4,2,208,128]{3,2,1,0:T(8,128)(2,1)S(1)}, bf16[4,2,208,128]{3,2,1,0:T(8,128)(2,1)S(1)}, u32[]{:S(2)}, u32[]{:S(2)}) collective-permute-start(bf16[4,2,208,128]{3,2,1,0:T(8,128)(2,1)S(1)} %pad_maximum_fusion.1.near), channel_id=1, source_target_pairs={{0,1},{1,0},{2,3},{3,2},{4,5},{5,4},{6,7},{7,6},{8,9},{9,8},{10,11... | collective-permute-start | bytes 1277960 | tf_op jit(solution)/shard_map/ppermute | solution.py:30
  69.9 14.5 %collective-permute-start.10 = (bf16[640,256]{1,0:T(8,128)(2,1)S(1)}, bf16[640,256]{1,0:T(8,128)(2,1)S(1)}, u32[]{:S(2)}, u32[]{:S(2)}) collective-permute-start(bf16[640,256]{1,0:T(8,128)(2,1)S(1)} %pad_maximum_fusion.10.refs_8_), channel_id=1, source_target_pairs={{0,16},{8,24},{16,0},{24,8},{1,17},{9,25},{17,1},{25,9},{2,18},{10... | collective-permute-start | bytes 983048 | tf_op jit(solution)/shard_map/ppermute | solution.py:30
  84.6 10.6 %collective-permute-start.20 = (bf16[4,2,208,128]{3,2,1,0:T(8,128)(2,1)S(1)}, bf16[4,2,208,128]{3,2,1,0:T(8,128)(2,1)S(1)}, u32[]{:S(2)}, u32[]{:S(2)}) collective-permute-start(bf16[4,2,208,128]{3,2,1,0:T(8,128)(2,1)S(1)} %pad_maximum_fusion.2.near), channel_id=1, source_target_pairs={{0,1},{1,0},{2,3},{3,2},{4,5},{5,4},{6,7},{7,6},{8,9},{9,8},{10,11... | collective-permute-start | bytes 1277960 | tf_op jit(solution)/shard_map/ppermute | solution.py:30
  85.9 1.6 collective-permute-start.18
  85.9 2.1 collective-permute-start.19
  96.0 12.1 %collective-permute-start.21 = (bf16[208,1024]{1,0:T(8,128)(2,1)}, bf16[208,1024]{1,0:T(8,128)(2,1)S(1)}, u32[]{:S(2)}, u32[]{:S(2)}) collective-permute-start(bf16[208,1024]{1,0:T(8,128)(2,1)} %get-tuple-element.313.part), channel_id=1, source_target_pairs={{0,1},{1,0},{2,3},{3,2},{4,5},{5,4},{6,7},{7,6},{8,9},{9,8},{10,11... | collective-permute-start | bytes 1277960 | tf_op jit(solution)/shard_map/ppermute | solution.py:30
  108.1 11.6 %collective-permute-start.22 = (bf16[208,1024]{1,0:T(8,128)(2,1)}, bf16[208,1024]{1,0:T(8,128)(2,1)S(1)}, u32[]{:S(2)}, u32[]{:S(2)}) collective-permute-start(bf16[208,1024]{1,0:T(8,128)(2,1)} %get-tuple-element.328.part), channel_id=1, source_target_pairs={{0,1},{1,0},{2,3},{3,2},{4,5},{5,4},{6,7},{7,6},{8,9},{9,8},{10,11... | collective-permute-start | bytes 1277960 | tf_op jit(solution)/shard_map/ppermute | solution.py:30
  119.7 12.0 %collective-permute-start.23 = (bf16[208,1024]{1,0:T(8,128)(2,1)}, bf16[208,1024]{1,0:T(8,128)(2,1)S(1)}, u32[]{:S(2)}, u32[]{:S(2)}) collective-permute-start(bf16[208,1024]{1,0:T(8,128)(2,1)} %get-tuple-element.376.back), channel_id=1, source_target_pairs={{0,1},{1,0},{2,3},{3,2},{4,5},{5,4},{6,7},{7,6},{8,9},{9,8},{10,11... | collective-permute-start | bytes 1277960 | tf_op jit(solution)/shard_map/ppermute | solution.py:30
  131.7 10.7 %collective-permute-start.24 = (bf16[208,1024]{1,0:T(8,128)(2,1)}, bf16[208,1024]{1,0:T(8,128)(2,1)S(1)}, u32[]{:S(2)}, u32[]{:S(2)}) collective-permute-start(bf16[208,1024]{1,0:T(8,128)(2,1)} %get-tuple-element.396.back), channel_id=1, source_target_pairs={{0,1},{1,0},{2,3},{3,2},{4,5},{5,4},{6,7},{7,6},{8,9},{9,8},{10,11... | collective-permute-start | bytes 1277960 | tf_op jit(solution)/shard_map/ppermute | solution.py:30
  143.7 11.3 %collective-permute-start.25 = (bf16[2,4,208,128]{3,2,1,0:T(8,128)(2,1)S(1)}, bf16[2,4,208,128]{3,2,1,0:T(8,128)(2,1)S(1)}, u32[]{:S(2)}, u32[]{:S(2)}) collective-permute-start(bf16[2,4,208,128]{3,2,1,0:T(8,128)(2,1)S(1)} %pad_maximum_fusion.3), channel_id=1, source_target_pairs={{0,1},{1,0},{2,3},{3,2},{4,5},{5,4},{6,7},{7,6},{8,9},{9,8},{10,11... | collective-permute-start | bytes 1277960 | tf_op jit(solution)/shard_map/ppermute | solution.py:30
  155.2 18.2 %collective-permute-start.29 = (bf16[2,208,128]{2,1,0:T(8,128)(2,1)S(1)}, bf16[2,208,128]{2,1,0:T(8,128)(2,1)S(1)}, u32[]{:S(2)}, u32[]{:S(2)}) collective-permute-start(bf16[2,208,128]{2,1,0:T(8,128)(2,1)S(1)} %get-tuple-element.503), channel_id=1, source_target_pairs={{0,6},{2,4},{4,2},{6,0},{1,7},{3,5},{5,3},{7,1},{8,14},{10,12},{12... | collective-permute-start | bytes 319496 | tf_op jit(solution)/shard_map/ppermute | solution.py:30
  161.0 12.4 %collective-permute-start.28 = (bf16[2,208,128]{2,1,0:T(8,128)(2,1)S(1)}, bf16[2,208,128]{2,1,0:T(8,128)(2,1)S(1)}, u32[]{:S(2)}, u32[]{:S(2)}) collective-permute-start(bf16[2,208,128]{2,1,0:T(8,128)(2,1)S(1)} %get-tuple-element.504), channel_id=1, source_target_pairs={{0,4},{2,6},{4,0},{6,2},{1,5},{3,7},{5,1},{7,3},{8,12},{10,14},{12... | collective-permute-start | bytes 319496 | tf_op jit(solution)/shard_map/ppermute | solution.py:30
  161.0 12.5 %collective-permute-start.27 = (bf16[2,208,128]{2,1,0:T(8,128)(2,1)S(1)}, bf16[2,208,128]{2,1,0:T(8,128)(2,1)S(1)}, u32[]{:S(2)}, u32[]{:S(2)}) collective-permute-start(bf16[2,208,128]{2,1,0:T(8,128)(2,1)S(1)} %get-tuple-element.502), channel_id=1, source_target_pairs={{0,2},{2,0},{4,6},{6,4},{1,3},{3,1},{5,7},{7,5},{8,10},{10,8},{12,... | collective-permute-start | bytes 319496 | tf_op jit(solution)/shard_map/ppermute | solution.py:30
  161.6 13.0 %collective-permute-start.26 = (bf16[208,1024]{1,0:T(8,128)(2,1)S(1)}, bf16[208,1024]{1,0:T(8,128)(2,1)S(1)}, u32[]{:S(2)}, u32[]{:S(2)}) collective-permute-start(bf16[208,1024]{1,0:T(8,128)(2,1)S(1)} %copy-done.22), channel_id=1, source_target_pairs={{0,1},{1,0},{2,3},{3,2},{4,5},{5,4},{6,7},{7,6},{8,9},{9,8},{10,11... | collective-permute-start | bytes 1277960 | tf_op jit(solution)/shard_map/ppermute | solution.py:30
  174.6 8.7 %collective-permute-start.30 = (bf16[208,1024]{1,0:T(8,128)(2,1)S(1)}, bf16[208,1024]{1,0:T(8,128)(2,1)S(1)}, u32[]{:S(2)}, u32[]{:S(2)}) collective-permute-start(bf16[208,1024]{1,0:T(8,128)(2,1)S(1)} %copy-done.24), channel_id=1, source_target_pairs={{0,1},{1,0},{2,3},{3,2},{4,5},{5,4},{6,7},{7,6},{8,9},{9,8},{10,11... | collective-permute-start | bytes 1277960 | tf_op jit(solution)/shard_map/ppermute | solution.py:30
  183.3 5.2 %collective-permute-start.31 = (bf16[4,512,256]{2,1,0:T(8,128)(2,1)}, bf16[4,512,256]{2,1,0:T(8,128)(2,1)S(1)}, u32[]{:S(2)}, u32[]{:S(2)}) collective-permute-start(bf16[4,512,256]{2,1,0:T(8,128)(2,1)} %get-tuple-element.427), channel_id=1, source_target_pairs={{0,8},{8,0},{16,24},{24,16},{1,9},{9,1},{17,25},{25,17},{2,10},{10... | collective-permute-start | bytes 3145736 | tf_op jit(solution)/shard_map/ppermute | solution.py:30
  183.3 5.5 %collective-permute-start.32 = (bf16[4,512,256]{2,1,0:T(8,128)(2,1)}, bf16[4,512,256]{2,1,0:T(8,128)(2,1)S(1)}, u32[]{:S(2)}, u32[]{:S(2)}) collective-permute-start(bf16[4,512,256]{2,1,0:T(8,128)(2,1)} %get-tuple-element.429), channel_id=1, source_target_pairs={{0,8},{8,0},{16,24},{24,16},{1,9},{9,1},{17,25},{25,17},{2,10},{10... | collective-permute-start | bytes 3145736 | tf_op jit(solution)/shard_map/ppermute | solution.py:30
  190.0 15.1 %collective-permute-start.33 = (bf16[2,512,256]{2,1,0:T(8,128)(2,1)S(1)}, bf16[2,512,256]{2,1,0:T(8,128)(2,1)S(1)}, u32[]{:S(2)}, u32[]{:S(2)}) collective-permute-start(bf16[2,512,256]{2,1,0:T(8,128)(2,1)S(1)} %slice.157), channel_id=1, source_target_pairs={{0,16},{8,24},{16,0},{24,8},{1,17},{9,25},{17,1},{25,9},{2,18},{10... | collective-permute-start | bytes 1572872 | tf_op jit(solution)/shard_map/ppermute | solution.py:30
  194.3 9.0 %collective-permute-start.36 = (f32[8,512]{1,0:T(8,128)S(1)}, f32[8,512]{1,0:T(8,128)S(1)}, u32[]{:S(2)}, u32[]{:S(2)}) collective-permute-start(f32[8,512]{1,0:T(8,128)S(1)} %get-tuple-element.520), channel_id=1, source_target_pairs={{0,24},{8,16},{16,8},{24,0},{1,25},{9,17},{17,9},{25,1},{2,26},{10... | collective-permute-start | bytes 49160 | tf_op jit(solution)/shard_map/ppermute | solution.py:30
  194.3 10.1 %collective-permute-start.35 = (f32[8,512]{1,0:T(8,128)S(1)}, f32[8,512]{1,0:T(8,128)S(1)}, u32[]{:S(2)}, u32[]{:S(2)}) collective-permute-start(f32[8,512]{1,0:T(8,128)S(1)} %get-tuple-element.521), channel_id=1, source_target_pairs={{0,16},{8,24},{16,0},{24,8},{1,17},{9,25},{17,1},{25,9},{2,18},{10... | collective-permute-start | bytes 49160 | tf_op jit(solution)/shard_map/ppermute | solution.py:30
  195.5 9.0 %collective-permute-start.34 = (f32[8,512]{1,0:T(8,128)S(1)}, f32[8,512]{1,0:T(8,128)S(1)}, u32[]{:S(2)}, u32[]{:S(2)}) collective-permute-start(f32[8,512]{1,0:T(8,128)S(1)} %get-tuple-element.519), channel_id=1, source_target_pairs={{0,8},{8,0},{16,24},{24,16},{1,9},{9,1},{17,25},{25,17},{2,10},{10... | collective-permute-start | bytes 49160 | tf_op jit(solution)/shard_map/ppermute | solution.py:30
  205.2 8.3 %collective-permute-start.43 = (f32[8,512]{1,0:T(8,128)S(1)}, f32[8,512]{1,0:T(8,128)S(1)}, u32[]{:S(2)}, u32[]{:S(2)}) collective-permute-start(f32[8,512]{1,0:T(8,128)S(1)} %fusion.39), channel_id=1, source_target_pairs={{0,4},{2,6},{4,0},{6,2},{1,5},{3,7},{5,1},{7,3},{8,12},{10,14},{12... | collective-permute-start | bytes 49160 | tf_op jit(solution)/shard_map/ppermute | solution.py:30
  207.5 8.4 %collective-permute-start.44 = (f32[8,512]{1,0:T(8,128)S(1)}, f32[8,512]{1,0:T(8,128)S(1)}, u32[]{:S(2)}, u32[]{:S(2)}) collective-permute-start(f32[8,512]{1,0:T(8,128)S(1)} %fusion.39), channel_id=1, source_target_pairs={{0,6},{2,4},{4,2},{6,0},{1,7},{3,5},{5,3},{7,1},{8,14},{10,12},{12... | collective-permute-start | bytes 49160 | tf_op jit(solution)/shard_map/ppermute | solution.py:30
  209.0 6.9 %collective-permute-start.42 = (f32[8,512]{1,0:T(8,128)S(1)}, f32[8,512]{1,0:T(8,128)S(1)}, u32[]{:S(2)}, u32[]{:S(2)}) collective-permute-start(f32[8,512]{1,0:T(8,128)S(1)} %fusion.39), channel_id=1, source_target_pairs={{0,2},{2,0},{4,6},{6,4},{1,3},{3,1},{5,7},{7,5},{8,10},{10,8},{12,... | collective-permute-start | bytes 49160 | tf_op jit(solution)/shard_map/ppermute | solution.py:30
  209.3 21.8 %collective-permute-start.37 = (bf16[2,512,256]{2,1,0:T(8,128)(2,1)S(1)}, bf16[2,512,256]{2,1,0:T(8,128)(2,1)S(1)}, u32[]{:S(2)}, u32[]{:S(2)}) collective-permute-start(bf16[2,512,256]{2,1,0:T(8,128)(2,1)S(1)} %slice.162), channel_id=1, source_target_pairs={{0,16},{8,24},{16,0},{24,8},{1,17},{9,25},{17,1},{25,9},{2,18},{10... | collective-permute-start | bytes 1572872 | tf_op jit(solution)/shard_map/ppermute | solution.py:30
  211.6 16.7 %collective-permute-start.38 = (bf16[512,256]{1,0:T(8,128)(2,1)}, bf16[512,256]{1,0:T(8,128)(2,1)S(1)}, u32[]{:S(2)}, u32[]{:S(2)}) collective-permute-start(bf16[512,256]{1,0:T(8,128)(2,1)} %get-tuple-element.491), channel_id=1, source_target_pairs={{0,2},{2,0},{4,6},{6,4},{1,3},{3,1},{5,7},{7,5},{8,10},{10,8},{12,... | collective-permute-start | bytes 786440 | tf_op jit(solution)/shard_map/ppermute | solution.py:30
  213.5 12.0 %collective-permute-start.41 = (bf16[2,208,128]{2,1,0:T(8,128)(2,1)S(1)}, bf16[2,208,128]{2,1,0:T(8,128)(2,1)S(1)}, u32[]{:S(2)}, u32[]{:S(2)}) collective-permute-start(bf16[2,208,128]{2,1,0:T(8,128)(2,1)S(1)} %get-tuple-element.498), channel_id=1, source_target_pairs={{0,6},{2,4},{4,2},{6,0},{1,7},{3,5},{5,3},{7,1},{8,14},{10,12},{12... | collective-permute-start | bytes 319496 | tf_op jit(solution)/shard_map/ppermute | solution.py:30
  215.9 9.6 %collective-permute-start.40 = (bf16[2,208,128]{2,1,0:T(8,128)(2,1)S(1)}, bf16[2,208,128]{2,1,0:T(8,128)(2,1)S(1)}, u32[]{:S(2)}, u32[]{:S(2)}) collective-permute-start(bf16[2,208,128]{2,1,0:T(8,128)(2,1)S(1)} %get-tuple-element.499), channel_id=1, source_target_pairs={{0,4},{2,6},{4,0},{6,2},{1,5},{3,7},{5,1},{7,3},{8,12},{10,14},{12... | collective-permute-start | bytes 319496 | tf_op jit(solution)/shard_map/ppermute | solution.py:30
  215.9 11.3 %collective-permute-start.39 = (bf16[2,208,128]{2,1,0:T(8,128)(2,1)S(1)}, bf16[2,208,128]{2,1,0:T(8,128)(2,1)S(1)}, u32[]{:S(2)}, u32[]{:S(2)}) collective-permute-start(bf16[2,208,128]{2,1,0:T(8,128)(2,1)S(1)} %get-tuple-element.500), channel_id=1, source_target_pairs={{0,2},{2,0},{4,6},{6,4},{1,3},{3,1},{5,7},{7,5},{8,10},{10,8},{12,... | collective-permute-start | bytes 319496 | tf_op jit(solution)/shard_map/ppermute | solution.py:30
  231.9 19.3 %collective-permute-start.45 = (bf16[512,256]{1,0:T(8,128)(2,1)S(1)}, bf16[512,256]{1,0:T(8,128)(2,1)S(1)}, u32[]{:S(2)}, u32[]{:S(2)}) collective-permute-start(bf16[512,256]{1,0:T(8,128)(2,1)S(1)} %get-tuple-element.489), channel_id=1, source_target_pairs={{0,2},{2,0},{4,6},{6,4},{1,3},{3,1},{5,7},{7,5},{8,10},{10,8},{12,... | collective-permute-start | bytes 786440 | tf_op jit(solution)/shard_map/ppermute | solution.py:30
  232.0 19.3 %collective-permute-start.46 = (bf16[512,256]{1,0:T(8,128)(2,1)S(1)}, bf16[512,256]{1,0:T(8,128)(2,1)S(1)}, u32[]{:S(2)}, u32[]{:S(2)}) collective-permute-start(bf16[512,256]{1,0:T(8,128)(2,1)S(1)} %add_convert_fusion.2), channel_id=1, source_target_pairs={{0,4},{2,6},{4,0},{6,2},{1,5},{3,7},{5,1},{7,3},{8,12},{10,14},{12... | collective-permute-start | bytes 786440 | tf_op jit(solution)/shard_map/ppermute | solution.py:30
  (39 other events, 404.2 us)
Sparse Core Ops, SparseCore 0:
  10.8 96.3 all-gather.2
  142.6 121.9 reduce-scatter.1

commit v3 on v2

--- a/solution.py
+++ b/solution.py
@@ -107,6 +107,13 @@
         outs[3 * i + 1][...] = change
         outs[3 * i + 2][0] = low_moment
         outs[3 * i + 2][1] = high_moment
+
+
+def join_kernel(qkv, out, up, down, head_o, feed_o):
+    head_o[: qkv.shape[0], :] = qkv[...]
+    head_o[qkv.shape[0] :, :] = out[...]
+    feed_o[: up.shape[0], :] = up[...]
+    feed_o[up.shape[0] :, :] = down[...]
 
 
 def collect_kernel(spec, pos, ones, *refs):
@@ -462,7 +469,7 @@
             out_o[k, i] = jnp.where(low_col, left, right).astype(LOW)
 
 
-ROOM = 56 * 1024 * 1024
+ROOM = 60 * 1024 * 1024
 
 
 def whole(array):
@@ -512,7 +519,12 @@
     up_own = w_up.transpose(1, 2, 0).reshape(-1, width)
     down_own = w_down.reshape(-1, width)
     qkv_count, unit_count = qkv_own.shape[0], up_own.shape[0]
-    head_own = jnp.concatenate([qkv_own, out_own])
+    head_own, feed_own = run_kernel(
+        join_kernel,
+        (qkv_own, out_own, up_own, down_own),
+        [shaped((qkv_count + out_own.shape[0], width), LOW), shaped((2 * unit_count, width), LOW)],
+        in_specs=[whole(a) for a in (qkv_own, out_own, up_own, down_own)],
+    )
     head_count = head_own.shape[0]
 
     at_me = (jnp.arange(parts) == me)[:, None]
@@ -545,7 +557,7 @@
         return values
 
     assert rows == 4 and images == 2 and lax.axis_size("col") == 2
-    feed_all = lax.all_gather(jnp.concatenate([after(up_own, head_own), down_own]), ("dp", "row"), axis=0).reshape(parts, rows, -1, width)
+    feed_all = lax.all_gather(feed_own, ("dp", "row"), axis=0).reshape(parts, rows, -1, width)
     head_two = near_two(head_own)
     head_x = across(head_own)
     head_plane = planes(head_own)

time: 277 us -> 274 us (0.989)
  waiting for transfers between devices: 90.3 us -> 84.2 us
    ppermute x47, waiting for transfers between devices: 84.6 us -> 78.6 us  [swap(): return lax.ppermute(values, name, [(i, i ^ bit) for i in range(count)])]
    concatenate x2 -> x0, other arithmetic: 3 us -> none  [the longest x1 1.95 us: on_device(): jnp.concatenate([after(up_own, head_own), down_own])]
    pallas_call x13 -> x14, Pallas kernels: 89 us -> 91.5 us  [run_kernel(): pl.pallas_call(body, grid=grid or (1,), in_specs=in_specs, out_specs=out_...]
  transfers between devices with their start and end apart: 49 -> 49, of which waited for: 20 -> 18; matrix products, arithmetic and copies ran while one was open for 4% -> 6% of each run, Pallas kernels for 31% -> 31%
where the time goes in v3:
time: 274 us; the launch traced here: 273 us
  Pallas kernels  91.5 us (33%)
  waiting for transfers between devices  84.2 us (31%)
  starting transfers between devices  61.1 us (22%)
  between operations  14.8 us (5%)
  local copies, waits for them, and re-layouts  11.9 us (4%)
  other arithmetic  9.48 us (3%)
    pallas_call x14, Pallas kernels, run_kernel(): pl.pallas_call(body, grid=grid or (1,), in_specs=in_specs, out_specs=out_...  91.5 us
    ppermute x47, waiting for transfers between devices, swap(): return lax.ppermute(values, name, [(i, i ^ bit) for i in range(count)])  78.6 us
    ppermute x47, starting transfers between devices, swap(): return lax.ppermute(values, name, [(i, i ^ bit) for i in range(count)])  61 us
    reduce_scatter x1, waiting for transfers between devices, on_device(): lax.psum_scatter(feed_grad.reshape(-1, width), ('dp', 'row'), scatter_dim...  5.59 us
  transfers between devices with their start and end apart: 49, of which 18 were waited for; matrix products, arithmetic and copies ran while one was open for 6% of the time, Pallas kernels for 31%

profile of v3, /device:TPU:0, one launch (start us, length us, event | category | flops | bytes accessed | tf_op | source)
XLA Modules:
  0.0 272.9 jit_solution(9594698490684135997)
XLA Ops:
  7.2 2.1 shard_map.335
  9.4 3.1 %collective-permute-start = (bf16[512,256]{1,0:T(8,128)(2,1)}, bf16[512,256]{1,0:T(8,128)(2,1)S(1)}, u32[]{:S(2)}, u32[]{:S(2)}) collective-permute-start(bf16[512,256]{1,0:T(8,128)(2,1)} %get-tuple-element.280.refs_0_), channel_id=1, source_target_pairs={{0,2},{2,0},{4,6},{6,4},{1,3},{3,1},{5,7},{7,5},{8,10},{10,8},{12,... | collective-permute-start | bytes 786440 | tf_op jit(solution)/shard_map/ppermute | solution.py:30
  12.5 2.6 collective-permute-start.1
  15.1 1.5 collective-permute-start.2
  17.5 1.6 collective-permute-start.4
  22.0 2.4 collective-permute-done
  24.5 3.5 %collective-permute-done.1 = bf16[512,256]{1,0:T(8,128)(2,1)} collective-permute-done((bf16[512,256]{1,0:T(8,128)(2,1)}, bf16[512,256]{1,0:T(8,128)(2,1)}, u32[]{:S(2)}, u32[]{:S(2)}) %collective-permute-start.1) | collective-permute-done | bytes 262176 | tf_op jit(solution)/shard_map/ppermute | solution.py:30
  29.8 1.6 collective-permute-start.9
  31.8 4.2 %collective-permute-start.5 = (bf16[512,256]{1,0:T(8,128)(2,1)}, bf16[512,256]{1,0:T(8,128)(2,1)}, u32[]{:S(2)}, u32[]{:S(2)}) collective-permute-start(bf16[512,256]{1,0:T(8,128)(2,1)} %collective-permute-done.1), channel_id=1, source_target_pairs={{0,2},{2,0},{4,6},{6,4},{1,3},{3,1},{5,7},{7,5},{8,10},{10,8},{12,... | collective-permute-start | bytes 786440 | tf_op jit(solution)/shard_map/ppermute | solution.py:30
  36.5 4.2 %collective-permute-start.7 = (bf16[2,216,128]{2,1,0:T(8,128)(2,1)S(1)}, bf16[2,216,128]{2,1,0:T(8,128)(2,1)S(1)}, u32[]{:S(2)}, u32[]{:S(2)}) collective-permute-start(bf16[2,216,128]{2,1,0:T(8,128)(2,1)S(1)} %copy-done.31), channel_id=1, source_target_pairs={{0,4},{2,6},{4,0},{6,2},{1,5},{3,7},{5,1},{7,3},{8,12},{10,14},{12... | collective-permute-start | bytes 331784 | tf_op jit(solution)/shard_map/ppermute | solution.py:30
  42.0 12.0 %collective-permute-done.6 = bf16[2,216,128]{2,1,0:T(8,128)(2,1)S(1)} collective-permute-done((bf16[2,216,128]{2,1,0:T(8,128)(2,1)}, bf16[2,216,128]{2,1,0:T(8,128)(2,1)S(1)}, u32[]{:S(2)}, u32[]{:S(2)}) %collective-permute-start.6) | collective-permute-done | bytes 110624 | tf_op jit(solution)/shard_map/ppermute | solution.py:30
  54.0 4.6 %collective-permute-start.16 = (bf16[2,208,128]{2,1,0:T(8,128)(2,1)S(1)}, bf16[2,208,128]{2,1,0:T(8,128)(2,1)S(1)}, u32[]{:S(2)}, u32[]{:S(2)}) collective-permute-start(bf16[2,208,128]{2,1,0:T(8,128)(2,1)S(1)} %get-tuple-element.511), channel_id=1, source_target_pairs={{0,4},{2,6},{4,0},{6,2},{1,5},{3,7},{5,1},{7,3},{8,12},{10,14},{12... | collective-permute-start | bytes 319496 | tf_op jit(solution)/shard_map/ppermute | solution.py:30
  59.4 2.8 %collective-permute-done.15 = bf16[2,208,128]{2,1,0:T(8,128)(2,1)S(1)} collective-permute-done((bf16[2,208,128]{2,1,0:T(8,128)(2,1)S(1)}, bf16[2,208,128]{2,1,0:T(8,128)(2,1)S(1)}, u32[]{:S(2)}, u32[]{:S(2)}) %collective-permute-start.15) | collective-permute-done | bytes 106528 | tf_op jit(solution)/shard_map/ppermute | solution.py:30
  62.2 1.6 collective-permute-start.14
  64.8 4.9 %collective-permute-done.16 = bf16[2,208,128]{2,1,0:T(8,128)(2,1)S(1)} collective-permute-done((bf16[2,208,128]{2,1,0:T(8,128)(2,1)S(1)}, bf16[2,208,128]{2,1,0:T(8,128)(2,1)S(1)}, u32[]{:S(2)}, u32[]{:S(2)}) %collective-permute-start.16) | collective-permute-done | bytes 106528 | tf_op jit(solution)/shard_map/ppermute | solution.py:30
  69.7 1.6 collective-permute-start.10
  71.3 1.5 collective-permute-done.11.refs_3_
  72.8 11.8 %collective-permute-done.10.refs_10_ = bf16[640,256]{1,0:T(8,128)(2,1)S(1)} collective-permute-done((bf16[640,256]{1,0:T(8,128)(2,1)S(1)}, bf16[640,256]{1,0:T(8,128)(2,1)S(1)}, u32[]{:S(2)}, u32[]{:S(2)}) %collective-permute-start.10) | collective-permute-done | bytes 327712 | tf_op jit(solution)/shard_map/ppermute | solution.py:30
  89.1 6.6 %shard_map.336 = (f32[8,1024]{1,0:T(8,128)}, bf16[208,1024]{1,0:T(8,128)(2,1)}, bf16[208,1024]{1,0:T(8,128)(2,1)}, bf16[208,1536]{1,0:T(8,128)(2,1)}, bf16[208,5...) custom-call(s32[3]{0:T(128)} %pad_add_fusion.pos, bf16[4,2,208,128]{3,2,1,0:T(8,128)(2,1)} %copy-done.11, ...), custom_call_target="tpu_custom_call" | custom-call | flops 1024 | bytes 1024 | tf_op jit(solution)/shard_map/pallas_call | solution.py:485
  97.9 6.3 %shard_map.337 = (f32[8,1024]{1,0:T(8,128)}, bf16[208,1024]{1,0:T(8,128)(2,1)}, bf16[208,1024]{1,0:T(8,128)(2,1)}, bf16[208,1536]{1,0:T(8,128)(2,1)}, bf16[208,5...) custom-call(s32[3]{0:T(128)} %pad_add_fusion.pos, bf16[4,2,208,128]{3,2,1,0:T(8,128)(2,1)} %copy-done.11, ...), custom_call_target="tpu_custom_call" | custom-call | flops 1024 | bytes 1024 | tf_op jit(solution)/shard_map/pallas_call | solution.py:485
  104.2 3.5 %collective-permute-done.21.came = bf16[208,1024]{1,0:T(8,128)(2,1)S(1)} collective-permute-done((bf16[208,1024]{1,0:T(8,128)(2,1)}, bf16[208,1024]{1,0:T(8,128)(2,1)S(1)}, u32[]{:S(2)}, u32[]{:S(2)}) %collective-permute-start.21) | collective-permute-done | bytes 426016 | tf_op jit(solution)/shard_map/ppermute | solution.py:30
  108.6 10.9 %shard_map.338 = (f32[208,1024]{1,0:T(8,128)}, bf16[208,1024]{1,0:T(8,128)(2,1)}, bf16[208,1024]{1,0:T(8,128)(2,1)}, f32[1,1024]{1,0:T(1,128)}, bf16[4,208,512]{...) custom-call(s32[3]{0:T(128)} %pad_add_fusion.pos, ...), custom_call_target="tpu_custom_call" | custom-call | flops 1024 | bytes 1024 | tf_op jit(solution)/shard_map/pallas_call | solution.py:485
  120.7 10.7 %shard_map.339 = (f32[208,1024]{1,0:T(8,128)}, bf16[208,1024]{1,0:T(8,128)(2,1)}, bf16[208,1024]{1,0:T(8,128)(2,1)}, f32[1,1024]{1,0:T(1,128)}, bf16[4,208,512]{...) custom-call(s32[3]{0:T(128)} %pad_add_fusion.pos, ...), custom_call_target="tpu_custom_call" | custom-call | flops 1024 | bytes 1024 | tf_op jit(solution)/shard_map/pallas_call | solution.py:485
  132.4 9.1 %shard_map.340 = bf16[4,4,1024,256]{3,2,1,0:T(8,128)(2,1)} custom-call(s32[3]{0:T(128)} %pad_add_fusion.pos, bf16[4,208,512]{2,1,0:T(8,128)(2,1)} %get-tuple-element.355.refs_0_, bf16[4,208,512]{2,1,0:T(8,128)(2,1)} %get-tuple-element.356.refs_1_, bf16[4,208,512]{2,1,0:T(8,128)(2,1)} %get-tuple-element.357.refs_2_, ...), custom_call_target="tpu_custom_call" | custom-call | flops 1024 | bytes 1024 | tf_op jit(solution)/shard_map/pallas_call | solution.py:485
  144.4 10.1 %shard_map.341 = (f32[208,1024]{1,0:T(8,128)}, bf16[208,1024]{1,0:T(8,128)(2,1)}, bf16[208,1536]{1,0:T(8,128)(2,1)}, bf16[208,1024]{1,0:T(8,128)(2,1)}, f32[8,1024]{1,0:T(8,128)}, /*index=5*/f32[1,1536]{1,0:T(1,128)}) custom-call(s32[3]{0:T(128)} %pad_add_fusion.pos, f32[8,1024]{1,0:T(8,128)} %get-tuple-element.301.vec, f32[208,1024]{1,0:T(8,128)} %get-tuple-element.377.mid, ...), custom_call_target="tpu_custom_call" | custom-call | flops 1024 | bytes 1024 | tf_op jit(solution)/shard_map/pallas_call | solution.py:485
  154.7 3.5 %collective-permute-start.29 = (bf16[2,208,128]{2,1,0:T(8,128)(2,1)S(1)}, bf16[2,208,128]{2,1,0:T(8,128)(2,1)S(1)}, u32[]{:S(2)}, u32[]{:S(2)}) collective-permute-start(bf16[2,208,128]{2,1,0:T(8,128)(2,1)S(1)} %get-tuple-element.505), channel_id=1, source_target_pairs={{0,6},{2,4},{4,2},{6,0},{1,7},{3,5},{5,3},{7,1},{8,14},{10,12},{12... | collective-permute-start | bytes 319496 | tf_op jit(solution)/shard_map/ppermute | solution.py:30
  160.2 10.8 %shard_map.342 = (f32[208,1024]{1,0:T(8,128)}, bf16[208,1024]{1,0:T(8,128)(2,1)}, bf16[208,1536]{1,0:T(8,128)(2,1)}, bf16[208,1024]{1,0:T(8,128)(2,1)}, f32[8,1024]{1,0:T(8,128)}, /*index=5*/f32[1,1536]{1,0:T(1,128)}) custom-call(s32[3]{0:T(128)} %pad_add_fusion.pos, f32[8,1024]{1,0:T(8,128)} %get-tuple-element.301.vec, f32[208,1024]{1,0:T(8,128)} %get-tuple-element.397.mid, ...), custom_call_target="tpu_custom_call" | custom-call | flops 1024 | bytes 1024 | tf_op jit(solution)/shard_map/pallas_call | solution.py:485
  173.2 7.4 %shard_map.343 = (bf16[4,512,256]{2,1,0:T(8,128)(2,1)}, bf16[4,512,256]{2,1,0:T(8,128)(2,1)}, bf16[4,512,256]{2,1,0:T(8,128)(2,1)}, bf16[4,512,256]{2,1,0:T(8,128)(2,1)}) custom-call(s32[3]{0:T(128)} %pad_add_fusion.pos, bf16[208,1536]{1,0:T(8,128)(2,1)} %get-tuple-element.413.refs_0_, bf16[208,1536]{1,0:T(8,128)(2,1)} %get-tuple-element.414.refs_1_, ...), custom_call_target="tpu_custom_call" | custom-call | flops 1024 | bytes 1024 | tf_op jit(solution)/shard_map/pallas_call | solution.py:485
  181.3 4.5 %shard_map.344 = (bf16[4,2,208,128]{3,2,1,0:T(8,128)(2,1)}, f32[8,1024]{1,0:T(8,128)}) custom-call(s32[3]{0:T(128)} %pad_add_fusion.pos, f32[8,1024]{1,0:T(8,128)} %get-tuple-element.301.vec, bf16[208,1024]{1,0:T(8,128)(2,1)} %get-tuple-element.314.x.refs_0_, bf16[208,1024]{1,0:T(8,128)(2,1)} %get-tuple-element.342.x.refs_1_, ...), custom_call_target="tpu_custom_call" | custom-call | flops 1024 | bytes 1024 | tf_op jit(solution)/shard_map/pallas_call | solution.py:485
  185.8 1.6 add_convert_fusion.1
  187.7 1.5 collective-permute-start.33
  189.2 1.9 shard_map.345
  193.7 7.1 %collective-permute-done.36 = f32[8,512]{1,0:T(8,128)S(1)} collective-permute-done((f32[8,512]{1,0:T(8,128)S(1)}, f32[8,512]{1,0:T(8,128)S(1)}, u32[]{:S(2)}, u32[]{:S(2)}) %collective-permute-start.36) | collective-permute-done | bytes 16416 | tf_op jit(solution)/shard_map/ppermute | solution.py:30
  202.9 2.1 collective-permute-start.43
  205.0 1.5 collective-permute-start.44
  206.9 1.6 collective-permute-start.37
  209.3 1.7 collective-permute-start.38
  212.1 2.4 collective-permute-start.41
  214.5 2.1 collective-permute-start.39
  217.2 5.9 %collective-permute-done.41 = bf16[2,208,128]{2,1,0:T(8,128)(2,1)S(1)} collective-permute-done((bf16[2,208,128]{2,1,0:T(8,128)(2,1)S(1)}, bf16[2,208,128]{2,1,0:T(8,128)(2,1)S(1)}, u32[]{:S(2)}, u32[]{:S(2)}) %collective-permute-start.41) | collective-permute-done | bytes 106528 | tf_op jit(solution)/shard_map/ppermute | solution.py:30
  223.0 1.8 collective-permute-done.39
  225.9 2.4 collective-permute-done.37
  229.3 3.6 %collective-permute-start.46 = (bf16[512,256]{1,0:T(8,128)(2,1)S(1)}, bf16[512,256]{1,0:T(8,128)(2,1)S(1)}, u32[]{:S(2)}, u32[]{:S(2)}) collective-permute-start(bf16[512,256]{1,0:T(8,128)(2,1)S(1)} %add_convert_fusion.2), channel_id=1, source_target_pairs={{0,4},{2,6},{4,0},{6,2},{1,5},{3,7},{5,1},{7,3},{8,12},{10,14},{12... | collective-permute-start | bytes 786440 | tf_op jit(solution)/shard_map/ppermute | solution.py:30
  232.9 15.6 %collective-permute-done.45.refs_0_ = bf16[512,256]{1,0:T(8,128)(2,1)S(1)} collective-permute-done((bf16[512,256]{1,0:T(8,128)(2,1)S(1)}, bf16[512,256]{1,0:T(8,128)(2,1)S(1)}, u32[]{:S(2)}, u32[]{:S(2)}) %collective-permute-start.45) | collective-permute-done | bytes 262176 | tf_op jit(solution)/shard_map/ppermute | solution.py:30
  249.3 3.2 %shard_map.346 = (f32[384,256]{1,0:T(8,128)}, f32[384,256]{1,0:T(8,128)}, f32[2,384,256]{2,1,0:T(8,128)}, f32[128,256]{1,0:T(8,128)}, f32[128,256]{1,0:T(8,128)}, /*index=5*/f32[2,128,256]{2,1,0:T(8,128)}) custom-call(bf16[512,256]{1,0:T(8,128)(2,1)} %get-tuple-element.464.first, bf16[512,256]{1,0:T(8,128)(2,1)} %copy-done.27, bf16[512,256]{1,0:T(8,128)(2,1)} %copy-done.28, ...), custom_call_target="tpu_custom_call" | custom-call | flops 1024 | bytes 1024 | tf_op jit(solution)/shard_map/pallas_call | solution.py:485
  252.5 3.7 %shard_map.347 = (f32[2,8,16]{2,1,0:T(8,128)}, f32[16,32]{1,0:T(8,128)}, f32[6,2,16]{2,1,0:T(2,128)}, f32[2,8,16]{2,1,0:T(8,128)}, f32[16,32]{1,0:T(8,128)}, /*i...) custom-call(s32[3]{0:T(128)} %pad_add_fusion.pos, ...), custom_call_target="tpu_custom_call" | custom-call | flops 1024 | bytes 1024 | tf_op jit(solution)/shard_map/pallas_call | solution.py:485
  256.2 5.6 %reduce-scatter.2.cloned.1.call-done.first = bf16[1024,256]{1,0:T(8,128)(2,1)} async-done(((bf16[16384,256]{1,0:T(8,128)(2,1)}), bf16[1024,256]{1,0:T(8,128)(2,1)}) %reduce-scatter.2.cloned.1.call-update) | async-done | bytes 524304 | tf_op jit(solution)/shard_map/reduce_scatter | solution.py:699
  261.8 4.3 %shard_map.348 = (f32[512,256]{1,0:T(8,128)}, f32[512,256]{1,0:T(8,128)}, f32[2,512,256]{2,1,0:T(8,128)}, f32[512,256]{1,0:T(8,128)}, f32[512,256]{1,0:T(8,128)}, /*index=5*/f32[2,512,256]{2,1,0:T(8,128)}) custom-call(bf16[1024,256]{1,0:T(8,128)(2,1)} %reduce-scatter.2.cloned.1.call-done.first, bf16[512,256]{1,0:T(8,128)(2,1)} %bitcast.183, ...), custom_call_target="tpu_custom_call" | custom-call | flops 1024 | bytes 1024 | tf_op jit(solution)/shard_map/pallas_call | solution.py:485
  (200 shorter events, 38.0 us)
Async XLA Ops:
  7.2 101.4 %all-gather.3.cloned.1.call-start = ((), (), s32[]{:S(2)}) async-start(), calls=%async_computation.2 | async-start | bytes 8912896 | tf_op jit(solution)/shard_map/all_gather | solution.py:560
  9.3 252.5 %reduce-scatter.2.cloned.1.call-start = ((), (), s32[]{:S(2)}) async-start(), calls=%async_computation.1 | async-start | bytes 8912896 | tf_op jit(solution)/shard_map/reduce_scatter | solution.py:699
  9.4 15.1 %collective-permute-start = (bf16[512,256]{1,0:T(8,128)(2,1)}, bf16[512,256]{1,0:T(8,128)(2,1)S(1)}, u32[]{:S(2)}, u32[]{:S(2)}) collective-permute-start(bf16[512,256]{1,0:T(8,128)(2,1)} %get-tuple-element.280.refs_0_), channel_id=1, source_target_pairs={{0,2},{2,0},{4,6},{6,4},{1,3},{3,1},{5,7},{7,5},{8,10},{10,8},{12,... | collective-permute-start | bytes 786440 | tf_op jit(solution)/shard_map/ppermute | solution.py:30
  12.5 15.5 %collective-permute-start.1 = (bf16[512,256]{1,0:T(8,128)(2,1)}, bf16[512,256]{1,0:T(8,128)(2,1)}, u32[]{:S(2)}, u32[]{:S(2)}) collective-permute-start(bf16[512,256]{1,0:T(8,128)(2,1)} %get-tuple-element.280.refs_0_), channel_id=1, source_target_pairs={{0,4},{2,6},{4,0},{6,2},{1,5},{3,7},{5,1},{7,3},{8,12},{10,14},{12... | collective-permute-start | bytes 786440 | tf_op jit(solution)/shard_map/ppermute | solution.py:30
  15.1 12.9 %collective-permute-start.2 = (bf16[512,256]{1,0:T(8,128)(2,1)}, bf16[512,256]{1,0:T(8,128)(2,1)S(1)}, u32[]{:S(2)}, u32[]{:S(2)}) collective-permute-start(bf16[512,256]{1,0:T(8,128)(2,1)} %get-tuple-element.280.refs_0_), channel_id=1, source_target_pairs={{0,16},{8,24},{16,0},{24,8},{1,17},{9,25},{17,1},{25,9},{2,18},{10... | collective-permute-start | bytes 786440 | tf_op jit(solution)/shard_map/ppermute | solution.py:30
  16.5 11.4 %collective-permute-start.3 = (bf16[512,256]{1,0:T(8,128)(2,1)}, bf16[512,256]{1,0:T(8,128)(2,1)S(1)}, u32[]{:S(2)}, u32[]{:S(2)}) collective-permute-start(bf16[512,256]{1,0:T(8,128)(2,1)} %get-tuple-element.280.refs_0_), channel_id=1, source_target_pairs={{0,8},{8,0},{16,24},{24,16},{1,9},{9,1},{17,25},{25,17},{2,10},{10... | collective-permute-start | bytes 786440 | tf_op jit(solution)/shard_map/ppermute | solution.py:30
  17.5 3.7 %collective-permute-start.4 = (bf16[6,128]{1,0:T(8,128)(2,1)S(1)}, bf16[6,128]{1,0:T(8,128)(2,1)S(1)}, u32[]{:S(2)}, u32[]{:S(2)}) collective-permute-start(bf16[6,128]{1,0:T(8,128)(2,1)S(1)} %broadcast_select_fusion.2), channel_id=1, source_target_pairs={{0,1},{1,0},{2,3},{3,2},{4,5},{5,4},{6,7},{7,6},{8,9},{9,8},{10,11... | collective-permute-start | bytes 4616 | tf_op jit(solution)/shard_map/ppermute | solution.py:30
  29.8 28.9 %collective-permute-start.9 = (bf16[1024,256]{1,0:T(8,128)(2,1)S(1)}, bf16[1024,256]{1,0:T(8,128)(2,1)S(1)}, u32[]{:S(2)}, u32[]{:S(2)}) collective-permute-start(bf16[1024,256]{1,0:T(8,128)(2,1)S(1)} %constant_dynamic-update-slice_fusion.refs_4_), channel_id=1, source_target_pairs={{0,16},{8,24},{16,0},{24,8},{1,17},{9,25},{17,1},{25,9},{2,18},{10... | collective-permute-start | bytes 1572872 | tf_op jit(solution)/shard_map/ppermute | solution.py:30
  31.8 26.8 %collective-permute-start.5 = (bf16[512,256]{1,0:T(8,128)(2,1)}, bf16[512,256]{1,0:T(8,128)(2,1)}, u32[]{:S(2)}, u32[]{:S(2)}) collective-permute-start(bf16[512,256]{1,0:T(8,128)(2,1)} %collective-permute-done.1), channel_id=1, source_target_pairs={{0,2},{2,0},{4,6},{6,4},{1,3},{3,1},{5,7},{7,5},{8,10},{10,8},{12,... | collective-permute-start | bytes 786440 | tf_op jit(solution)/shard_map/ppermute | solution.py:30
  36.4 17.6 %collective-permute-start.6 = (bf16[2,216,128]{2,1,0:T(8,128)(2,1)}, bf16[2,216,128]{2,1,0:T(8,128)(2,1)S(1)}, u32[]{:S(2)}, u32[]{:S(2)}) collective-permute-start(bf16[2,216,128]{2,1,0:T(8,128)(2,1)} %get-tuple-element.261), channel_id=1, source_target_pairs={{0,2},{2,0},{4,6},{6,4},{1,3},{3,1},{5,7},{7,5},{8,10},{10,8},{12,... | collective-permute-start | bytes 331784 | tf_op jit(solution)/shard_map/ppermute | solution.py:30
  36.5 17.6 %collective-permute-start.7 = (bf16[2,216,128]{2,1,0:T(8,128)(2,1)S(1)}, bf16[2,216,128]{2,1,0:T(8,128)(2,1)S(1)}, u32[]{:S(2)}, u32[]{:S(2)}) collective-permute-start(bf16[2,216,128]{2,1,0:T(8,128)(2,1)S(1)} %copy-done.31), channel_id=1, source_target_pairs={{0,4},{2,6},{4,0},{6,2},{1,5},{3,7},{5,1},{7,3},{8,12},{10,14},{12... | collective-permute-start | bytes 331784 | tf_op jit(solution)/shard_map/ppermute | solution.py:30
  40.6 18.0 %collective-permute-start.8 = (bf16[2,216,128]{2,1,0:T(8,128)(2,1)S(1)}, bf16[2,216,128]{2,1,0:T(8,128)(2,1)S(1)}, u32[]{:S(2)}, u32[]{:S(2)}) collective-permute-start(bf16[2,216,128]{2,1,0:T(8,128)(2,1)S(1)} %get-tuple-element.263), channel_id=1, source_target_pairs={{0,6},{2,4},{4,2},{6,0},{1,7},{3,5},{5,3},{7,1},{8,14},{10,12},{12... | collective-permute-start | bytes 331784 | tf_op jit(solution)/shard_map/ppermute | solution.py:30
  54.0 8.2 %collective-permute-start.15 = (bf16[2,208,128]{2,1,0:T(8,128)(2,1)S(1)}, bf16[2,208,128]{2,1,0:T(8,128)(2,1)S(1)}, u32[]{:S(2)}, u32[]{:S(2)}) collective-permute-start(bf16[2,208,128]{2,1,0:T(8,128)(2,1)S(1)} %get-tuple-element.510), channel_id=1, source_target_pairs={{0,2},{2,0},{4,6},{6,4},{1,3},{3,1},{5,7},{7,5},{8,10},{10,8},{12,... | collective-permute-start | bytes 319496 | tf_op jit(solution)/shard_map/ppermute | solution.py:30
  54.0 15.7 %collective-permute-start.16 = (bf16[2,208,128]{2,1,0:T(8,128)(2,1)S(1)}, bf16[2,208,128]{2,1,0:T(8,128)(2,1)S(1)}, u32[]{:S(2)}, u32[]{:S(2)}) collective-permute-start(bf16[2,208,128]{2,1,0:T(8,128)(2,1)S(1)} %get-tuple-element.511), channel_id=1, source_target_pairs={{0,4},{2,6},{4,0},{6,2},{1,5},{3,7},{5,1},{7,3},{8,12},{10,14},{12... | collective-permute-start | bytes 319496 | tf_op jit(solution)/shard_map/ppermute | solution.py:30
  58.6 12.7 %collective-permute-start.17 = (bf16[2,208,128]{2,1,0:T(8,128)(2,1)S(1)}, bf16[2,208,128]{2,1,0:T(8,128)(2,1)S(1)}, u32[]{:S(2)}, u32[]{:S(2)}) collective-permute-start(bf16[2,208,128]{2,1,0:T(8,128)(2,1)S(1)} %get-tuple-element.509), channel_id=1, source_target_pairs={{0,6},{2,4},{4,2},{6,0},{1,7},{3,5},{5,3},{7,1},{8,14},{10,12},{12... | collective-permute-start | bytes 319496 | tf_op jit(solution)/shard_map/ppermute | solution.py:30
  58.6 26.0 %collective-permute-start.12 = (bf16[1024,256]{1,0:T(8,128)(2,1)S(1)}, bf16[1024,256]{1,0:T(8,128)(2,1)S(1)}, u32[]{:S(2)}, u32[]{:S(2)}) collective-permute-start(bf16[1024,256]{1,0:T(8,128)(2,1)S(1)} %constant_dynamic-update-slice_fusion.refs_4_), channel_id=1, source_target_pairs={{0,8},{8,0},{16,24},{24,16},{1,9},{9,1},{17,25},{25,17},{2,10},{10... | collective-permute-start | bytes 1572872 | tf_op jit(solution)/shard_map/ppermute | solution.py:30
  58.7 25.9 %collective-permute-start.13 = (bf16[1024,256]{1,0:T(8,128)(2,1)S(1)}, bf16[1024,256]{1,0:T(8,128)(2,1)S(1)}, u32[]{:S(2)}, u32[]{:S(2)}) collective-permute-start(bf16[1024,256]{1,0:T(8,128)(2,1)S(1)} %collective-permute-done.9.refs_6_), channel_id=1, source_target_pairs={{0,8},{8,0},{16,24},{24,16},{1,9},{9,1},{17,25},{25,17},{2,10},{10... | collective-permute-start | bytes 1572872 | tf_op jit(solution)/shard_map/ppermute | solution.py:30
  62.2 22.4 %collective-permute-start.14 = (bf16[4,2,208,128]{3,2,1,0:T(8,128)(2,1)S(1)}, bf16[4,2,208,128]{3,2,1,0:T(8,128)(2,1)S(1)}, u32[]{:S(2)}, u32[]{:S(2)}) collective-permute-start(bf16[4,2,208,128]{3,2,1,0:T(8,128)(2,1)S(1)} %pad_maximum_fusion.near), channel_id=1, source_target_pairs={{0,1},{1,0},{2,3},{3,2},{4,5},{5,4},{6,7},{7,6},{8,9},{9,8},{10,11... | collective-permute-start | bytes 1277960 | tf_op jit(solution)/shard_map/ppermute | solution.py:30
  69.7 14.9 %collective-permute-start.10 = (bf16[640,256]{1,0:T(8,128)(2,1)S(1)}, bf16[640,256]{1,0:T(8,128)(2,1)S(1)}, u32[]{:S(2)}, u32[]{:S(2)}) collective-permute-start(bf16[640,256]{1,0:T(8,128)(2,1)S(1)} %pad_maximum_fusion.9.refs_8_), channel_id=1, source_target_pairs={{0,16},{8,24},{16,0},{24,8},{1,17},{9,25},{17,1},{25,9},{2,18},{10... | collective-permute-start | bytes 983048 | tf_op jit(solution)/shard_map/ppermute | solution.py:30
  84.7 10.9 %collective-permute-start.20 = (bf16[4,2,208,128]{3,2,1,0:T(8,128)(2,1)S(1)}, bf16[4,2,208,128]{3,2,1,0:T(8,128)(2,1)}, u32[]{:S(2)}, u32[]{:S(2)}) collective-permute-start(bf16[4,2,208,128]{3,2,1,0:T(8,128)(2,1)S(1)} %pad_maximum_fusion.1.near), channel_id=1, source_target_pairs={{0,1},{1,0},{2,3},{3,2},{4,5},{5,4},{6,7},{7,6},{8,9},{9,8},{10,11... | collective-permute-start | bytes 1277960 | tf_op jit(solution)/shard_map/ppermute | solution.py:30
  86.0 1.6 collective-permute-start.18
  86.0 2.1 collective-permute-start.19
  95.7 12.0 %collective-permute-start.21 = (bf16[208,1024]{1,0:T(8,128)(2,1)}, bf16[208,1024]{1,0:T(8,128)(2,1)S(1)}, u32[]{:S(2)}, u32[]{:S(2)}) collective-permute-start(bf16[208,1024]{1,0:T(8,128)(2,1)} %get-tuple-element.315.part), channel_id=1, source_target_pairs={{0,1},{1,0},{2,3},{3,2},{4,5},{5,4},{6,7},{7,6},{8,9},{9,8},{10,11... | collective-permute-start | bytes 1277960 | tf_op jit(solution)/shard_map/ppermute | solution.py:30
  107.7 11.8 %collective-permute-start.22 = (bf16[208,1024]{1,0:T(8,128)(2,1)}, bf16[208,1024]{1,0:T(8,128)(2,1)S(1)}, u32[]{:S(2)}, u32[]{:S(2)}) collective-permute-start(bf16[208,1024]{1,0:T(8,128)(2,1)} %get-tuple-element.330.part), channel_id=1, source_target_pairs={{0,1},{1,0},{2,3},{3,2},{4,5},{5,4},{6,7},{7,6},{8,9},{9,8},{10,11... | collective-permute-start | bytes 1277960 | tf_op jit(solution)/shard_map/ppermute | solution.py:30
  119.5 11.9 %collective-permute-start.23 = (bf16[208,1024]{1,0:T(8,128)(2,1)}, bf16[208,1024]{1,0:T(8,128)(2,1)S(1)}, u32[]{:S(2)}, u32[]{:S(2)}) collective-permute-start(bf16[208,1024]{1,0:T(8,128)(2,1)} %get-tuple-element.378.back), channel_id=1, source_target_pairs={{0,1},{1,0},{2,3},{3,2},{4,5},{5,4},{6,7},{7,6},{8,9},{9,8},{10,11... | collective-permute-start | bytes 1277960 | tf_op jit(solution)/shard_map/ppermute | solution.py:30
  131.4 10.7 %collective-permute-start.24 = (bf16[208,1024]{1,0:T(8,128)(2,1)}, bf16[208,1024]{1,0:T(8,128)(2,1)S(1)}, u32[]{:S(2)}, u32[]{:S(2)}) collective-permute-start(bf16[208,1024]{1,0:T(8,128)(2,1)} %get-tuple-element.398.back), channel_id=1, source_target_pairs={{0,1},{1,0},{2,3},{3,2},{4,5},{5,4},{6,7},{7,6},{8,9},{9,8},{10,11... | collective-permute-start | bytes 1277960 | tf_op jit(solution)/shard_map/ppermute | solution.py:30
  143.3 11.1 %collective-permute-start.25 = (bf16[2,4,208,128]{3,2,1,0:T(8,128)(2,1)S(1)}, bf16[2,4,208,128]{3,2,1,0:T(8,128)(2,1)S(1)}, u32[]{:S(2)}, u32[]{:S(2)}) collective-permute-start(bf16[2,4,208,128]{3,2,1,0:T(8,128)(2,1)S(1)} %pad_maximum_fusion.2), channel_id=1, source_target_pairs={{0,1},{1,0},{2,3},{3,2},{4,5},{5,4},{6,7},{7,6},{8,9},{9,8},{10,11... | collective-permute-start | bytes 1277960 | tf_op jit(solution)/shard_map/ppermute | solution.py:30
  154.7 16.3 %collective-permute-start.29 = (bf16[2,208,128]{2,1,0:T(8,128)(2,1)S(1)}, bf16[2,208,128]{2,1,0:T(8,128)(2,1)S(1)}, u32[]{:S(2)}, u32[]{:S(2)}) collective-permute-start(bf16[2,208,128]{2,1,0:T(8,128)(2,1)S(1)} %get-tuple-element.505), channel_id=1, source_target_pairs={{0,6},{2,4},{4,2},{6,0},{1,7},{3,5},{5,3},{7,1},{8,14},{10,12},{12... | collective-permute-start | bytes 319496 | tf_op jit(solution)/shard_map/ppermute | solution.py:30
  158.2 12.8 %collective-permute-start.28 = (bf16[2,208,128]{2,1,0:T(8,128)(2,1)S(1)}, bf16[2,208,128]{2,1,0:T(8,128)(2,1)S(1)}, u32[]{:S(2)}, u32[]{:S(2)}) collective-permute-start(bf16[2,208,128]{2,1,0:T(8,128)(2,1)S(1)} %get-tuple-element.506), channel_id=1, source_target_pairs={{0,4},{2,6},{4,0},{6,2},{1,5},{3,7},{5,1},{7,3},{8,12},{10,14},{12... | collective-permute-start | bytes 319496 | tf_op jit(solution)/shard_map/ppermute | solution.py:30
  158.2 12.8 %collective-permute-start.27 = (bf16[2,208,128]{2,1,0:T(8,128)(2,1)S(1)}, bf16[2,208,128]{2,1,0:T(8,128)(2,1)S(1)}, u32[]{:S(2)}, u32[]{:S(2)}) collective-permute-start(bf16[2,208,128]{2,1,0:T(8,128)(2,1)S(1)} %get-tuple-element.504), channel_id=1, source_target_pairs={{0,2},{2,0},{4,6},{6,4},{1,3},{3,1},{5,7},{7,5},{8,10},{10,8},{12,... | collective-permute-start | bytes 319496 | tf_op jit(solution)/shard_map/ppermute | solution.py:30
  159.1 13.0 %collective-permute-start.26 = (bf16[208,1024]{1,0:T(8,128)(2,1)S(1)}, bf16[208,1024]{1,0:T(8,128)(2,1)S(1)}, u32[]{:S(2)}, u32[]{:S(2)}) collective-permute-start(bf16[208,1024]{1,0:T(8,128)(2,1)S(1)} %copy-done.19), channel_id=1, source_target_pairs={{0,1},{1,0},{2,3},{3,2},{4,5},{5,4},{6,7},{7,6},{8,9},{9,8},{10,11... | collective-permute-start | bytes 1277960 | tf_op jit(solution)/shard_map/ppermute | solution.py:30
  172.1 8.4 %collective-permute-start.30 = (bf16[208,1024]{1,0:T(8,128)(2,1)S(1)}, bf16[208,1024]{1,0:T(8,128)(2,1)S(1)}, u32[]{:S(2)}, u32[]{:S(2)}) collective-permute-start(bf16[208,1024]{1,0:T(8,128)(2,1)S(1)} %copy-done.21), channel_id=1, source_target_pairs={{0,1},{1,0},{2,3},{3,2},{4,5},{5,4},{6,7},{7,6},{8,9},{9,8},{10,11... | collective-permute-start | bytes 1277960 | tf_op jit(solution)/shard_map/ppermute | solution.py:30
  180.5 5.2 %collective-permute-start.31 = (bf16[4,512,256]{2,1,0:T(8,128)(2,1)}, bf16[4,512,256]{2,1,0:T(8,128)(2,1)}, u32[]{:S(2)}, u32[]{:S(2)}) collective-permute-start(bf16[4,512,256]{2,1,0:T(8,128)(2,1)} %get-tuple-element.429), channel_id=1, source_target_pairs={{0,8},{8,0},{16,24},{24,16},{1,9},{9,1},{17,25},{25,17},{2,10},{10... | collective-permute-start | bytes 3145736 | tf_op jit(solution)/shard_map/ppermute | solution.py:30
  180.6 6.7 %collective-permute-start.32 = (bf16[4,512,256]{2,1,0:T(8,128)(2,1)}, bf16[4,512,256]{2,1,0:T(8,128)(2,1)S(1)}, u32[]{:S(2)}, u32[]{:S(2)}) collective-permute-start(bf16[4,512,256]{2,1,0:T(8,128)(2,1)} %get-tuple-element.431), channel_id=1, source_target_pairs={{0,8},{8,0},{16,24},{24,16},{1,9},{9,1},{17,25},{25,17},{2,10},{10... | collective-permute-start | bytes 3145736 | tf_op jit(solution)/shard_map/ppermute | solution.py:30
  187.7 15.2 %collective-permute-start.33 = (bf16[2,512,256]{2,1,0:T(8,128)(2,1)S(1)}, bf16[2,512,256]{2,1,0:T(8,128)(2,1)S(1)}, u32[]{:S(2)}, u32[]{:S(2)}) collective-permute-start(bf16[2,512,256]{2,1,0:T(8,128)(2,1)S(1)} %slice.157), channel_id=1, source_target_pairs={{0,16},{8,24},{16,0},{24,8},{1,17},{9,25},{17,1},{25,9},{2,18},{10... | collective-permute-start | bytes 1572872 | tf_op jit(solution)/shard_map/ppermute | solution.py:30
  191.9 9.0 %collective-permute-start.36 = (f32[8,512]{1,0:T(8,128)S(1)}, f32[8,512]{1,0:T(8,128)S(1)}, u32[]{:S(2)}, u32[]{:S(2)}) collective-permute-start(f32[8,512]{1,0:T(8,128)S(1)} %get-tuple-element.522), channel_id=1, source_target_pairs={{0,24},{8,16},{16,8},{24,0},{1,25},{9,17},{17,9},{25,1},{2,26},{10... | collective-permute-start | bytes 49160 | tf_op jit(solution)/shard_map/ppermute | solution.py:30
  191.9 10.3 %collective-permute-start.35 = (f32[8,512]{1,0:T(8,128)S(1)}, f32[8,512]{1,0:T(8,128)S(1)}, u32[]{:S(2)}, u32[]{:S(2)}) collective-permute-start(f32[8,512]{1,0:T(8,128)S(1)} %get-tuple-element.523), channel_id=1, source_target_pairs={{0,16},{8,24},{16,0},{24,8},{1,17},{9,25},{17,1},{25,9},{2,18},{10... | collective-permute-start | bytes 49160 | tf_op jit(solution)/shard_map/ppermute | solution.py:30
  193.0 9.1 %collective-permute-start.34 = (f32[8,512]{1,0:T(8,128)S(1)}, f32[8,512]{1,0:T(8,128)S(1)}, u32[]{:S(2)}, u32[]{:S(2)}) collective-permute-start(f32[8,512]{1,0:T(8,128)S(1)} %get-tuple-element.521), channel_id=1, source_target_pairs={{0,8},{8,0},{16,24},{24,16},{1,9},{9,1},{17,25},{25,17},{2,10},{10... | collective-permute-start | bytes 49160 | tf_op jit(solution)/shard_map/ppermute | solution.py:30
  202.9 9.2 %collective-permute-start.43 = (f32[8,512]{1,0:T(8,128)S(1)}, f32[8,512]{1,0:T(8,128)S(1)}, u32[]{:S(2)}, u32[]{:S(2)}) collective-permute-start(f32[8,512]{1,0:T(8,128)S(1)} %fusion.39), channel_id=1, source_target_pairs={{0,4},{2,6},{4,0},{6,2},{1,5},{3,7},{5,1},{7,3},{8,12},{10,14},{12... | collective-permute-start | bytes 49160 | tf_op jit(solution)/shard_map/ppermute | solution.py:30
  205.0 9.5 %collective-permute-start.44 = (f32[8,512]{1,0:T(8,128)S(1)}, f32[8,512]{1,0:T(8,128)S(1)}, u32[]{:S(2)}, u32[]{:S(2)}) collective-permute-start(f32[8,512]{1,0:T(8,128)S(1)} %fusion.39), channel_id=1, source_target_pairs={{0,6},{2,4},{4,2},{6,0},{1,7},{3,5},{5,3},{7,1},{8,14},{10,12},{12... | collective-permute-start | bytes 49160 | tf_op jit(solution)/shard_map/ppermute | solution.py:30
  206.5 8.0 %collective-permute-start.42 = (f32[8,512]{1,0:T(8,128)S(1)}, f32[8,512]{1,0:T(8,128)S(1)}, u32[]{:S(2)}, u32[]{:S(2)}) collective-permute-start(f32[8,512]{1,0:T(8,128)S(1)} %fusion.39), channel_id=1, source_target_pairs={{0,2},{2,0},{4,6},{6,4},{1,3},{3,1},{5,7},{7,5},{8,10},{10,8},{12,... | collective-permute-start | bytes 49160 | tf_op jit(solution)/shard_map/ppermute | solution.py:30
  206.9 21.5 %collective-permute-start.37 = (bf16[2,512,256]{2,1,0:T(8,128)(2,1)S(1)}, bf16[2,512,256]{2,1,0:T(8,128)(2,1)S(1)}, u32[]{:S(2)}, u32[]{:S(2)}) collective-permute-start(bf16[2,512,256]{2,1,0:T(8,128)(2,1)S(1)} %slice.162), channel_id=1, source_target_pairs={{0,16},{8,24},{16,0},{24,8},{1,17},{9,25},{17,1},{25,9},{2,18},{10... | collective-permute-start | bytes 1572872 | tf_op jit(solution)/shard_map/ppermute | solution.py:30
  209.3 16.7 %collective-permute-start.38 = (bf16[512,256]{1,0:T(8,128)(2,1)}, bf16[512,256]{1,0:T(8,128)(2,1)S(1)}, u32[]{:S(2)}, u32[]{:S(2)}) collective-permute-start(bf16[512,256]{1,0:T(8,128)(2,1)} %get-tuple-element.493), channel_id=1, source_target_pairs={{0,2},{2,0},{4,6},{6,4},{1,3},{3,1},{5,7},{7,5},{8,10},{10,8},{12,... | collective-permute-start | bytes 786440 | tf_op jit(solution)/shard_map/ppermute | solution.py:30
  212.1 10.9 %collective-permute-start.41 = (bf16[2,208,128]{2,1,0:T(8,128)(2,1)S(1)}, bf16[2,208,128]{2,1,0:T(8,128)(2,1)S(1)}, u32[]{:S(2)}, u32[]{:S(2)}) collective-permute-start(bf16[2,208,128]{2,1,0:T(8,128)(2,1)S(1)} %get-tuple-element.500), channel_id=1, source_target_pairs={{0,6},{2,4},{4,2},{6,0},{1,7},{3,5},{5,3},{7,1},{8,14},{10,12},{12... | collective-permute-start | bytes 319496 | tf_op jit(solution)/shard_map/ppermute | solution.py:30
  214.5 8.6 %collective-permute-start.40 = (bf16[2,208,128]{2,1,0:T(8,128)(2,1)S(1)}, bf16[2,208,128]{2,1,0:T(8,128)(2,1)S(1)}, u32[]{:S(2)}, u32[]{:S(2)}) collective-permute-start(bf16[2,208,128]{2,1,0:T(8,128)(2,1)S(1)} %get-tuple-element.501), channel_id=1, source_target_pairs={{0,4},{2,6},{4,0},{6,2},{1,5},{3,7},{5,1},{7,3},{8,12},{10,14},{12... | collective-permute-start | bytes 319496 | tf_op jit(solution)/shard_map/ppermute | solution.py:30
  214.5 10.3 %collective-permute-start.39 = (bf16[2,208,128]{2,1,0:T(8,128)(2,1)S(1)}, bf16[2,208,128]{2,1,0:T(8,128)(2,1)S(1)}, u32[]{:S(2)}, u32[]{:S(2)}) collective-permute-start(bf16[2,208,128]{2,1,0:T(8,128)(2,1)S(1)} %get-tuple-element.502), channel_id=1, source_target_pairs={{0,2},{2,0},{4,6},{6,4},{1,3},{3,1},{5,7},{7,5},{8,10},{10,8},{12,... | collective-permute-start | bytes 319496 | tf_op jit(solution)/shard_map/ppermute | solution.py:30
  229.2 19.3 %collective-permute-start.45 = (bf16[512,256]{1,0:T(8,128)(2,1)S(1)}, bf16[512,256]{1,0:T(8,128)(2,1)S(1)}, u32[]{:S(2)}, u32[]{:S(2)}) collective-permute-start(bf16[512,256]{1,0:T(8,128)(2,1)S(1)} %get-tuple-element.491), channel_id=1, source_target_pairs={{0,2},{2,0},{4,6},{6,4},{1,3},{3,1},{5,7},{7,5},{8,10},{10,8},{12,... | collective-permute-start | bytes 786440 | tf_op jit(solution)/shard_map/ppermute | solution.py:30
  229.3 19.2 %collective-permute-start.46 = (bf16[512,256]{1,0:T(8,128)(2,1)S(1)}, bf16[512,256]{1,0:T(8,128)(2,1)S(1)}, u32[]{:S(2)}, u32[]{:S(2)}) collective-permute-start(bf16[512,256]{1,0:T(8,128)(2,1)S(1)} %add_convert_fusion.2), channel_id=1, source_target_pairs={{0,4},{2,6},{4,0},{6,2},{1,5},{3,7},{5,1},{7,3},{8,12},{10,14},{12... | collective-permute-start | bytes 786440 | tf_op jit(solution)/shard_map/ppermute | solution.py:30
  (35 other events, 315.3 us)
Sparse Core Ops, SparseCore 0:
  10.8 94.5 all-gather.2
  142.2 119.5 reduce-scatter.1
